TPU v7x, 512 devices: a whole 4x8x8 slice. The times are simulated.
512 devices in a mesh: head: 8 (over y), inner: 8 (over z_lo, core), outer: 8 (over x, z_hi).
Axes of the slice: x: 4, y: 8, z: 8 (z_hi: 2, z_lo: 4; z = z_hi * 4 + z_lo), core: 2. Of those that a mesh axis runs over, the one named last changes fastest.
Arguments:
- queries: bfloat16 [16384, 6144], P(('outer', 'inner', 'head')), may hold values from -6 to 6, as said below
- keys: bfloat16 [16384, 1024], P(('outer', 'inner', 'head')), may hold values from -4 to 4, as said below
- values: bfloat16 [16384, 1024], P(('outer', 'inner', 'head')), may hold values from -5 to 5
- order: int32 [128], replicated, may hold values from 0 to 127, as said below
Outputs:
- attended: bfloat16 [16384, 6144], P(('outer', 'inner', 'head'))
Inputs may be any that keep to these rules, and one draw needn't show every extreme that they name: Entries of queries stay in the stated range. Entries of keys stay in the stated range. order is a permutation of the 128 blocks; stored blocks 2 r and 2 r + 1 hold sequence blocks c and 127 - c for some c, in either order.
All inputs are finite; a program needn't handle non-finite values.
Results may differ from a plain program's by a relative error of at most 0.0075.
Values may be sent and summed in bfloat16 or wider, within the bound.
No kernel may reach another device: no remote copies, remote signals or barrier semaphores. Data moves between devices by JAX's collectives and lax.ppermute only.
A program may use at most 64 MiB of HBM per device.

v0:
```python
import math

import jax
import jax.numpy as jnp
from jax import lax
from jax.sharding import PartitionSpec as P

QUERY_HEADS = 48
KEY_VALUE_HEADS = 8
HEAD_SIZE = 128
CH = 128


def tile_update(state, qchunk, qpos, kblock, vblock, kpos, scale):
    top, total, summed = state
    score = jnp.einsum("tkgd,skd->tkgs", qchunk, kblock, preferred_element_type=jnp.float32) * scale
    allowed = (kpos[None, :] <= qpos[:, None])[:, None, None, :]
    newtop = jnp.maximum(top, jnp.max(jnp.where(allowed, score, -1e30), axis=-1))
    expo = jnp.where(allowed, jnp.exp(score - newtop[..., None]), 0.0)
    factor = jnp.exp(top - newtop)
    total = total * factor + jnp.sum(expo, axis=-1)
    weight = expo.astype(jnp.bfloat16)
    summed = summed * factor[..., None] + jnp.einsum(
        "tkgs,skd->tkgd", weight, vblock, preferred_element_type=jnp.float32
    )
    return (newtop, total, summed)


def shards(queries, keys, values, order):
    head_list = lax.axis_size("head")
    inner_count = lax.axis_size("inner")
    outer_count = lax.axis_size("outer")
    local_q, local_k, local_v = (
        lax.all_to_all(queries, "head", split_axis=1, concat_axis=0, tiled=True),
        lax.all_to_all(keys, "head", split_axis=1, concat_axis=0, tiled=True),
        lax.all_to_all(values, "head", split_axis=1, concat_axis=0, tiled=True),
    )
    rows = local_q.shape[0]
    span_total = order.shape[0]
    per_q = QUERY_HEADS // head_list
    queries_per_group = KEY_VALUE_HEADS // head_list
    query_group = per_q // queries_per_group
    scale = 1.0 / math.sqrt(HEAD_SIZE)
    span_table = jnp.arange(span_total, dtype=jnp.int32)

    def stored_positions(gathered_spans):
        shard = gathered_spans // 2
        within = gathered_spans % 2
        inner_at = shard // outer_count
        outer_at = shard % outer_count
        stored = (outer_at * inner_count + inner_at) * 2 + within
        picks = span_table[None, :] == stored[:, None]
        span_ids = jnp.sum(jnp.where(picks, order[None, :], 0), axis=1)
        count = gathered_spans.shape[0]
        return (span_ids[:, None] * CH + jnp.arange(CH, dtype=jnp.int32)[None, :]).reshape(
            count * CH
        )

    cycle = lax.axis_index("outer") * inner_count + lax.axis_index("inner")
    slots = cycle * 2 + jnp.arange(2, dtype=jnp.int32)
    own_picks = span_table[None, :] == slots[:, None]
    own_ids = jnp.sum(jnp.where(own_picks, order[None, :], 0), axis=1)
    qpositions = own_ids[:, None] * CH + jnp.arange(CH, dtype=jnp.int32)[None, :]
    qchunks = local_q.reshape(2, CH, queries_per_group, query_group, HEAD_SIZE)
    kv_keys = local_k.reshape(rows, queries_per_group, HEAD_SIZE)
    kv_values = local_v.reshape(rows, queries_per_group, HEAD_SIZE)
    start_top = jnp.full((2, CH, queries_per_group, query_group), -1e30, jnp.float32)
    start_total = jnp.zeros((2, CH, queries_per_group, query_group), jnp.float32)
    start_sum = jnp.zeros((2, CH, queries_per_group, query_group, HEAD_SIZE), jnp.float32)
    piece_k = lax.all_gather(kv_keys, ("inner", "outer"), axis=0, tiled=True)
    piece_v = lax.all_gather(kv_values, ("inner", "outer"), axis=0, tiled=True)
    length = piece_k.shape[0]
    block_rows = math.gcd(length, 8 * CH)
    nblocks = length // block_rows
    spans_in_block = block_rows // CH

    def one_block(index, inner_carry):
        kstart = index * block_rows
        kblock = lax.dynamic_slice_in_dim(piece_k, kstart, block_rows, 0)
        vblock = lax.dynamic_slice_in_dim(piece_v, kstart, block_rows, 0)
        first_span = kstart // CH
        kpos = stored_positions(first_span + jnp.arange(spans_in_block, dtype=jnp.int32))
        lowest = jnp.min(kpos)
        tops, totals, sums = inner_carry
        new_tops, new_totals, new_sums = ([], [], [])
        for which in range(2):
            state = (tops[which], totals[which], sums[which])
            qchunk = qchunks[which]
            qpos = qpositions[which]
            state = lax.cond(
                lowest <= qpos[CH - 1],
                lambda st: tile_update(st, qchunk, qpos, kblock, vblock, kpos, scale),
                lambda st: st,
                state,
            )
            new_tops.append(state[0])
            new_totals.append(state[1])
            new_sums.append(state[2])
        return (jnp.stack(new_tops), jnp.stack(new_totals), jnp.stack(new_sums))

    top, total, summed = lax.fori_loop(0, nblocks, one_block, (start_top, start_total, start_sum))
    attention_output = (
        (summed / total[..., None]).astype(jnp.bfloat16).reshape(rows, per_q * HEAD_SIZE)
    )
    return lax.all_to_all(attention_output, "head", split_axis=0, concat_axis=1, tiled=True)


def solution(mesh):
    placed = (
        P(("outer", "inner", "head"), None),
        P(("outer", "inner", "head"), None),
        P(("outer", "inner", "head"), None),
        P(),
    )
    return jax.shard_map(
        shards,
        mesh=mesh,
        in_specs=placed,
        out_specs=P(("outer", "inner", "head"), None),
        check_vma=False,
    )
```

profile of v0, /device:TPU:192, one launch (start us, length us, event | category | flops | bytes accessed | tf_op | source)
XLA Modules:
  0.0 608.6 jit_solution(16249085784363328991)
XLA Ops:
  7.4 15.4 %all_to_all.67 = bf16[32,8,128]{2,0,1:T(8,128)(2,1)} all-to-all(bf16[32,8,128]{2,0,1:T(8,128)(2,1)S(1)} %copy_bitcast_fusion.2), channel_id=1, replica_groups=mesh['head'=8,'inner'=8,'outer'=8] {'head'}, dimensions={1} | all-to-all | bytes 131072 | tf_op jit(solution)/shard_map/all_to_all | solution.py:35
  23.7 11.4 %all_to_all.68 = bf16[32,8,128]{2,0,1:T(8,128)(2,1)} all-to-all(bf16[32,8,128]{2,0,1:T(8,128)(2,1)S(1)} %copy_bitcast_fusion.1), channel_id=1, replica_groups=mesh['head'=8,'inner'=8,'outer'=8] {'head'}, dimensions={1} | all-to-all | bytes 131072 | tf_op jit(solution)/shard_map/all_to_all | solution.py:36
  36.9 3.5 all-to-all-start.2
  41.3 11.4 %all-to-all-done.2 = bf16[32,8,768]{2,0,1:T(8,128)(2,1)S(1)} async-done(((bf16[32,8,768]{2,0,1:T(8,128)(2,1)}), bf16[32,8,768]{2,0,1:T(8,128)(2,1)S(1)}, u32[]{:S(2)}, u32[]{:S(2)}) %all-to-all-start.2) | async-done | bytes 393248 | tf_op jit(solution)/shard_map/all_to_all | solution.py:34
  53.2 160.8 %all-gather.3.cloned.1.call-done = bf16[16384,1,128]{2,0,1:T(8,128)(2,1)} async-done(((bf16[256,1,128]{2,0,1:T(8,128)(2,1)}), bf16[16384,1,128]{2,0,1:T(8,128)(2,1)}) %all-gather.3.cloned.1.call-update) | async-done | bytes 4194320 | tf_op jit(solution)/shard_map/all_gather | solution.py:70
  214.0 194.8 %all-gather.5.cloned.1.call-done = bf16[16384,1,128]{2,0,1:T(8,128)(2,1)} async-done(((bf16[256,1,128]{2,0,1:T(8,128)(2,1)}), bf16[16384,1,128]{2,0,1:T(8,128)(2,1)}) %all-gather.5.cloned.1.call-update) | async-done | bytes 4194320 | tf_op jit(solution)/shard_map/all_gather | solution.py:71
  408.9 170.5 %while.21 = (s32[]{:T(128)}, f32[2,128,1,6]{1,3,2,0:T(8,128)S(1)}, f32[2,128,1,6]{1,3,2,0:T(8,128)S(1)}, f32[2,128,1,6,128]{4,1,3,2,0:T(8,128)S(1)}, s32[128]{0:...) while((s32[]{:T(128)}, f32[2,128,1,6]{1,3,2,0:T(8,128)S(1)}, ...), condition=%wide.region_12.13_spmd.clone, body=%wide.region_1.12_spmd.clone.sunk | while | flops 823473024 | bytes 27289904 | solution.py:101
  412.9 2.6 conditional.6
  416.8 2.6 conditional.7
  423.6 2.6 conditional.6
  434.2 2.6 conditional.6
  444.9 2.6 conditional.6
  448.8 2.6 conditional.7
  455.5 2.6 conditional.6
  466.2 2.6 conditional.6
  470.1 2.6 conditional.7
  476.8 2.6 conditional.6
  487.5 2.6 conditional.6
  491.4 2.6 conditional.7
  498.1 2.6 conditional.6
  508.8 2.6 conditional.6
  512.7 2.6 conditional.7
  519.5 2.6 conditional.6
  530.1 2.6 conditional.6
  534.0 2.6 conditional.7
  540.8 2.6 conditional.6
  551.4 2.6 conditional.6
  555.3 2.6 conditional.7
  562.1 2.6 conditional.6
  572.7 2.6 conditional.6
  576.6 2.6 conditional.7
  580.4 20.7 %all_to_all.69 = bf16[8,32,768]{2,1,0:T(8,128)(2,1)S(1)} all-to-all(bf16[8,32,768]{2,1,0:T(8,128)(2,1)S(1)} %all_to_all.59), channel_id=1, replica_groups=mesh['head'=8,'inner'=8,'outer'=8] {'head'}, dimensions={0} | all-to-all | bytes 786432 | tf_op jit(solution)/shard_map/all_to_all | solution.py:105
  (432 shorter events, 153.8 us)
Async XLA Ops:
  6.5 0.8 copy-start
  6.5 402.3 %copy-start.1 = (s32[128]{0:T(128)S(1)}, s32[128]{0:T(128)}, u32[]{:S(2)}) copy-start(s32[128]{0:T(128)} %param.13) | copy-start | bytes 1540
  6.5 207.5 %all-gather.3.cloned.1.call-start = ((), (), s32[]{:S(2)}) async-start(), calls=%async_computation.4 | async-start | bytes 4259840 | tf_op jit(solution)/shard_map/all_gather | solution.py:70
  22.8 386.0 %all-gather.5.cloned.1.call-start = ((), (), s32[]{:S(2)}) async-start(), calls=%async_computation.5 | async-start | bytes 4259840 | tf_op jit(solution)/shard_map/all_gather | solution.py:71
  36.9 15.8 %all-to-all-start.2 = ((bf16[32,8,768]{2,0,1:T(8,128)(2,1)}), bf16[32,8,768]{2,0,1:T(8,128)(2,1)S(1)}, u32[]{:S(2)}, u32[]{:S(2)}) async-start(bf16[32,8,768]{2,0,1:T(8,128)(2,1)} %bitcast.216), calls=%async_computation.2 | async-start | bytes 786432 | tf_op jit(solution)/shard_map/all_to_all | solution.py:34
Sparse Core Ops, SparseCore 0:
  22.9 191.0 all-gather.2
  216.1 192.6 all-gather.4
where the time goes:
time: 610 us; the launch traced here: 609 us
  waiting for transfers between devices  367 us (60%)
  matrix products  53.7 us (9%)
  blocking collectives  47.5 us (8%)
  other arithmetic  45.2 us (7%)
  loops' own time  44.5 us (7%)
  local copies, waits for them, and re-layouts  33.9 us (6%)
  between operations  13.5 us (2%)
    all_gather x1, waiting for transfers between devices, shards(): piece_v = lax.all_gather(kv_values, ('inner', 'outer'), axis=0, tiled=True)  195 us
    all_gather x1, waiting for transfers between devices, shards(): piece_k = lax.all_gather(kv_keys, ('inner', 'outer'), axis=0, tiled=True)  161 us
    another operation x1, loops' own time, shards(): lax.fori_loop(0, nblocks, one_block, (start_top, start_total, start_sum))  42.7 us
    dot_general x32, matrix products, tile_update(): jnp.einsum('tkgs,skd->tkgd', weight, vblock, preferred_element_type=jnp.f...  34.2 us
    reduce_sum x32, other arithmetic, tile_update(): total = total * factor + jnp.sum(expo, axis=-1)  21.3 us
    all_to_all x1, blocking collectives, shards(): lax.all_to_all(attention_output, 'head', split_axis=0, concat_axis=1, til...  20.7 us
    dot_general x32, matrix products, tile_update(): jnp.einsum('tkgd,skd->tkgs', qchunk, kblock, preferred_element_type=jnp.f...  19.5 us
    dynamic_slice x16, local copies, waits for them, and re-layouts, one_block(): kblock = lax.dynamic_slice_in_dim(piece_k, kstart, block_rows, 0)  17.1 us
  transfers between devices with their start and end apart: 3, of which 3 were waited for; matrix products, arithmetic and copies ran while one was open for 1% of the time, Pallas kernels for 0%

commit v1 on v0

v1 whole, which is shorter than its diff:
```python
import functools
import math

import jax
import jax.numpy as jnp
from jax import lax
from jax.experimental import pallas as pl
from jax.experimental.pallas import tpu as pltpu
from jax.sharding import Mesh, PartitionSpec as P

HEADS = 8
GROUP = 6
HD = 128
CH = 128
ROWS = GROUP * CH
NX, NZ = 4, 8
BLOCKS = 2 * NX * NZ
SLICE = CH // 4
C = math.log2(math.e) / math.sqrt(HD)
LOW = -1e30
MASKED = -3e38
GB = 4
OUTR = HD + 16


def positions(order):
    x, zhi, zlo, core = (lax.axis_index(a) for a in ("x", "zhi", "zlo", "core"))
    shard = jnp.arange(NX * NZ, dtype=jnp.int32)
    piece = shard // NZ
    xs = (x + jnp.where(piece == 2, 3, jnp.where(piece == 3, 2, piece))) % NX
    zs = shard % NZ

    def blocks_of(xv, zv, cv):
        r = (xv * NZ + zv) * 2 + cv
        return (r[:, None] * 2 + jnp.arange(2, dtype=jnp.int32)[None, :]).reshape(-1)

    table = jnp.arange(order.shape[0], dtype=jnp.int32)

    def look(ids):
        return jnp.sum(jnp.where(ids[:, None] == table[None, :], order[None, :], 0), axis=1)

    kseq = look(blocks_of(xs, zs, core))
    own = jnp.stack([core, 1 - core])
    qseq = look(blocks_of(jnp.full(2, x), jnp.full(2, zhi * 4 + zlo), own))
    before = kseq[None, :] < qseq[:, None]
    same = kseq[None, :] == qseq[:, None]
    nfull = jnp.sum(before, axis=1)
    rank = jnp.where(before, jnp.cumsum(before, axis=1) - 1, jnp.where(same, nfull[:, None], -1))
    slot = jnp.arange(BLOCKS + 8, dtype=jnp.int32)
    lists = jnp.sum(
        jnp.where(rank[:, :, None] == slot[None, None, :], jnp.arange(BLOCKS)[None, :, None], 0), axis=1
    )
    count = nfull + jnp.sum(same, axis=1)
    return (
        lists.astype(jnp.int32),
        count.astype(jnp.int32),
        (nfull // GB).astype(jnp.int32),
        kseq.astype(jnp.int32),
        qseq.astype(jnp.int32),
    )


def attend(lst, cnt, full, kseq, qseq, q_ref, qo_ref, kv0, kv1, kv2, kv3a, kv3b, own_ref, ownl_ref, send_ref,
           qt, kbuf, vt, acc, top):
    for piece, refs in enumerate(((kv0,), (kv1,), (kv2,), (kv3a, kv3b))):
        for z in range(NZ):
            for w in range(2):
                at = ((piece * NZ + z) * 2 + w) * CH
                for i in range(4):
                    y = 4 * w + i
                    src = refs[0] if len(refs) == 1 else refs[y // 4]
                    yy = y if len(refs) == 1 else y % 4
                    kbuf[at + i * SLICE : at + (i + 1) * SLICE, :] = src[yy, z, :, :HD]
                v = jnp.concatenate(
                    [
                        (refs[0] if len(refs) == 1 else refs[w])[(4 * w + i) if len(refs) == 1 else i, z, :, HD:]
                        for i in range(4)
                    ],
                    axis=0,
                )
                vt[:HD, at : at + CH] = v.T
    vt[HD:, :] = jnp.ones((OUTR - HD, vt.shape[1]), jnp.bfloat16)
    for j in range(4):
        src = q_ref if j < 2 else qo_ref
        for h in range(GROUP):
            t = src[(j % 2) * CH : (j % 2 + 1) * CH, h * HD : (h + 1) * HD].T.astype(jnp.float32) * C
            hi = t.astype(jnp.bfloat16)
            qt[:HD, h * CH : (h + 1) * CH] = hi
            qt[HD:, h * CH : (h + 1) * CH] = (t - hi.astype(jnp.float32)).astype(jnp.bfloat16)
        acc[...] = jnp.zeros_like(acc)
        top[...] = jnp.full_like(top, LOW)

        def step(base, masked):
            ks, vs, ok = [], [], []
            for g in range(GB):
                s = lst[j, base + g]
                r = pl.multiple_of(s * CH, CH)
                ks.append(kbuf[pl.ds(r, CH), :])
                vs.append(vt[:, pl.ds(r, CH)])
                if masked:
                    kpos = jnp.where(base + g < cnt[j], kseq[s], 1 << 20) * CH
                    ok.append(
                        kpos + lax.broadcasted_iota(jnp.int32, (CH, CH), 0)
                        <= qseq[j] * CH + lax.broadcasted_iota(jnp.int32, (CH, CH), 1)
                    )
            k = jnp.concatenate(ks, axis=0)
            k = jnp.concatenate([k, k], axis=1)
            v = jnp.concatenate(vs, axis=1)
            parts = 3
            width = ROWS // parts
            scores = [
                jnp.dot(k, qt[:, c * width : (c + 1) * width], preferred_element_type=jnp.float32)
                for c in range(parts)
            ]
            if masked:
                okay = jnp.concatenate(ok, axis=0)
                okay = jnp.concatenate([okay] * (width // CH), axis=1)
            for c in range(parts):
                s = scores[c]
                if masked:
                    s = jnp.where(okay, s, MASKED)
                cs = slice(c * width, (c + 1) * width)
                old = top[0:1, cs]
                new = jnp.maximum(old, jnp.max(s, axis=0, keepdims=True))
                p = jnp.exp2(s - new).astype(jnp.bfloat16)
                acc[:, cs] = acc[:, cs] * jnp.exp2(old - new) + jnp.dot(v, p, preferred_element_type=jnp.float32)
                top[0:1, cs] = new

        lax.fori_loop(0, full[j], lambda i, c: (step(i * GB, False), c)[1], 0)

        @pl.when(full[j] * GB < cnt[j])
        def _():
            step(full[j] * GB, True)

        total = acc[HD : HD + 1]
        some = total > 0
        safe = jnp.where(some, total, 1.0)
        out = acc[:HD] * jnp.where(some, 1.0 / safe, 0.0)
        level = top[0:1] + jnp.log2(safe)
        if j < 2:
            own_ref[j] = out
            ownl_ref[j] = level
        else:
            send_ref[j - 2, :HD] = out.astype(jnp.bfloat16)
            hi = level.astype(jnp.bfloat16)
            rest = level - hi.astype(jnp.float32)
            mid = rest.astype(jnp.bfloat16)
            low = (rest - mid.astype(jnp.float32)).astype(jnp.bfloat16)
            at = lax.broadcasted_iota(jnp.int32, (OUTR - HD, ROWS), 0)
            rows = jnp.where(at == 0, hi.astype(jnp.float32), jnp.where(at == 1, mid.astype(jnp.float32), low.astype(jnp.float32)))
            send_ref[j - 2, HD:] = rows.astype(jnp.bfloat16)


def merge(own_ref, ownl_ref, got_ref, out_ref):
    for j in range(2):
        tail = got_ref[j, HD:].astype(jnp.float32)
        theirs = tail[0:1] + tail[1:2] + tail[2:3]
        mine = ownl_ref[j]
        high = jnp.maximum(mine, theirs)
        a, b = jnp.exp2(mine - high), jnp.exp2(theirs - high)
        inv = 1.0 / (a + b)
        out = own_ref[j] * (a * inv) + got_ref[j, :HD].astype(jnp.float32) * (b * inv)
        for h in range(GROUP):
            out_ref[j * CH : (j + 1) * CH, h * HD : (h + 1) * HD] = (
                out[:, h * CH : (h + 1) * CH].T.astype(jnp.bfloat16)
            )


def shards(queries, keys, values, order):
    smem = pl.BlockSpec(memory_space=pltpu.SMEM)
    vmem = pl.BlockSpec(memory_space=pltpu.VMEM)
    f32, bf16 = jnp.float32, jnp.bfloat16

    def turn(n, s):
        return [(i, (i + s) % n) for i in range(n)]

    kv = jnp.concatenate([keys.reshape(SLICE, HEADS, HD), values.reshape(SLICE, HEADS, HD)], axis=2)
    kv = jnp.broadcast_to(kv.transpose(1, 0, 2)[:, None], (HEADS, NZ, SLICE, 2 * HD))
    kv = lax.all_to_all(
        kv.reshape(HEADS * NZ, SLICE, 2 * HD), ("head", "zhi", "zlo"), split_axis=0, concat_axis=0, tiled=True
    )
    kv0 = kv.reshape(HEADS, NZ, SLICE, 2 * HD)
    q = lax.all_to_all(queries, "head", split_axis=1, concat_axis=0, tiled=True)
    kv1 = lax.ppermute(kv0, "x", turn(NX, -1))
    kv3 = lax.ppermute(kv0, "x", turn(NX, 1))
    qo = lax.ppermute(q, "core", turn(2, 1))
    kv2a = lax.ppermute(kv1[:4], "x", turn(NX, -1))
    kv2b = lax.ppermute(kv3[4:], "x", turn(NX, 1))
    tables = positions(order)
    own, ownl, send = pl.pallas_call(
        attend,
        out_shape=(
            jax.ShapeDtypeStruct((2, HD, ROWS), f32),
            jax.ShapeDtypeStruct((2, 1, ROWS), f32),
            jax.ShapeDtypeStruct((2, OUTR, ROWS), bf16),
        ),
        in_specs=[smem] * 5 + [vmem] * 7,
        out_specs=(vmem,) * 3,
        scratch_shapes=[
            pltpu.VMEM((2 * HD, ROWS), bf16),
            pltpu.VMEM((BLOCKS * CH, HD), bf16),
            pltpu.VMEM((OUTR, BLOCKS * CH), bf16),
            pltpu.VMEM((OUTR, ROWS), f32),
            pltpu.VMEM((8, ROWS), f32),
        ],
        compiler_params=pltpu.CompilerParams(vmem_limit_bytes=56 << 20),
        name="attend",
    )(*tables, q, qo, kv0, kv1, kv3, kv2a, kv2b)
    got = lax.ppermute(send, "core", turn(2, 1))
    out = pl.pallas_call(
        merge,
        out_shape=jax.ShapeDtypeStruct((2 * CH, ROWS), bf16),
        in_specs=[vmem] * 3,
        out_specs=vmem,
        compiler_params=pltpu.CompilerParams(vmem_limit_bytes=32 << 20),
        name="merge",
    )(own, ownl, got)
    return lax.all_to_all(out, "head", split_axis=0, concat_axis=1, tiled=True)


def solution(mesh):
    split = Mesh(mesh.devices.reshape(HEADS, 4, 2, NX, 2), ("head", "zlo", "core", "x", "zhi"))
    rows = P(("x", "zhi", "zlo", "core", "head"), None)
    return jax.shard_map(
        shards, mesh=split, in_specs=(rows, rows, rows, P()), out_specs=rows, check_vma=False
    )
```

time: 610 us -> 157 us (0.26)
  the two profiles are of different devices: /device:TPU:192 before, /device:TPU:1 now
where the time goes in v1:
time: 157 us; the launch traced here: 154 us
  starting transfers between devices  48.3 us (31%)
  waiting for transfers between devices  43.5 us (28%)
  Pallas kernels  30.4 us (19%)
  blocking collectives  20 us (13%)
  local copies, waits for them, and re-layouts  8.19 us (5%)
  other arithmetic  3.69 us (2%)
    pallas_call x1, Pallas kernels, shards(): pl.pallas_call(attend, out_shape=(jax.ShapeDtypeStruct((2, HD, ROWS), f32...  30.2 us
    all_to_all x1, waiting for transfers between devices, shards(): lax.all_to_all(kv.reshape(HEADS * NZ, SLICE, 2 * HD), ('head', 'zhi', 'zl...  25.9 us
    all_to_all x1, blocking collectives, shards(): return lax.all_to_all(out, 'head', split_axis=0, concat_axis=1, tiled=True)  20 us
    all_to_all x1, starting transfers between devices, shards(): lax.all_to_all(kv.reshape(HEADS * NZ, SLICE, 2 * HD), ('head', 'zhi', 'zl...  17.3 us
    ppermute x1, waiting for transfers between devices, shards(): kv3 = lax.ppermute(kv0, 'x', turn(NX, 1))  8.07 us
    all_to_all x1, starting transfers between devices, shards(): q = lax.all_to_all(queries, 'head', split_axis=1, concat_axis=0, tiled=True)  6.55 us
    ppermute x1, starting transfers between devices, shards(): got = lax.ppermute(send, 'core', turn(2, 1))  6.15 us
    ppermute x1, starting transfers between devices, shards(): qo = lax.ppermute(q, 'core', turn(2, 1))  5.35 us
  transfers between devices with their start and end apart: 8, of which 6 were waited for; matrix products, arithmetic and copies ran while one was open for 4% of the time, Pallas kernels for 0%

profile of v1, /device:TPU:1, one launch (start us, length us, event | category | flops | bytes accessed | tf_op | source)
XLA Modules:
  0.0 154.4 jit_solution(12919925760293789164)
XLA Ops:
  0.0 0.9 copy.16
  1.0 1.1 broadcast_in_dim.80
  2.1 17.3 %all-to-all-start.1 = ((bf16[64,32,256]{2,1,0:T(8,128)(2,1)}), bf16[64,32,256]{2,1,0:T(8,128)(2,1)S(1)}, u32[]{:S(2)}, u32[]{:S(2)}) async-start(bf16[64,32,256]{2,1,0:T(8,128)(2,1)} %bitcast.6), calls=%async_computation.1 | async-start | bytes 2097152 | tf_op jit(solution)/shard_map/all_to_all | solution.py:179
  19.4 0.8 copy.19
  20.2 25.9 %all-to-all-done.1 = bf16[64,32,256]{2,1,0:T(8,128)(2,1)S(1)} async-done(((bf16[64,32,256]{2,1,0:T(8,128)(2,1)}), bf16[64,32,256]{2,1,0:T(8,128)(2,1)S(1)}, u32[]{:S(2)}, u32[]{:S(2)}) %all-to-all-start.1) | async-done | bytes 1048608 | tf_op jit(solution)/shard_map/all_to_all | solution.py:179
  46.1 6.6 %all-to-all-start = ((bf16[32,8,768]{2,0,1:T(8,128)(2,1)}), bf16[32,8,768]{2,0,1:T(8,128)(2,1)S(1)}, u32[]{:S(2)}, u32[]{:S(2)}) async-start(bf16[32,8,768]{2,0,1:T(8,128)(2,1)} %bitcast.20), calls=%async_computation | async-start | bytes 786432 | tf_op jit(solution)/shard_map/all_to_all | solution.py:183
  52.6 3.1 %collective-permute-start.2 = (bf16[8,8,32,256]{3,2,1,0:T(8,128)(2,1)S(1)}, bf16[8,8,32,256]{3,2,1,0:T(8,128)(2,1)S(1)}, u32[]{:S(2)}, u32[]{:S(2)}) collective-permute-start(bf16[8,8,32,256]{3,2,1,0:T(8,128)(2,1)S(1)} %bitcast.22), channel_id=1, source_target_pairs={{0,2},{2,4},{4,6},{6,0},{1,3},{3,5},{5,7},{7,1},{8,10},{10,12},{12... | collective-permute-start | bytes 3145736 | tf_op jit(solution)/shard_map/ppermute | solution.py:185
  55.8 3.4 %collective-permute-start.1 = (bf16[8,8,32,256]{3,2,1,0:T(8,128)(2,1)S(1)}, bf16[8,8,32,256]{3,2,1,0:T(8,128)(2,1)S(1)}, u32[]{:S(2)}, u32[]{:S(2)}) collective-permute-start(bf16[8,8,32,256]{3,2,1,0:T(8,128)(2,1)S(1)} %bitcast.23), channel_id=1, source_target_pairs={{0,6},{2,0},{4,2},{6,4},{1,7},{3,1},{5,3},{7,5},{8,14},{10,8},{12,... | collective-permute-start | bytes 3145736 | tf_op jit(solution)/shard_map/ppermute | solution.py:184
  59.2 0.6 add.130
  59.9 0.7 add.123
  60.6 0.9 select_reduce_fusion.2.qseq
  61.8 0.2 reduce_window_sum.11
  62.0 0.7 fusion
  62.7 2.1 %all-to-all-done = bf16[32,8,768]{2,0,1:T(8,128)(2,1)S(1)} async-done(((bf16[32,8,768]{2,0,1:T(8,128)(2,1)}), bf16[32,8,768]{2,0,1:T(8,128)(2,1)S(1)}, u32[]{:S(2)}, u32[]{:S(2)}) %all-to-all-start) | async-done | bytes 393248 | tf_op jit(solution)/shard_map/all_to_all | solution.py:183
  64.8 5.3 %collective-permute-start = (bf16[256,768]{1,0:T(8,128)(2,1)S(1)}, bf16[256,768]{1,0:T(8,128)(2,1)S(1)}, u32[]{:S(2)}, u32[]{:S(2)}) collective-permute-start(bf16[256,768]{1,0:T(8,128)(2,1)S(1)} %bitcast.25), channel_id=1, source_target_pairs={{0,8},{8,0},{1,9},{9,1},{2,10},{10,2},{3,11},{11,3},{4,12},{12,4},... | collective-permute-start | bytes 1179656 | tf_op jit(solution)/shard_map/ppermute | solution.py:186
  70.2 8.1 %collective-permute-done.2.kv2 = bf16[8,8,32,256]{3,2,1,0:T(8,128)(2,1)S(1)} collective-permute-done((bf16[8,8,32,256]{3,2,1,0:T(8,128)(2,1)S(1)}, bf16[8,8,32,256]{3,2,1,0:T(8,128)(2,1)S(1)}, u32[]{:S(2)}, u32[]{:S(2)}) %collective-permute-start.2) | collective-permute-done | bytes 1048608 | tf_op jit(solution)/shard_map/ppermute | solution.py:185
  78.3 1.9 %collective-permute-start.4 = (bf16[4,8,32,256]{3,2,1,0:T(8,128)(2,1)S(1)}, bf16[4,8,32,256]{3,2,1,0:T(8,128)(2,1)S(1)}, u32[]{:S(2)}, u32[]{:S(2)}) collective-permute-start(bf16[4,8,32,256]{3,2,1,0:T(8,128)(2,1)S(1)} %slice.9), channel_id=1, source_target_pairs={{0,2},{2,4},{4,6},{6,0},{1,3},{3,5},{5,7},{7,1},{8,10},{10,12},{12... | collective-permute-start | bytes 1572872 | tf_op jit(solution)/shard_map/ppermute | solution.py:188
  80.3 4.6 %collective-permute-start.3 = (bf16[4,8,32,256]{3,2,1,0:T(8,128)(2,1)S(1)}, bf16[4,8,32,256]{3,2,1,0:T(8,128)(2,1)S(1)}, u32[]{:S(2)}, u32[]{:S(2)}) collective-permute-start(bf16[4,8,32,256]{3,2,1,0:T(8,128)(2,1)S(1)} %slice.8), channel_id=1, source_target_pairs={{0,6},{2,0},{4,2},{6,4},{1,7},{3,1},{5,3},{7,5},{8,14},{10,8},{12,... | collective-permute-start | bytes 1572872 | tf_op jit(solution)/shard_map/ppermute | solution.py:187
  85.0 0.7 select_reduce_fusion.lst
  85.7 0.6 copy-done.14
  86.3 0.5 and_select_fusion
  86.9 4.9 %collective-permute-done.4.kv3b = bf16[4,8,32,256]{3,2,1,0:T(8,128)(2,1)S(1)} collective-permute-done((bf16[4,8,32,256]{3,2,1,0:T(8,128)(2,1)S(1)}, bf16[4,8,32,256]{3,2,1,0:T(8,128)(2,1)S(1)}, u32[]{:S(2)}, u32[]{:S(2)}) %collective-permute-start.4) | collective-permute-done | bytes 524320 | tf_op jit(solution)/shard_map/ppermute | solution.py:188
  91.8 1.0 collective-permute-done.3.kv3a
  92.8 0.8 copy-done.7
  93.6 30.2 %attend.1 = (f32[2,128,768]{2,1,0:T(8,128)}, f32[2,1,768]{2,1,0:T(1,128)}, bf16[2,144,768]{2,1,0:T(8,128)(2,1)}) custom-call(s32[4,72]{1,0:T(4,128)} %select_reduce_fusion.lst, s32[4]{0:T(128)} %get-tuple-element.14.cnt, s32[4]{0:T(128)} %get-tuple-element.13.full, s32[64]{0:T(128)} %copy-done.12, s32[4]{0:T(128)} %copy-done.11, bf16[256,768]{1,0:T(8,128)(2,1)} %bitcast.26, ...), custom_call_target="tpu_custom_call" | custom-call | tf_op jit(solution)/shard_map/attend/pallas_call | solution.py:190
  123.7 6.1 %collective-permute-start.5 = (bf16[2,144,768]{2,1,0:T(8,128)(2,1)}, bf16[2,144,768]{2,1,0:T(8,128)(2,1)S(1)}, u32[]{:S(2)}, u32[]{:S(2)}) collective-permute-start(bf16[2,144,768]{2,1,0:T(8,128)(2,1)} %get-tuple-element.10), channel_id=1, source_target_pairs={{0,8},{8,0},{1,9},{9,1},{2,10},{10,2},{3,11},{11,3},{4,12},{12,4},... | collective-permute-start | bytes 1327112 | tf_op jit(solution)/shard_map/ppermute | solution.py:209
  129.9 1.6 %collective-permute-done.5.got_ref = bf16[2,144,768]{2,1,0:T(8,128)(2,1)S(1)} collective-permute-done((bf16[2,144,768]{2,1,0:T(8,128)(2,1)}, bf16[2,144,768]{2,1,0:T(8,128)(2,1)S(1)}, u32[]{:S(2)}, u32[]{:S(2)}) %collective-permute-start.5) | collective-permute-done | bytes 442400 | tf_op jit(solution)/shard_map/ppermute | solution.py:209
  131.5 1.1 copy-done
  132.6 0.7 copy-done.1
  133.3 0.2 merge.1
  133.6 20.0 %all_to_all.43 = bf16[8,32,768]{2,1,0:T(8,128)(2,1)S(1)} all-to-all(bf16[8,32,768]{2,1,0:T(8,128)(2,1)S(1)} %bitcast.21), channel_id=1, replica_groups=mesh['head'=8,'zlo'=4,'core'=2,'x'=4,'zhi'=2] {'head'}, dimensions={0} | all-to-all | bytes 786432 | tf_op jit(solution)/shard_map/all_to_all | solution.py:218
  153.6 0.8 copy.15
  (44 shorter events, 0.7 us)
Async XLA Ops:
  0.0 0.9 copy-start.10
  2.1 17.3 %copy-start.9 = (bf16[32,6144]{1,0:T(8,128)(2,1)S(1)}, bf16[32,6144]{1,0:T(8,128)(2,1)}, u32[]{:S(2)}) copy-start(bf16[32,6144]{1,0:T(8,128)(2,1)} %param.4) | copy-start | bytes 1179652
  2.1 44.0 %all-to-all-start.1 = ((bf16[64,32,256]{2,1,0:T(8,128)(2,1)}), bf16[64,32,256]{2,1,0:T(8,128)(2,1)S(1)}, u32[]{:S(2)}, u32[]{:S(2)}) async-start(bf16[64,32,256]{2,1,0:T(8,128)(2,1)} %bitcast.6), calls=%async_computation.1 | async-start | bytes 2097152 | tf_op jit(solution)/shard_map/all_to_all | solution.py:179
  46.1 34.2 %copy-start.2 = (bf16[64,32,256]{2,1,0:T(8,128)(2,1)}, bf16[64,32,256]{2,1,0:T(8,128)(2,1)S(1)}, u32[]{:S(2)}) copy-start(bf16[64,32,256]{2,1,0:T(8,128)(2,1)S(1)} %all-to-all-done.1) | copy-start | bytes 3145732
  46.1 18.7 %all-to-all-start = ((bf16[32,8,768]{2,0,1:T(8,128)(2,1)}), bf16[32,8,768]{2,0,1:T(8,128)(2,1)S(1)}, u32[]{:S(2)}, u32[]{:S(2)}) async-start(bf16[32,8,768]{2,0,1:T(8,128)(2,1)} %bitcast.20), calls=%async_computation | async-start | bytes 786432 | tf_op jit(solution)/shard_map/all_to_all | solution.py:183
  52.6 25.6 %collective-permute-start.2 = (bf16[8,8,32,256]{3,2,1,0:T(8,128)(2,1)S(1)}, bf16[8,8,32,256]{3,2,1,0:T(8,128)(2,1)S(1)}, u32[]{:S(2)}, u32[]{:S(2)}) collective-permute-start(bf16[8,8,32,256]{3,2,1,0:T(8,128)(2,1)S(1)} %bitcast.22), channel_id=1, source_target_pairs={{0,2},{2,4},{4,6},{6,0},{1,3},{3,5},{5,7},{7,1},{8,10},{10,12},{12... | collective-permute-start | bytes 3145736 | tf_op jit(solution)/shard_map/ppermute | solution.py:185
  55.8 24.5 %collective-permute-start.1 = (bf16[8,8,32,256]{3,2,1,0:T(8,128)(2,1)S(1)}, bf16[8,8,32,256]{3,2,1,0:T(8,128)(2,1)S(1)}, u32[]{:S(2)}, u32[]{:S(2)}) collective-permute-start(bf16[8,8,32,256]{3,2,1,0:T(8,128)(2,1)S(1)} %bitcast.23), channel_id=1, source_target_pairs={{0,6},{2,0},{4,2},{6,4},{1,7},{3,1},{5,3},{7,5},{8,14},{10,8},{12,... | collective-permute-start | bytes 3145736 | tf_op jit(solution)/shard_map/ppermute | solution.py:184
  60.6 0.9 copy-start.15
  60.6 0.9 copy-start.16
  61.5 23.4 %copy-start.11 = (s32[4]{0:T(128)}, s32[4]{0:T(128)S(1)}, u32[]{:S(2)}) copy-start(s32[4]{0:T(128)S(1)} %select_reduce_fusion.2.qseq) | copy-start | bytes 52
  61.7 23.2 %copy-start.12 = (s32[64]{0:T(128)}, s32[64]{0:T(128)S(1)}, u32[]{:S(2)}) copy-start(s32[64]{0:T(128)S(1)} %select_reduce_fusion.1.kseq) | copy-start | bytes 772
  64.8 13.5 %copy-start.5 = (bf16[32,8,768]{2,0,1:T(8,128)(2,1)}, bf16[32,8,768]{2,0,1:T(8,128)(2,1)S(1)}, u32[]{:S(2)}) copy-start(bf16[32,8,768]{2,0,1:T(8,128)(2,1)S(1)} %all-to-all-done) | copy-start | bytes 1179652
  64.8 22.1 %collective-permute-start = (bf16[256,768]{1,0:T(8,128)(2,1)S(1)}, bf16[256,768]{1,0:T(8,128)(2,1)S(1)}, u32[]{:S(2)}, u32[]{:S(2)}) collective-permute-start(bf16[256,768]{1,0:T(8,128)(2,1)S(1)} %bitcast.25), channel_id=1, source_target_pairs={{0,8},{8,0},{1,9},{9,1},{2,10},{10,2},{3,11},{11,3},{4,12},{12,4},... | collective-permute-start | bytes 1179656 | tf_op jit(solution)/shard_map/ppermute | solution.py:186
  78.3 6.7 %copy-start.3 = (bf16[8,8,32,256]{3,2,1,0:T(8,128)(2,1)}, bf16[8,8,32,256]{3,2,1,0:T(8,128)(2,1)S(1)}, u32[]{:S(2)}) copy-start(bf16[8,8,32,256]{3,2,1,0:T(8,128)(2,1)S(1)} %collective-permute-done.2.kv2) | copy-start | bytes 3145732
  78.3 13.5 %collective-permute-start.4 = (bf16[4,8,32,256]{3,2,1,0:T(8,128)(2,1)S(1)}, bf16[4,8,32,256]{3,2,1,0:T(8,128)(2,1)S(1)}, u32[]{:S(2)}, u32[]{:S(2)}) collective-permute-start(bf16[4,8,32,256]{3,2,1,0:T(8,128)(2,1)S(1)} %slice.9), channel_id=1, source_target_pairs={{0,2},{2,4},{4,6},{6,0},{1,3},{3,5},{5,7},{7,1},{8,10},{10,12},{12... | collective-permute-start | bytes 1572872 | tf_op jit(solution)/shard_map/ppermute | solution.py:188
  80.2 12.5 %copy-start.4 = (bf16[8,8,32,256]{3,2,1,0:T(8,128)(2,1)}, bf16[8,8,32,256]{3,2,1,0:T(8,128)(2,1)S(1)}, u32[]{:S(2)}) copy-start(bf16[8,8,32,256]{3,2,1,0:T(8,128)(2,1)S(1)} %collective-permute-done.1.kv1) | copy-start | bytes 3145732
  80.3 4.6 %copy-start.13 = (s32[4]{0:T(128)S(1)}, s32[4]{0:T(128)}, u32[]{:S(2)}) copy-start(s32[4]{0:T(128)} %get-tuple-element.12) | copy-start | bytes 52
  80.3 12.5 %collective-permute-start.3 = (bf16[4,8,32,256]{3,2,1,0:T(8,128)(2,1)S(1)}, bf16[4,8,32,256]{3,2,1,0:T(8,128)(2,1)S(1)}, u32[]{:S(2)}, u32[]{:S(2)}) collective-permute-start(bf16[4,8,32,256]{3,2,1,0:T(8,128)(2,1)S(1)} %slice.8), channel_id=1, source_target_pairs={{0,6},{2,0},{4,2},{6,4},{1,7},{3,1},{5,3},{7,5},{8,14},{10,8},{12,... | collective-permute-start | bytes 1572872 | tf_op jit(solution)/shard_map/ppermute | solution.py:187
  85.7 0.6 copy-start.14
  86.9 5.9 %copy-start.8 = (bf16[256,768]{1,0:T(8,128)(2,1)}, bf16[256,768]{1,0:T(8,128)(2,1)S(1)}, u32[]{:S(2)}) copy-start(bf16[256,768]{1,0:T(8,128)(2,1)S(1)} %collective-permute-done.qo_ref) | copy-start | bytes 1179652
  91.8 1.0 copy-start.6
  92.8 0.8 copy-start.7
  123.7 7.8 %collective-permute-start.5 = (bf16[2,144,768]{2,1,0:T(8,128)(2,1)}, bf16[2,144,768]{2,1,0:T(8,128)(2,1)S(1)}, u32[]{:S(2)}, u32[]{:S(2)}) collective-permute-start(bf16[2,144,768]{2,1,0:T(8,128)(2,1)} %get-tuple-element.10), channel_id=1, source_target_pairs={{0,8},{8,0},{1,9},{9,1},{2,10},{10,2},{3,11},{11,3},{4,12},{12,4},... | collective-permute-start | bytes 1327112 | tf_op jit(solution)/shard_map/ppermute | solution.py:209
  131.5 1.1 copy-start
  132.6 0.7 copy-start.1

commit v2 on v1

v2 whole, which is shorter than its diff:
```python
import functools
import math

import jax
import jax.numpy as jnp
from jax import lax
from jax.experimental import pallas as pl
from jax.experimental.pallas import tpu as pltpu
from jax.sharding import Mesh, PartitionSpec as P

HEADS = 8
GROUP = 6
HD = 128
CH = 128
ROWS = GROUP * CH
NX, NZ = 4, 8
SLICE = CH // 4
C = math.log2(math.e) / math.sqrt(HD)
LOW = -1e30
MASKED = -3e38
GB = 4
WIDTH = 256
BEHIND = 0
OUTR = HD + 16
F32, BF16 = jnp.float32, jnp.bfloat16


def spread_queries(q_ref, qt, j, w):
    for h in range(GROUP):
        t = q_ref[w * CH : (w + 1) * CH, h * HD : (h + 1) * HD].T.astype(F32) * C
        hi = t.astype(BF16)
        qt[j, :HD, h * CH : (h + 1) * CH] = hi
        qt[j, HD:, h * CH : (h + 1) * CH] = (t - hi.astype(F32)).astype(BF16)


def fill(piece, at, rows, kbuf, vt):
    for z in range(NZ):
        for w in range(rows // CH):
            to = (at + z * (rows // CH) + w) * CH
            block = piece[4 * w : 4 * w + 4, z].reshape(CH, 2 * HD)
            kbuf[to : to + CH, :] = block[:, :HD]
            vt[:HD, to : to + CH] = block[:, HD:].T
    return at + NZ * (rows // CH)


def attend(stage, sources, *refs):
    first, last = stage == 0, stage == 2
    order, pos = refs[:2]
    refs = refs[2:]
    pieces, refs = refs[: len(sources)], refs[len(sources) :]
    if first:
        q_ref, qo_ref, acc, top, qt = refs[:5]
        refs = refs[5:]
    elif not last:
        qt, acc_in, top_in, acc, top = refs[:5]
        refs = refs[5:]
    else:
        qt, acc_in, top_in, own_ref, ownl_ref, send_ref = refs[:6]
        refs = refs[6:]
        acc, top = acc_in, top_in
        refs, (acc, top) = refs[:-2], refs[-2:]
    kbuf, vt, sa, sb, tabj, tabk, tabv = refs
    x, z, core = pos[0], pos[1], pos[2]

    def stored(xv, zv, cv, w):
        return ((xv * NZ + zv) * 2 + cv) * 2 + w

    blocks = sum(NZ * (rows // CH) for _, _, rows in sources)
    dummy = blocks

    t = jnp.int32(0)
    for j in range(4):
        cv = core if j < 2 else 1 - core
        mine = order[stored(x, z, cv, j % 2)]
        n = t * GB
        start = n
        slot = 0
        for shift, y0, rows in sources:
            xv = (x + shift) % NX
            per = rows // CH

            def scan(i, n, xv=xv, y0=y0, per=per, slot=slot, mine=mine):
                w = i % per + y0 // 4
                tabk[n] = i + slot
                tabv[n] = i + slot
                return n + (order[stored(xv, i // per, core, w)] < mine).astype(jnp.int32)

            n = lax.fori_loop(0, NZ * per, scan, n, unroll=True)
            slot += NZ * per
        steps = (n - start + GB - 1) // GB
        keep = tabk[jnp.maximum(n - 1, 0)]
        for g in range(GB - 1):
            tabk[n + g] = keep
            tabv[n + g] = dummy

        def mark(i, c, j=j):
            tabj[i] = j
            return c

        lax.fori_loop(t, t + steps, mark, 0)
        t = t + steps
    for e in range(3):
        back = jnp.maximum(t - 1, 0)
        tabj[t + e] = jnp.where(t > 0, tabj[back], 0)
        for g in range(GB):
            tabk[(t + e) * GB + g] = jnp.where(t > 0, tabk[back * GB + g], 0)
            tabv[(t + e) * GB + g] = dummy

    at = 0
    for piece, (_, _, rows) in zip(pieces, sources):
        at = fill(piece, at, rows, kbuf, vt)
    vt[HD:, : blocks * CH] = jnp.ones((OUTR - HD, blocks * CH), BF16)
    vt[:, blocks * CH :] = jnp.zeros((OUTR, CH), BF16)

    def scores(i, out):
        k = jnp.concatenate(
            [kbuf[pl.ds(pl.multiple_of(tabk[i * GB + g] * CH, CH), CH), :] for g in range(GB)], axis=0
        )
        out[...] = jnp.dot(jnp.concatenate([k, k], axis=1), qt[tabj[i]], preferred_element_type=F32)

    def gather(i, s_ref):
        j = tabj[i]
        v = jnp.concatenate([vt[:, pl.ds(pl.multiple_of(tabv[i * GB + g] * CH, CH), CH)] for g in range(GB)], axis=1)
        s = s_ref[...]
        old = top[j]
        new = jnp.maximum(old, jnp.max(s, axis=0, keepdims=True))
        p = jnp.exp2(s - new).astype(BF16)
        acc[j] = acc[j] * jnp.exp2(old - new) + jnp.dot(v, p, preferred_element_type=F32)
        top[j] = new

    if first:
        for j in range(4):
            spread_queries(q_ref if j < 2 else qo_ref, qt, j, j % 2)
        below = lax.broadcasted_iota(jnp.int32, (CH, CH), 0) <= lax.broadcasted_iota(jnp.int32, (CH, CH), 1)
        below = jnp.concatenate([below] * GROUP, axis=1)
        for j in range(2):
            r = pl.multiple_of((z * 2 + j) * CH, CH)
            k = kbuf[pl.ds(r, CH), :]
            s = jnp.dot(jnp.concatenate([k, k], axis=1), qt[j], preferred_element_type=F32)
            s = jnp.where(below, s, MASKED)
            high = jnp.max(s, axis=0, keepdims=True)
            p = jnp.exp2(s - high).astype(BF16)
            acc[j] = jnp.dot(vt[:, pl.ds(r, CH)], p, preferred_element_type=F32)
            top[j] = high
        for j in range(2, 4):
            acc[j] = jnp.zeros((OUTR, ROWS), F32)
            top[j] = jnp.full((1, ROWS), LOW, F32)
    else:
        acc[...] = acc_in[...]
        top[...] = top_in[...]

    scores(0, sa)

    def both(i, s_ref, n_ref):
        j, jn = tabj[i], tabj[i + 1]
        k = jnp.concatenate(
            [kbuf[pl.ds(pl.multiple_of(tabk[(i + 1) * GB + g] * CH, CH), CH), :] for g in range(GB)], axis=0
        )
        k = jnp.concatenate([k, k], axis=1)
        v = jnp.concatenate([vt[:, pl.ds(pl.multiple_of(tabv[i * GB + g] * CH, CH), CH)] for g in range(GB)], axis=1)

        def add(cs, old, new, p):
            acc[j, :, cs] = acc[j, :, cs] * jnp.exp2(old - new) + jnp.dot(v, p, preferred_element_type=F32)
            top[j, :, cs] = new

        waiting = []
        for c in range(ROWS // WIDTH):
            cs = slice(c * WIDTH, (c + 1) * WIDTH)
            n_ref[:, cs] = jnp.dot(k, qt[jn, :, cs], preferred_element_type=F32)
            s = s_ref[:, cs]
            old = top[j, :, cs]
            new = jnp.maximum(old, jnp.max(s, axis=0, keepdims=True))
            waiting.append((cs, old, new, jnp.exp2(s - new).astype(BF16)))
            if len(waiting) > BEHIND:
                add(*waiting.pop(0))
        for w in waiting:
            add(*w)

    def pair(i, c):
        both(2 * i, sa, sb)
        both(2 * i + 1, sb, sa)
        return c

    lax.fori_loop(0, (t + 1) // 2, pair, 0)

    if last:
        for j in range(4):
            total = acc[j, HD : HD + 1]
            some = total > 0
            safe = jnp.where(some, total, 1.0)
            out = acc[j, :HD] * jnp.where(some, 1.0 / safe, 0.0)
            level = top[j] + jnp.log2(safe)
            if j < 2:
                own_ref[j] = out
                ownl_ref[j] = level
            else:
                send_ref[j - 2, :HD] = out.astype(BF16)
                hi = level.astype(BF16).astype(F32)
                mid = (level - hi).astype(BF16).astype(F32)
                row = lax.broadcasted_iota(jnp.int32, (OUTR - HD, ROWS), 0)
                tail = jnp.where(row == 0, hi, jnp.where(row == 1, mid, level - hi - mid))
                send_ref[j - 2, HD:] = tail.astype(BF16)


def merge(own_ref, ownl_ref, got_ref, out_ref):
    for j in range(2):
        tail = got_ref[j, HD:].astype(F32)
        theirs = tail[0:1] + tail[1:2] + tail[2:3]
        mine = ownl_ref[j]
        high = jnp.maximum(mine, theirs)
        a, b = jnp.exp2(mine - high), jnp.exp2(theirs - high)
        inv = 1.0 / (a + b)
        out = own_ref[j] * (a * inv) + got_ref[j, :HD].astype(F32) * (b * inv)
        for h in range(GROUP):
            out_ref[j * CH : (j + 1) * CH, h * HD : (h + 1) * HD] = (
                out[:, h * CH : (h + 1) * CH].T.astype(BF16)
            )


VMEM = pl.BlockSpec(memory_space=pltpu.VMEM)
SMEM = pl.BlockSpec(memory_space=pltpu.SMEM)
SOURCES = (((0, 0, 256),), ((1, 0, 256), (3, 0, 256)), ((2, 0, 128), (2, 4, 128)))


def call(stage, order, pos, *arrays):
    sources = SOURCES[stage]
    blocks = sum(NZ * (rows // CH) for _, _, rows in sources)
    state = (jax.ShapeDtypeStruct((4, OUTR, ROWS), F32), jax.ShapeDtypeStruct((4, 1, ROWS), F32))
    scratch = [
        pltpu.VMEM((blocks * CH, HD), BF16),
        pltpu.VMEM((OUTR, (blocks + 1) * CH), BF16),
        pltpu.VMEM((GB * CH, ROWS), F32),
        pltpu.VMEM((GB * CH, ROWS), F32),
        pltpu.SMEM((blocks + 16,), jnp.int32),
        pltpu.SMEM((GB * (blocks + 16),), jnp.int32),
        pltpu.SMEM((GB * (blocks + 16),), jnp.int32),
    ]
    if stage == 0:
        outs = state + (jax.ShapeDtypeStruct((4, 2 * HD, ROWS), BF16),)
    elif stage == 1:
        outs = state
    else:
        outs = (
            jax.ShapeDtypeStruct((2, HD, ROWS), F32),
            jax.ShapeDtypeStruct((2, 1, ROWS), F32),
            jax.ShapeDtypeStruct((2, OUTR, ROWS), BF16),
        )
        scratch += [pltpu.VMEM((4, OUTR, ROWS), F32), pltpu.VMEM((4, 1, ROWS), F32)]
    flops = blocks * 2 * 2 * 2 * HD * CH * ROWS
    return pl.pallas_call(
        functools.partial(attend, stage, sources),
        out_shape=outs,
        in_specs=[SMEM] * 2 + [VMEM] * len(arrays),
        out_specs=(VMEM,) * len(outs),
        scratch_shapes=scratch,
        cost_estimate=pl.CostEstimate(flops=2 * flops, bytes_accessed=blocks * CH * 512, transcendentals=blocks * 2 * CH * ROWS),
        compiler_params=pltpu.CompilerParams(vmem_limit_bytes=20 << 20),
        name=f"attend{stage}",
    )(order, pos, *arrays)


def shards(queries, keys, values, order):
    def turn(n, s):
        return [(i, (i + s) % n) for i in range(n)]

    kv = jnp.concatenate([keys.reshape(SLICE, HEADS, HD), values.reshape(SLICE, HEADS, HD)], axis=2)
    kv = jnp.broadcast_to(kv.transpose(1, 0, 2)[:, None], (HEADS, NZ, SLICE, 2 * HD))
    kv = lax.all_to_all(
        kv.reshape(HEADS * NZ, SLICE, 2 * HD), ("head", "zhi", "zlo"), split_axis=0, concat_axis=0, tiled=True
    )
    kv0 = kv.reshape(HEADS, NZ, SLICE, 2 * HD)
    q = lax.all_to_all(queries, "head", split_axis=1, concat_axis=0, tiled=True)
    kv1 = lax.ppermute(kv0, "x", turn(NX, -1))
    kv3 = lax.ppermute(kv0, "x", turn(NX, 1))
    qo = lax.ppermute(q, "core", turn(2, 1))
    kv2a = lax.ppermute(kv1[:4], "x", turn(NX, -1))
    kv2b = lax.ppermute(kv3[4:], "x", turn(NX, 1))
    pos = jnp.stack(
        [lax.axis_index("x"), lax.axis_index("zhi") * 4 + lax.axis_index("zlo"), lax.axis_index("core")]
    ).astype(jnp.int32)
    acc, top, qt = call(0, order, pos, kv0, q, qo)
    acc, top = call(1, order, pos, kv1, kv3, qt, acc, top)
    own, ownl, send = call(2, order, pos, kv2a, kv2b, qt, acc, top)
    got = lax.ppermute(send, "core", turn(2, 1))
    out = pl.pallas_call(
        merge,
        out_shape=jax.ShapeDtypeStruct((2 * CH, ROWS), BF16),
        in_specs=[VMEM] * 3,
        out_specs=VMEM,
        compiler_params=pltpu.CompilerParams(vmem_limit_bytes=32 << 20),
        name="merge",
    )(own, ownl, got)
    return lax.all_to_all(out, "head", split_axis=0, concat_axis=1, tiled=True)


def solution(mesh):
    split = Mesh(mesh.devices.reshape(HEADS, 4, 2, NX, 2), ("head", "zlo", "core", "x", "zhi"))
    rows = P(("x", "zhi", "zlo", "core", "head"), None)
    return jax.shard_map(
        shards, mesh=split, in_specs=(rows, rows, rows, P()), out_specs=rows, check_vma=False
    )
```

time: 157 us -> 132 us (0.84); the launches traced: 154 us -> 132 us
  waiting for transfers between devices: 43.5 us -> 35.8 us
  Pallas kernels: 30.4 us -> 25 us
  local copies, waits for them, and re-layouts: 8.19 us -> 4.47 us
  other arithmetic: 3.69 us -> 0.09 us
    ppermute x1, waiting for transfers between devices: 8.07 us -> 0.01 us  [shards(): kv3 = lax.ppermute(kv0, 'x', turn(NX, 1))]
    pallas_call x2 -> x4, Pallas kernels: 30.4 us -> 25 us  [the longest x3 24.7 us: call(): pl.pallas_call(functools.partial(attend, stage, sources), out_shape=outs,...]
    all_to_all x1, waiting for transfers between devices: 2.09 us -> 5.88 us  [shards(): q = lax.all_to_all(queries, 'head', split_axis=1, concat_axis=0, tiled=True)]
    ppermute x1, waiting for transfers between devices: 4.89 us -> 1.24 us  [shards(): kv2b = lax.ppermute(kv3[4:], 'x', turn(NX, 1))]
    reduce_sum x4 -> x0, other arithmetic: 2.5 us -> none  [the longest x2 1.08 us: look(): jnp.sum(jnp.where(ids[:, None] == table[None, :], order[None, :], 0), axi...]
    unnamed x36 -> x6, local copies, waits for them, and re-layouts: 4.16 us -> 1.71 us
  transfers between devices with their start and end apart: 8 -> 8, of which waited for: 6 -> 5; matrix products, arithmetic and copies ran while one was open for 4% -> 1% of each run, Pallas kernels for 0% -> 14%
where the time goes in v2:
time: 132 us
  starting transfers between devices  47.1 us (36%)
  waiting for transfers between devices  35.8 us (27%)
  Pallas kernels  25 us (19%)
  blocking collectives  19.2 us (15%)
  local copies, waits for them, and re-layouts  4.47 us (3%)
    all_to_all x1, waiting for transfers between devices, shards(): lax.all_to_all(kv.reshape(HEADS * NZ, SLICE, 2 * HD), ('head', 'zhi', 'zl...  25.9 us
    pallas_call x3, Pallas kernels, call(): pl.pallas_call(functools.partial(attend, stage, sources), out_shape=outs,...  24.7 us
    all_to_all x1, blocking collectives, shards(): return lax.all_to_all(out, 'head', split_axis=0, concat_axis=1, tiled=True)  19.2 us
    all_to_all x1, starting transfers between devices, shards(): lax.all_to_all(kv.reshape(HEADS * NZ, SLICE, 2 * HD), ('head', 'zhi', 'zl...  17.3 us
    all_to_all x1, starting transfers between devices, shards(): q = lax.all_to_all(queries, 'head', split_axis=1, concat_axis=0, tiled=True)  6.55 us
    all_to_all x1, waiting for transfers between devices, shards(): q = lax.all_to_all(queries, 'head', split_axis=1, concat_axis=0, tiled=True)  5.88 us
    ppermute x1, starting transfers between devices, shards(): qo = lax.ppermute(q, 'core', turn(2, 1))  5.35 us
    ppermute x1, starting transfers between devices, shards(): got = lax.ppermute(send, 'core', turn(2, 1))  5.33 us
  transfers between devices with their start and end apart: 8, of which 5 were waited for; matrix products, arithmetic and copies ran while one was open for 1% of the time, Pallas kernels for 14%

profile of v2, /device:TPU:1, one launch (start us, length us, event | category | flops | bytes accessed | tf_op | source)
XLA Modules:
  0.0 131.9 jit_solution(13819189373502448633)
XLA Ops:
  0.0 0.8 copy.10
  0.9 0.9 copy.11
  1.7 0.0 copy-start.1
  1.8 1.1 broadcast_in_dim.2
  2.9 0.0 copy-start
  2.9 17.3 %all-to-all-start = ((bf16[64,32,256]{2,1,0:T(8,128)(2,1)}), bf16[64,32,256]{2,1,0:T(8,128)(2,1)S(1)}, u32[]{:S(2)}, u32[]{:S(2)}) async-start(bf16[64,32,256]{2,1,0:T(8,128)(2,1)} %bitcast.4), calls=%async_computation | async-start | bytes 2097152 | tf_op jit(solution)/shard_map/all_to_all | solution.py:268
  20.2 0.0 copy-done.1
  20.2 0.8 copy.13
  21.0 25.9 %all-to-all-done = bf16[64,32,256]{2,1,0:T(8,128)(2,1)S(1)} async-done(((bf16[64,32,256]{2,1,0:T(8,128)(2,1)}), bf16[64,32,256]{2,1,0:T(8,128)(2,1)S(1)}, u32[]{:S(2)}, u32[]{:S(2)}) %all-to-all-start) | async-done | bytes 1048608 | tf_op jit(solution)/shard_map/all_to_all | solution.py:268
  46.9 6.6 %all-to-all-start.1 = ((bf16[32,8,768]{2,0,1:T(8,128)(2,1)}), bf16[32,8,768]{2,0,1:T(8,128)(2,1)S(1)}, u32[]{:S(2)}, u32[]{:S(2)}) async-start(bf16[32,8,768]{2,0,1:T(8,128)(2,1)} %bitcast.21), calls=%async_computation.1 | async-start | bytes 786432 | tf_op jit(solution)/shard_map/all_to_all | solution.py:272
  53.4 4.4 %collective-permute-start = (bf16[8,8,32,256]{3,2,1,0:T(8,128)(2,1)S(1)}, bf16[8,8,32,256]{3,2,1,0:T(8,128)(2,1)S(1)}, u32[]{:S(2)}, u32[]{:S(2)}) collective-permute-start(bf16[8,8,32,256]{3,2,1,0:T(8,128)(2,1)S(1)} %bitcast.23), channel_id=1, source_target_pairs={{0,6},{2,0},{4,2},{6,4},{1,7},{3,1},{5,3},{7,5},{8,14},{10,8},{12,... | collective-permute-start | bytes 3145736 | tf_op jit(solution)/shard_map/ppermute | solution.py:273
  57.8 1.9 %collective-permute-start.2 = (bf16[8,8,32,256]{3,2,1,0:T(8,128)(2,1)S(1)}, bf16[8,8,32,256]{3,2,1,0:T(8,128)(2,1)S(1)}, u32[]{:S(2)}, u32[]{:S(2)}) collective-permute-start(bf16[8,8,32,256]{3,2,1,0:T(8,128)(2,1)S(1)} %bitcast.24), channel_id=1, source_target_pairs={{0,2},{2,4},{4,6},{6,0},{1,3},{3,5},{5,7},{7,1},{8,10},{10,12},{12... | collective-permute-start | bytes 3145736 | tf_op jit(solution)/shard_map/ppermute | solution.py:274
  59.8 5.9 %all-to-all-done.1 = bf16[32,8,768]{2,0,1:T(8,128)(2,1)S(1)} async-done(((bf16[32,8,768]{2,0,1:T(8,128)(2,1)}), bf16[32,8,768]{2,0,1:T(8,128)(2,1)S(1)}, u32[]{:S(2)}, u32[]{:S(2)}) %all-to-all-start.1) | async-done | bytes 393248 | tf_op jit(solution)/shard_map/all_to_all | solution.py:272
  65.6 5.3 %collective-permute-start.4 = (bf16[256,768]{1,0:T(8,128)(2,1)S(1)}, bf16[256,768]{1,0:T(8,128)(2,1)}, u32[]{:S(2)}, u32[]{:S(2)}) collective-permute-start(bf16[256,768]{1,0:T(8,128)(2,1)S(1)} %bitcast.26), channel_id=1, source_target_pairs={{0,8},{8,0},{1,9},{9,1},{2,10},{10,2},{3,11},{11,3},{4,12},{12,4},... | collective-permute-start | bytes 1179656 | tf_op jit(solution)/shard_map/ppermute | solution.py:275
  71.0 0.1 pad_add_fusion.refs_1_
  71.1 1.4 %collective-permute-done.4.refs_4_ = bf16[256,768]{1,0:T(8,128)(2,1)} collective-permute-done((bf16[256,768]{1,0:T(8,128)(2,1)S(1)}, bf16[256,768]{1,0:T(8,128)(2,1)}, u32[]{:S(2)}, u32[]{:S(2)}) %collective-permute-start.4) | collective-permute-done | bytes 393248 | tf_op jit(solution)/shard_map/ppermute | solution.py:275
  72.5 0.0 copy-done
  72.5 7.4 %attend0.1 = (f32[4,144,768]{2,1,0:T(8,128)S(1)}, f32[4,1,768]{2,1,0:T(1,128)S(1)}, bf16[4,256,768]{2,1,0:T(8,128)(2,1)S(1)}) custom-call(s32[128]{0:T(128)S(1)} %copy-done, s32[3]{0:T(128)S(1)} %pad_add_fusion.refs_1_, bf16[8,8,32,256]{3,2,1,0:T(8,128)(2,1)S(1)} %bitcast.25, bf16[256,768]{1,0:T(8,128)(2,1)S(1)} %bitcast.27, ...), custom_call_target="tpu_custom_call" | custom-call | flops 3221225472 | bytes 1048576 | tf_op jit(solution)/shard_map/attend0/pallas_call | solution.py:250
  79.9 0.0 collective-permute-done.refs_2_
  79.9 4.4 %collective-permute-start.1 = (bf16[4,8,32,256]{3,2,1,0:T(8,128)(2,1)S(1)}, bf16[4,8,32,256]{3,2,1,0:T(8,128)(2,1)S(1)}, u32[]{:S(2)}, u32[]{:S(2)}) collective-permute-start(bf16[4,8,32,256]{3,2,1,0:T(8,128)(2,1)S(1)} %slice.8), channel_id=1, source_target_pairs={{0,6},{2,0},{4,2},{6,4},{1,7},{3,1},{5,3},{7,5},{8,14},{10,8},{12,... | collective-permute-start | bytes 1572872 | tf_op jit(solution)/shard_map/ppermute | solution.py:276
  84.3 0.0 collective-permute-done.2.refs_3_
  84.4 1.9 %collective-permute-start.3 = (bf16[4,8,32,256]{3,2,1,0:T(8,128)(2,1)S(1)}, bf16[4,8,32,256]{3,2,1,0:T(8,128)(2,1)S(1)}, u32[]{:S(2)}, u32[]{:S(2)}) collective-permute-start(bf16[4,8,32,256]{3,2,1,0:T(8,128)(2,1)S(1)} %slice.9), channel_id=1, source_target_pairs={{0,2},{2,4},{4,6},{6,0},{1,3},{3,5},{5,7},{7,1},{8,10},{10,12},{12... | collective-permute-start | bytes 1572872 | tf_op jit(solution)/shard_map/ppermute | solution.py:277
  86.3 10.8 %attend1.1 = (f32[4,144,768]{2,1,0:T(8,128)S(1)}, f32[4,1,768]{2,1,0:T(1,128)S(1)}) custom-call(s32[128]{0:T(128)S(1)} %copy-done, s32[3]{0:T(128)S(1)} %pad_add_fusion.refs_1_, bf16[8,8,32,256]{3,2,1,0:T(8,128)(2,1)S(1)} %collective-permute-done.refs_2_, bf16[8,8,32,256]{3,2,1,0:T(8,128)(2,1)S(1)} %collective-permute-done.2.refs_3_, ...), custom_call_target="tpu_custom_call" | custom-call | flops 6442450944 | bytes 2097152 | tf_op jit(solution)/shard_map/attend1/pallas_call | solution.py:250
  97.1 0.0 collective-permute-done.1.refs_2_
  97.1 1.2 collective-permute-done.3.refs_3_
  98.4 6.5 %attend2.1 = (f32[2,128,768]{2,1,0:T(8,128)S(1)}, f32[2,1,768]{2,1,0:T(1,128)S(1)}, bf16[2,144,768]{2,1,0:T(8,128)(2,1)S(1)}) custom-call(s32[128]{0:T(128)S(1)} %copy-done, s32[3]{0:T(128)S(1)} %pad_add_fusion.refs_1_, bf16[4,8,32,256]{3,2,1,0:T(8,128)(2,1)S(1)} %collective-permute-done.1.refs_2_, ...), custom_call_target="tpu_custom_call" | custom-call | flops 3221225472 | bytes 1048576 | tf_op jit(solution)/shard_map/attend2/pallas_call | solution.py:250
  104.9 5.3 %collective-permute-start.5 = (bf16[2,144,768]{2,1,0:T(8,128)(2,1)S(1)}, bf16[2,144,768]{2,1,0:T(8,128)(2,1)S(1)}, u32[]{:S(2)}, u32[]{:S(2)}) collective-permute-start(bf16[2,144,768]{2,1,0:T(8,128)(2,1)S(1)} %get-tuple-element.20), channel_id=1, source_target_pairs={{0,8},{8,0},{1,9},{9,1},{2,10},{10,2},{3,11},{11,3},{4,12},{12,4},... | collective-permute-start | bytes 1327112 | tf_op jit(solution)/shard_map/ppermute | solution.py:284
  110.2 1.4 %collective-permute-done.5.got_ref = bf16[2,144,768]{2,1,0:T(8,128)(2,1)S(1)} collective-permute-done((bf16[2,144,768]{2,1,0:T(8,128)(2,1)S(1)}, bf16[2,144,768]{2,1,0:T(8,128)(2,1)S(1)}, u32[]{:S(2)}, u32[]{:S(2)}) %collective-permute-start.5) | collective-permute-done | bytes 442400 | tf_op jit(solution)/shard_map/ppermute | solution.py:284
  111.6 0.2 merge.1
  111.9 19.2 %all_to_all.43 = bf16[8,32,768]{2,1,0:T(8,128)(2,1)S(1)} all-to-all(bf16[8,32,768]{2,1,0:T(8,128)(2,1)S(1)} %bitcast.22), channel_id=1, replica_groups=mesh['head'=8,'zlo'=4,'core'=2,'x'=4,'zhi'=2] {'head'}, dimensions={0} | all-to-all | bytes 786432 | tf_op jit(solution)/shard_map/all_to_all | solution.py:293
  131.1 0.8 copy.9
  (4 shorter events, 0.1 us)
Async XLA Ops:
  1.7 18.4 %copy-start.1 = (bf16[32,6144]{1,0:T(8,128)(2,1)S(1)}, bf16[32,6144]{1,0:T(8,128)(2,1)}, u32[]{:S(2)}) copy-start(bf16[32,6144]{1,0:T(8,128)(2,1)} %param.4) | copy-start | bytes 1179652
  2.9 69.6 %copy-start = (s32[128]{0:T(128)S(1)}, s32[128]{0:T(128)}, u32[]{:S(2)}) copy-start(s32[128]{0:T(128)} %refs_0_.5) | copy-start | bytes 1540
  2.9 44.0 %all-to-all-start = ((bf16[64,32,256]{2,1,0:T(8,128)(2,1)}), bf16[64,32,256]{2,1,0:T(8,128)(2,1)S(1)}, u32[]{:S(2)}, u32[]{:S(2)}) async-start(bf16[64,32,256]{2,1,0:T(8,128)(2,1)} %bitcast.4), calls=%async_computation | async-start | bytes 2097152 | tf_op jit(solution)/shard_map/all_to_all | solution.py:268
  46.9 18.7 %all-to-all-start.1 = ((bf16[32,8,768]{2,0,1:T(8,128)(2,1)}), bf16[32,8,768]{2,0,1:T(8,128)(2,1)S(1)}, u32[]{:S(2)}, u32[]{:S(2)}) async-start(bf16[32,8,768]{2,0,1:T(8,128)(2,1)} %bitcast.21), calls=%async_computation.1 | async-start | bytes 786432 | tf_op jit(solution)/shard_map/all_to_all | solution.py:272
  53.4 26.4 %collective-permute-start = (bf16[8,8,32,256]{3,2,1,0:T(8,128)(2,1)S(1)}, bf16[8,8,32,256]{3,2,1,0:T(8,128)(2,1)S(1)}, u32[]{:S(2)}, u32[]{:S(2)}) collective-permute-start(bf16[8,8,32,256]{3,2,1,0:T(8,128)(2,1)S(1)} %bitcast.23), channel_id=1, source_target_pairs={{0,6},{2,0},{4,2},{6,4},{1,7},{3,1},{5,3},{7,5},{8,14},{10,8},{12,... | collective-permute-start | bytes 3145736 | tf_op jit(solution)/shard_map/ppermute | solution.py:273
  57.8 26.5 %collective-permute-start.2 = (bf16[8,8,32,256]{3,2,1,0:T(8,128)(2,1)S(1)}, bf16[8,8,32,256]{3,2,1,0:T(8,128)(2,1)S(1)}, u32[]{:S(2)}, u32[]{:S(2)}) collective-permute-start(bf16[8,8,32,256]{3,2,1,0:T(8,128)(2,1)S(1)} %bitcast.24), channel_id=1, source_target_pairs={{0,2},{2,4},{4,6},{6,0},{1,3},{3,5},{5,7},{7,1},{8,10},{10,12},{12... | collective-permute-start | bytes 3145736 | tf_op jit(solution)/shard_map/ppermute | solution.py:274
  65.6 6.8 %collective-permute-start.4 = (bf16[256,768]{1,0:T(8,128)(2,1)S(1)}, bf16[256,768]{1,0:T(8,128)(2,1)}, u32[]{:S(2)}, u32[]{:S(2)}) collective-permute-start(bf16[256,768]{1,0:T(8,128)(2,1)S(1)} %bitcast.26), channel_id=1, source_target_pairs={{0,8},{8,0},{1,9},{9,1},{2,10},{10,2},{3,11},{11,3},{4,12},{12,4},... | collective-permute-start | bytes 1179656 | tf_op jit(solution)/shard_map/ppermute | solution.py:275
  79.9 17.2 %collective-permute-start.1 = (bf16[4,8,32,256]{3,2,1,0:T(8,128)(2,1)S(1)}, bf16[4,8,32,256]{3,2,1,0:T(8,128)(2,1)S(1)}, u32[]{:S(2)}, u32[]{:S(2)}) collective-permute-start(bf16[4,8,32,256]{3,2,1,0:T(8,128)(2,1)S(1)} %slice.8), channel_id=1, source_target_pairs={{0,6},{2,0},{4,2},{6,4},{1,7},{3,1},{5,3},{7,5},{8,14},{10,8},{12,... | collective-permute-start | bytes 1572872 | tf_op jit(solution)/shard_map/ppermute | solution.py:276
  84.4 14.0 %collective-permute-start.3 = (bf16[4,8,32,256]{3,2,1,0:T(8,128)(2,1)S(1)}, bf16[4,8,32,256]{3,2,1,0:T(8,128)(2,1)S(1)}, u32[]{:S(2)}, u32[]{:S(2)}) collective-permute-start(bf16[4,8,32,256]{3,2,1,0:T(8,128)(2,1)S(1)} %slice.9), channel_id=1, source_target_pairs={{0,2},{2,4},{4,6},{6,0},{1,3},{3,5},{5,7},{7,1},{8,10},{10,12},{12... | collective-permute-start | bytes 1572872 | tf_op jit(solution)/shard_map/ppermute | solution.py:277
  104.9 6.7 %collective-permute-start.5 = (bf16[2,144,768]{2,1,0:T(8,128)(2,1)S(1)}, bf16[2,144,768]{2,1,0:T(8,128)(2,1)S(1)}, u32[]{:S(2)}, u32[]{:S(2)}) collective-permute-start(bf16[2,144,768]{2,1,0:T(8,128)(2,1)S(1)} %get-tuple-element.20), channel_id=1, source_target_pairs={{0,8},{8,0},{1,9},{9,1},{2,10},{10,2},{3,11},{11,3},{4,12},{12,4},... | collective-permute-start | bytes 1327112 | tf_op jit(solution)/shard_map/ppermute | solution.py:284

commit v3 on v2

--- a/solution.py
+++ b/solution.py
@@ -33,14 +33,13 @@
         qt[j, HD:, h * CH : (h + 1) * CH] = (t - hi.astype(F32)).astype(BF16)
 
 
-def fill(piece, at, rows, kbuf, vt):
+def fill(piece, at, kbuf, vt):
     for z in range(NZ):
-        for w in range(rows // CH):
-            to = (at + z * (rows // CH) + w) * CH
+        for w in range(2):
+            to = (at + 2 * z + w) * CH
             block = piece[4 * w : 4 * w + 4, z].reshape(CH, 2 * HD)
             kbuf[to : to + CH, :] = block[:, :HD]
             vt[:HD, to : to + CH] = block[:, HD:].T
-    return at + NZ * (rows // CH)
 
 
 def attend(stage, sources, *refs):
@@ -65,7 +64,7 @@
     def stored(xv, zv, cv, w):
         return ((xv * NZ + zv) * 2 + cv) * 2 + w
 
-    blocks = sum(NZ * (rows // CH) for _, _, rows in sources)
+    blocks = 2 * NZ * len(sources)
     dummy = blocks
 
     t = jnp.int32(0)
@@ -75,18 +74,16 @@
         n = t * GB
         start = n
         slot = 0
-        for shift, y0, rows in sources:
-            xv = (x + shift) % NX
-            per = rows // CH
-
-            def scan(i, n, xv=xv, y0=y0, per=per, slot=slot, mine=mine):
-                w = i % per + y0 // 4
+        for shifts in sources:
+            xv = (x + jnp.where(core == 0, *shifts)) % NX
+
+            def scan(i, n, xv=xv, slot=slot, mine=mine):
                 tabk[n] = i + slot
                 tabv[n] = i + slot
-                return n + (order[stored(xv, i // per, core, w)] < mine).astype(jnp.int32)
-
-            n = lax.fori_loop(0, NZ * per, scan, n, unroll=True)
-            slot += NZ * per
+                return n + (order[stored(xv, i // 2, core, i % 2)] < mine).astype(jnp.int32)
+
+            n = lax.fori_loop(0, 2 * NZ, scan, n, unroll=True)
+            slot += 2 * NZ
         steps = (n - start + GB - 1) // GB
         keep = tabk[jnp.maximum(n - 1, 0)]
         for g in range(GB - 1):
@@ -106,9 +103,8 @@
             tabk[(t + e) * GB + g] = jnp.where(t > 0, tabk[back * GB + g], 0)
             tabv[(t + e) * GB + g] = dummy
 
-    at = 0
-    for piece, (_, _, rows) in zip(pieces, sources):
-        at = fill(piece, at, rows, kbuf, vt)
+    for at, piece in enumerate(pieces):
+        fill(piece, at * 2 * NZ, kbuf, vt)
     vt[HD:, : blocks * CH] = jnp.ones((OUTR - HD, blocks * CH), BF16)
     vt[:, blocks * CH :] = jnp.zeros((OUTR, CH), BF16)
 
@@ -202,6 +198,14 @@
                 send_ref[j - 2, HD:] = tail.astype(BF16)
 
 
+def arrange(k_ref, v_ref, out_ref):
+    for h in range(HEADS):
+        cols = slice(h * HD, (h + 1) * HD)
+        both = jnp.concatenate([k_ref[:, cols], v_ref[:, cols]], axis=1)
+        for z in range(NZ):
+            out_ref[h, z] = both
+
+
 def merge(own_ref, ownl_ref, got_ref, out_ref):
     for j in range(2):
         tail = got_ref[j, HD:].astype(F32)
@@ -219,12 +223,12 @@
 
 VMEM = pl.BlockSpec(memory_space=pltpu.VMEM)
 SMEM = pl.BlockSpec(memory_space=pltpu.SMEM)
-SOURCES = (((0, 0, 256),), ((1, 0, 256), (3, 0, 256)), ((2, 0, 128), (2, 4, 128)))
+SOURCES = (((0, 0),), ((1, 3), (3, 1)), ((2, 2),))
 
 
 def call(stage, order, pos, *arrays):
     sources = SOURCES[stage]
-    blocks = sum(NZ * (rows // CH) for _, _, rows in sources)
+    blocks = 2 * NZ * len(sources)
     state = (jax.ShapeDtypeStruct((4, OUTR, ROWS), F32), jax.ShapeDtypeStruct((4, 1, ROWS), F32))
     scratch = [
         pltpu.VMEM((blocks * CH, HD), BF16),
@@ -260,34 +264,38 @@
 
 
 def shards(queries, keys, values, order):
-    def turn(n, s):
-        return [(i, (i + s) % n) for i in range(n)]
-
-    kv = jnp.concatenate([keys.reshape(SLICE, HEADS, HD), values.reshape(SLICE, HEADS, HD)], axis=2)
-    kv = jnp.broadcast_to(kv.transpose(1, 0, 2)[:, None], (HEADS, NZ, SLICE, 2 * HD))
+    def around(s):
+        return [(c * NX + i, c * NX + (i + (s if c else -s)) % NX) for c in range(2) for i in range(NX)]
+
+    kv = pl.pallas_call(
+        arrange,
+        out_shape=jax.ShapeDtypeStruct((HEADS, NZ, SLICE, 2 * HD), BF16),
+        in_specs=[VMEM] * 2,
+        out_specs=VMEM,
+        name="arrange",
+    )(keys, values)
     kv = lax.all_to_all(
         kv.reshape(HEADS * NZ, SLICE, 2 * HD), ("head", "zhi", "zlo"), split_axis=0, concat_axis=0, tiled=True
     )
     kv0 = kv.reshape(HEADS, NZ, SLICE, 2 * HD)
     q = lax.all_to_all(queries, "head", split_axis=1, concat_axis=0, tiled=True)
-    kv1 = lax.ppermute(kv0, "x", turn(NX, -1))
-    kv3 = lax.ppermute(kv0, "x", turn(NX, 1))
-    qo = lax.ppermute(q, "core", turn(2, 1))
-    kv2a = lax.ppermute(kv1[:4], "x", turn(NX, -1))
-    kv2b = lax.ppermute(kv3[4:], "x", turn(NX, 1))
+    kv1 = lax.ppermute(kv0, ("core", "x"), around(1))
+    kv3 = lax.ppermute(kv0, ("core", "x"), around(-1))
+    qo = lax.ppermute(q, "core", [(0, 1), (1, 0)])
+    kv2 = lax.ppermute(kv1, ("core", "x"), around(1))
     pos = jnp.stack(
         [lax.axis_index("x"), lax.axis_index("zhi") * 4 + lax.axis_index("zlo"), lax.axis_index("core")]
     ).astype(jnp.int32)
     acc, top, qt = call(0, order, pos, kv0, q, qo)
     acc, top = call(1, order, pos, kv1, kv3, qt, acc, top)
-    own, ownl, send = call(2, order, pos, kv2a, kv2b, qt, acc, top)
-    got = lax.ppermute(send, "core", turn(2, 1))
+    own, ownl, send = call(2, order, pos, kv2, qt, acc, top)
+    got = lax.ppermute(send, "core", [(0, 1), (1, 0)])
     out = pl.pallas_call(
         merge,
         out_shape=jax.ShapeDtypeStruct((2 * CH, ROWS), BF16),
         in_specs=[VMEM] * 3,
         out_specs=VMEM,
-        compiler_params=pltpu.CompilerParams(vmem_limit_bytes=32 << 20),
+        compiler_params=pltpu.CompilerParams(vmem_limit_bytes=20 << 20),
         name="merge",
     )(own, ownl, got)
     return lax.all_to_all(out, "head", split_axis=0, concat_axis=1, tiled=True)

time: 132 us -> 127 us (0.962)
  blocking collectives: 19.2 us -> 62.6 us
  waiting for transfers between devices: 35.8 us -> 8.84 us
  starting transfers between devices: 47.1 us -> 25.2 us
  Pallas kernels: 25 us -> 28.2 us
  local copies, waits for them, and re-layouts: 4.47 us -> 1.56 us
    all_to_all x0 -> x1, blocking collectives: none -> 44 us  [shards(): lax.all_to_all(kv.reshape(HEADS * NZ, SLICE, 2 * HD), ('head', 'zhi', 'zl...]
    all_to_all x1 -> x0, waiting for transfers between devices: 25.9 us -> none  [shards(): lax.all_to_all(kv.reshape(HEADS * NZ, SLICE, 2 * HD), ('head', 'zhi', 'zl...]
    all_to_all x1 -> x0, starting transfers between devices: 17.3 us -> none  [shards(): lax.all_to_all(kv.reshape(HEADS * NZ, SLICE, 2 * HD), ('head', 'zhi', 'zl...]
    ppermute x6 -> x5, starting transfers between devices: 23.3 us -> 18.6 us  [the longest x1 6.98 us: shards(): qo = lax.ppermute(q, 'core', [(0, 1), (1, 0)])]
    ppermute x6 -> x5, waiting for transfers between devices: 4.02 us -> 1.54 us  [the longest x1 1.53 us: shards(): got = lax.ppermute(send, 'core', [(0, 1), (1, 0)])]
    pallas_call x0 -> x1, Pallas kernels: none -> 1.96 us  [shards(): pl.pallas_call(arrange, out_shape=jax.ShapeDtypeStruct((HEADS, NZ, SLICE,...]
    unnamed x6 -> x4, local copies, waits for them, and re-layouts: 1.71 us -> 0.01 us
    all_to_all x1, waiting for transfers between devices: 5.88 us -> 7.3 us  [shards(): q = lax.all_to_all(queries, 'head', split_axis=1, concat_axis=0, tiled=True)]
  transfers between devices with their start and end apart: 8 -> 6, of which waited for: 5 -> 2; matrix products, arithmetic and copies ran while one was open for 1% -> 1% of each run, Pallas kernels for 14% -> 15%
where the time goes in v3:
time: 127 us
  blocking collectives  62.6 us (49%)
  Pallas kernels  28.2 us (22%)
  starting transfers between devices  25.2 us (20%)
  waiting for transfers between devices  8.84 us (7%)
  local copies, waits for them, and re-layouts  1.56 us (1%)
    all_to_all x1, blocking collectives, shards(): lax.all_to_all(kv.reshape(HEADS * NZ, SLICE, 2 * HD), ('head', 'zhi', 'zl...  44 us
    pallas_call x3, Pallas kernels, call(): pl.pallas_call(functools.partial(attend, stage, sources), out_shape=outs,...  26 us
    all_to_all x1, blocking collectives, shards(): return lax.all_to_all(out, 'head', split_axis=0, concat_axis=1, tiled=True)  18.6 us
    all_to_all x1, waiting for transfers between devices, shards(): q = lax.all_to_all(queries, 'head', split_axis=1, concat_axis=0, tiled=True)  7.3 us
    ppermute x1, starting transfers between devices, shards(): qo = lax.ppermute(q, 'core', [(0, 1), (1, 0)])  6.98 us
    all_to_all x1, starting transfers between devices, shards(): q = lax.all_to_all(queries, 'head', split_axis=1, concat_axis=0, tiled=True)  6.55 us
    ppermute x1, starting transfers between devices, shards(): kv3 = lax.ppermute(kv0, ('core', 'x'), around(-1))  3.36 us
    ppermute x1, starting transfers between devices, shards(): kv1 = lax.ppermute(kv0, ('core', 'x'), around(1))  3.11 us
  transfers between devices with their start and end apart: 6, of which 2 were waited for; matrix products, arithmetic and copies ran while one was open for 1% of the time, Pallas kernels for 15%

profile of v3, /device:TPU:1, one launch (start us, length us, event | category | flops | bytes accessed | tf_op | source)
XLA Modules:
  0.0 126.5 jit_solution(14825401328313508557)
XLA Ops:
  0.0 0.0 copy-start.1
  0.0 2.0 %arrange.1 = bf16[8,8,32,256]{3,2,1,0:T(8,128)(2,1)} custom-call(bf16[32,1024]{1,0:T(8,128)(2,1)} %k_ref.1, bf16[32,1024]{1,0:T(8,128)(2,1)} %v_ref.1), custom_call_target="tpu_custom_call" | custom-call | tf_op jit(solution)/shard_map/arrange/pallas_call | solution.py:270
  2.0 0.0 copy-start
  2.0 44.0 %all_to_all.43 = bf16[64,32,256]{2,1,0:T(8,128)(2,1)S(1)} all-to-all(bf16[64,32,256]{2,1,0:T(8,128)(2,1)} %bitcast.22), channel_id=1, replica_groups=mesh['head'=8,'zlo'=4,'core'=2,'x'=4,'zhi'=2] {'head','zhi','zlo'}, dimensions={0} | all-to-all | bytes 2097152 | tf_op jit(solution)/shard_map/all_to_all | solution.py:277
  46.0 3.1 %collective-permute-start = (bf16[8,8,32,256]{3,2,1,0:T(8,128)(2,1)S(1)}, bf16[8,8,32,256]{3,2,1,0:T(8,128)(2,1)S(1)}, u32[]{:S(2)}, u32[]{:S(2)}) collective-permute-start(bf16[8,8,32,256]{3,2,1,0:T(8,128)(2,1)S(1)} %bitcast.17), channel_id=1, source_target_pairs={{0,6},{2,0},{4,2},{6,4},{8,10},{10,12},{12,14},{14,8},{1,7},{3,1},... | collective-permute-start | bytes 3145736 | tf_op jit(solution)/shard_map/ppermute | solution.py:282
  49.1 0.0 copy-done.1
  49.1 0.8 copy.10
  49.9 6.6 %all-to-all-start.1 = ((bf16[32,8,768]{2,0,1:T(8,128)(2,1)}), bf16[32,8,768]{2,0,1:T(8,128)(2,1)S(1)}, u32[]{:S(2)}, u32[]{:S(2)}) async-start(bf16[32,8,768]{2,0,1:T(8,128)(2,1)} %bitcast.15), calls=%async_computation.1 | async-start | bytes 786432 | tf_op jit(solution)/shard_map/all_to_all | solution.py:281
  56.4 3.4 %collective-permute-start.3 = (bf16[8,8,32,256]{3,2,1,0:T(8,128)(2,1)S(1)}, bf16[8,8,32,256]{3,2,1,0:T(8,128)(2,1)S(1)}, u32[]{:S(2)}, u32[]{:S(2)}) collective-permute-start(bf16[8,8,32,256]{3,2,1,0:T(8,128)(2,1)S(1)} %bitcast.18), channel_id=1, source_target_pairs={{0,2},{2,4},{4,6},{6,0},{8,14},{10,8},{12,10},{14,12},{1,3},{3,5},... | collective-permute-start | bytes 3145736 | tf_op jit(solution)/shard_map/ppermute | solution.py:283
  59.8 7.3 %all-to-all-done.1 = bf16[32,8,768]{2,0,1:T(8,128)(2,1)S(1)} async-done(((bf16[32,8,768]{2,0,1:T(8,128)(2,1)}), bf16[32,8,768]{2,0,1:T(8,128)(2,1)S(1)}, u32[]{:S(2)}, u32[]{:S(2)}) %all-to-all-start.1) | async-done | bytes 393248 | tf_op jit(solution)/shard_map/all_to_all | solution.py:281
  67.1 7.0 %collective-permute-start.2 = (bf16[256,768]{1,0:T(8,128)(2,1)S(1)}, bf16[256,768]{1,0:T(8,128)(2,1)}, u32[]{:S(2)}, u32[]{:S(2)}) collective-permute-start(bf16[256,768]{1,0:T(8,128)(2,1)S(1)} %bitcast.20), channel_id=1, source_target_pairs={{0,8},{8,0},{1,9},{9,1},{2,10},{10,2},{3,11},{11,3},{4,12},{12,4},... | collective-permute-start | bytes 1179656 | tf_op jit(solution)/shard_map/ppermute | solution.py:284
  74.1 0.0 collective-permute-done.refs_2_
  74.1 3.0 %collective-permute-start.1 = (bf16[8,8,32,256]{3,2,1,0:T(8,128)(2,1)S(1)}, bf16[8,8,32,256]{3,2,1,0:T(8,128)(2,1)}, u32[]{:S(2)}, u32[]{:S(2)}) collective-permute-start(bf16[8,8,32,256]{3,2,1,0:T(8,128)(2,1)S(1)} %collective-permute-done.refs_2_), channel_id=1, source_target_pairs={{0,6},{2,0},{4,2},{6,4},{8,10},{10,12},{12,14},{14,8},{1,7},{3,1},... | collective-permute-start | bytes 3145736 | tf_op jit(solution)/shard_map/ppermute | solution.py:285
  77.1 0.1 pad_add_fusion.refs_1_
  77.2 0.0 collective-permute-done.2.refs_4_
  77.2 0.0 copy-done
  77.2 7.6 %attend0.1 = (f32[4,144,768]{2,1,0:T(8,128)S(1)}, f32[4,1,768]{2,1,0:T(1,128)S(1)}, bf16[4,256,768]{2,1,0:T(8,128)(2,1)S(1)}) custom-call(s32[128]{0:T(128)S(1)} %copy-done, s32[3]{0:T(128)S(1)} %pad_add_fusion.refs_1_, bf16[8,8,32,256]{3,2,1,0:T(8,128)(2,1)S(1)} %bitcast.19, bf16[256,768]{1,0:T(8,128)(2,1)S(1)} %bitcast.21, ...), custom_call_target="tpu_custom_call" | custom-call | flops 3221225472 | bytes 1048576 | tf_op jit(solution)/shard_map/attend0/pallas_call | solution.py:254
  84.8 0.0 collective-permute-done.3.refs_3_
  84.8 11.0 %attend1.1 = (f32[4,144,768]{2,1,0:T(8,128)S(1)}, f32[4,1,768]{2,1,0:T(1,128)S(1)}) custom-call(s32[128]{0:T(128)S(1)} %copy-done, s32[3]{0:T(128)S(1)} %pad_add_fusion.refs_1_, bf16[8,8,32,256]{3,2,1,0:T(8,128)(2,1)S(1)} %collective-permute-done.refs_2_, bf16[8,8,32,256]{3,2,1,0:T(8,128)(2,1)S(1)} %collective-permute-done.3.refs_3_, ...), custom_call_target="tpu_custom_call" | custom-call | flops 6442450944 | bytes 2097152 | tf_op jit(solution)/shard_map/attend1/pallas_call | solution.py:254
  95.8 0.0 collective-permute-done.1.refs_2_
  95.8 7.4 %attend2.1 = (f32[2,128,768]{2,1,0:T(8,128)S(1)}, f32[2,1,768]{2,1,0:T(1,128)S(1)}, bf16[2,144,768]{2,1,0:T(8,128)(2,1)S(1)}) custom-call(s32[128]{0:T(128)S(1)} %copy-done, s32[3]{0:T(128)S(1)} %pad_add_fusion.refs_1_, bf16[8,8,32,256]{3,2,1,0:T(8,128)(2,1)} %collective-permute-done.1.refs_2_, bf16[4,256,768]{2,1,0:T(8,128)(2,1)S(1)} %get-tuple-element.13.refs_4_.refs_3_, ...), custom_call_target="tpu_custom_call" | custom-call | flops 3221225472 | bytes 1048576 | tf_op jit(solution)/shard_map/attend2/pallas_call | solution.py:254
  103.2 2.2 %collective-permute-start.4 = (bf16[2,144,768]{2,1,0:T(8,128)(2,1)S(1)}, bf16[2,144,768]{2,1,0:T(8,128)(2,1)S(1)}, u32[]{:S(2)}, u32[]{:S(2)}) collective-permute-start(bf16[2,144,768]{2,1,0:T(8,128)(2,1)S(1)} %get-tuple-element.20), channel_id=1, source_target_pairs={{0,8},{8,0},{1,9},{9,1},{2,10},{10,2},{3,11},{11,3},{4,12},{12,4},... | collective-permute-start | bytes 1327112 | tf_op jit(solution)/shard_map/ppermute | solution.py:292
  105.4 1.5 %collective-permute-done.4.got_ref = bf16[2,144,768]{2,1,0:T(8,128)(2,1)S(1)} collective-permute-done((bf16[2,144,768]{2,1,0:T(8,128)(2,1)S(1)}, bf16[2,144,768]{2,1,0:T(8,128)(2,1)S(1)}, u32[]{:S(2)}, u32[]{:S(2)}) %collective-permute-start.4) | collective-permute-done | bytes 442400 | tf_op jit(solution)/shard_map/ppermute | solution.py:292
  106.9 0.3 merge.1
  107.1 18.6 %all_to_all.44 = bf16[8,32,768]{2,1,0:T(8,128)(2,1)S(1)} all-to-all(bf16[8,32,768]{2,1,0:T(8,128)(2,1)S(1)} %bitcast.16), channel_id=1, replica_groups=mesh['head'=8,'zlo'=4,'core'=2,'x'=4,'zhi'=2] {'head'}, dimensions={0} | all-to-all | bytes 786432 | tf_op jit(solution)/shard_map/all_to_all | solution.py:301
  125.7 0.8 copy.8
Async XLA Ops:
  0.0 49.1 %copy-start.1 = (bf16[32,6144]{1,0:T(8,128)(2,1)S(1)}, bf16[32,6144]{1,0:T(8,128)(2,1)}, u32[]{:S(2)}) copy-start(bf16[32,6144]{1,0:T(8,128)(2,1)} %param.4) | copy-start | bytes 1179652
  2.0 75.2 %copy-start = (s32[128]{0:T(128)S(1)}, s32[128]{0:T(128)}, u32[]{:S(2)}) copy-start(s32[128]{0:T(128)} %refs_0_.5) | copy-start | bytes 1540
  46.0 28.1 %collective-permute-start = (bf16[8,8,32,256]{3,2,1,0:T(8,128)(2,1)S(1)}, bf16[8,8,32,256]{3,2,1,0:T(8,128)(2,1)S(1)}, u32[]{:S(2)}, u32[]{:S(2)}) collective-permute-start(bf16[8,8,32,256]{3,2,1,0:T(8,128)(2,1)S(1)} %bitcast.17), channel_id=1, source_target_pairs={{0,6},{2,0},{4,2},{6,4},{8,10},{10,12},{12,14},{14,8},{1,7},{3,1},... | collective-permute-start | bytes 3145736 | tf_op jit(solution)/shard_map/ppermute | solution.py:282
  49.9 17.2 %all-to-all-start.1 = ((bf16[32,8,768]{2,0,1:T(8,128)(2,1)}), bf16[32,8,768]{2,0,1:T(8,128)(2,1)S(1)}, u32[]{:S(2)}, u32[]{:S(2)}) async-start(bf16[32,8,768]{2,0,1:T(8,128)(2,1)} %bitcast.15), calls=%async_computation.1 | async-start | bytes 786432 | tf_op jit(solution)/shard_map/all_to_all | solution.py:281
  56.4 28.4 %collective-permute-start.3 = (bf16[8,8,32,256]{3,2,1,0:T(8,128)(2,1)S(1)}, bf16[8,8,32,256]{3,2,1,0:T(8,128)(2,1)S(1)}, u32[]{:S(2)}, u32[]{:S(2)}) collective-permute-start(bf16[8,8,32,256]{3,2,1,0:T(8,128)(2,1)S(1)} %bitcast.18), channel_id=1, source_target_pairs={{0,2},{2,4},{4,6},{6,0},{8,14},{10,8},{12,10},{14,12},{1,3},{3,5},... | collective-permute-start | bytes 3145736 | tf_op jit(solution)/shard_map/ppermute | solution.py:283
  67.1 10.1 %collective-permute-start.2 = (bf16[256,768]{1,0:T(8,128)(2,1)S(1)}, bf16[256,768]{1,0:T(8,128)(2,1)}, u32[]{:S(2)}, u32[]{:S(2)}) collective-permute-start(bf16[256,768]{1,0:T(8,128)(2,1)S(1)} %bitcast.20), channel_id=1, source_target_pairs={{0,8},{8,0},{1,9},{9,1},{2,10},{10,2},{3,11},{11,3},{4,12},{12,4},... | collective-permute-start | bytes 1179656 | tf_op jit(solution)/shard_map/ppermute | solution.py:284
  74.1 21.8 %collective-permute-start.1 = (bf16[8,8,32,256]{3,2,1,0:T(8,128)(2,1)S(1)}, bf16[8,8,32,256]{3,2,1,0:T(8,128)(2,1)}, u32[]{:S(2)}, u32[]{:S(2)}) collective-permute-start(bf16[8,8,32,256]{3,2,1,0:T(8,128)(2,1)S(1)} %collective-permute-done.refs_2_), channel_id=1, source_target_pairs={{0,6},{2,0},{4,2},{6,4},{8,10},{10,12},{12,14},{14,8},{1,7},{3,1},... | collective-permute-start | bytes 3145736 | tf_op jit(solution)/shard_map/ppermute | solution.py:285
  103.2 3.7 %collective-permute-start.4 = (bf16[2,144,768]{2,1,0:T(8,128)(2,1)S(1)}, bf16[2,144,768]{2,1,0:T(8,128)(2,1)S(1)}, u32[]{:S(2)}, u32[]{:S(2)}) collective-permute-start(bf16[2,144,768]{2,1,0:T(8,128)(2,1)S(1)} %get-tuple-element.20), channel_id=1, source_target_pairs={{0,8},{8,0},{1,9},{9,1},{2,10},{10,2},{3,11},{11,3},{4,12},{12,4},... | collective-permute-start | bytes 1327112 | tf_op jit(solution)/shard_map/ppermute | solution.py:292

commit v4 on v3

--- a/solution.py
+++ b/solution.py
@@ -19,7 +19,7 @@
 LOW = -1e30
 MASKED = -3e38
 GB = 4
-WIDTH = 256
+WIDTH = 768
 BEHIND = 0
 OUTR = HD + 16
 F32, BF16 = jnp.float32, jnp.bfloat16
@@ -43,7 +43,7 @@
 
 
 def attend(stage, sources, *refs):
-    first, last = stage == 0, stage == 2
+    first, last = stage == 0, stage == STAGES - 1
     order, pos = refs[:2]
     refs = refs[2:]
     pieces, refs = refs[: len(sources)], refs[len(sources) :]
@@ -177,7 +177,16 @@
         both(2 * i + 1, sb, sa)
         return c
 
-    lax.fori_loop(0, (t + 1) // 2, pair, 0)
+    pairs = (t + 1) // 2
+
+    def several(i, c):
+        for e in range(4):
+            pair(4 * i + e, c)
+        return c
+
+    many = pairs // 4
+    lax.fori_loop(0, many, several, 0)
+    lax.fori_loop(many * 4, pairs, pair, 0)
 
     if last:
         for j in range(4):
@@ -223,7 +232,8 @@
 
 VMEM = pl.BlockSpec(memory_space=pltpu.VMEM)
 SMEM = pl.BlockSpec(memory_space=pltpu.SMEM)
-SOURCES = (((0, 0),), ((1, 3), (3, 1)), ((2, 2),))
+SOURCES = (((0, 0), (1, 3), (3, 1)), ((2, 2),))
+STAGES = len(SOURCES)
 
 
 def call(stage, order, pos, *arrays):
@@ -241,7 +251,7 @@
     ]
     if stage == 0:
         outs = state + (jax.ShapeDtypeStruct((4, 2 * HD, ROWS), BF16),)
-    elif stage == 1:
+    elif stage < STAGES - 1:
         outs = state
     else:
         outs = (
@@ -286,9 +296,8 @@
     pos = jnp.stack(
         [lax.axis_index("x"), lax.axis_index("zhi") * 4 + lax.axis_index("zlo"), lax.axis_index("core")]
     ).astype(jnp.int32)
-    acc, top, qt = call(0, order, pos, kv0, q, qo)
-    acc, top = call(1, order, pos, kv1, kv3, qt, acc, top)
-    own, ownl, send = call(2, order, pos, kv2, qt, acc, top)
+    acc, top, qt = call(0, order, pos, kv0, kv1, kv3, q, qo)
+    own, ownl, send = call(1, order, pos, kv2, qt, acc, top)
     got = lax.ppermute(send, "core", [(0, 1), (1, 0)])
     out = pl.pallas_call(
         merge,

time: 127 us -> 126 us (level)
  Pallas kernels: 28.2 us -> 20.8 us
  blocking collectives: 62.6 us -> 67 us
    pallas_call x3 -> x2, Pallas kernels: 26 us -> 18.6 us  [call(): pl.pallas_call(functools.partial(attend, stage, sources), out_shape=outs,...]
    all_to_all x1, blocking collectives: 18.6 us -> 23 us  [shards(): return lax.all_to_all(out, 'head', split_axis=0, concat_axis=1, tiled=True)]
  transfers between devices with their start and end apart: 6 -> 6, of which waited for: 2 -> 4; matrix products, arithmetic and copies ran while one was open for 1% -> 1% of each run, Pallas kernels for 15% -> 10%
where the time goes in v4:
time: 126 us; the launch traced here: 125 us
  blocking collectives  67 us (53%)
  starting transfers between devices  25.8 us (20%)
  Pallas kernels  20.8 us (17%)
  waiting for transfers between devices  10.1 us (8%)
  local copies, waits for them, and re-layouts  1.56 us (1%)
    all_to_all x1, blocking collectives, shards(): lax.all_to_all(kv.reshape(HEADS * NZ, SLICE, 2 * HD), ('head', 'zhi', 'zl...  44 us
    all_to_all x1, blocking collectives, shards(): return lax.all_to_all(out, 'head', split_axis=0, concat_axis=1, tiled=True)  23 us
    pallas_call x2, Pallas kernels, call(): pl.pallas_call(functools.partial(attend, stage, sources), out_shape=outs,...  18.6 us
    all_to_all x1, waiting for transfers between devices, shards(): q = lax.all_to_all(queries, 'head', split_axis=1, concat_axis=0, tiled=True)  7.3 us
    ppermute x1, starting transfers between devices, shards(): qo = lax.ppermute(q, 'core', [(0, 1), (1, 0)])  6.98 us
    all_to_all x1, starting transfers between devices, shards(): q = lax.all_to_all(queries, 'head', split_axis=1, concat_axis=0, tiled=True)  6.55 us
    ppermute x1, starting transfers between devices, shards(): kv3 = lax.ppermute(kv0, ('core', 'x'), around(-1))  3.36 us
    ppermute x1, starting transfers between devices, shards(): kv1 = lax.ppermute(kv0, ('core', 'x'), around(1))  3.11 us
  transfers between devices with their start and end apart: 6, of which 4 were waited for; matrix products, arithmetic and copies ran while one was open for 1% of the time, Pallas kernels for 10%

profile of v4, /device:TPU:1, one launch (start us, length us, event | category | flops | bytes accessed | tf_op | source)
XLA Modules:
  0.0 125.4 jit_solution(9147158776918788278)
XLA Ops:
  0.0 0.0 copy-start.1
  0.0 2.0 %arrange.1 = bf16[8,8,32,256]{3,2,1,0:T(8,128)(2,1)} custom-call(bf16[32,1024]{1,0:T(8,128)(2,1)} %k_ref.1, bf16[32,1024]{1,0:T(8,128)(2,1)} %v_ref.1), custom_call_target="tpu_custom_call" | custom-call | tf_op jit(solution)/shard_map/arrange/pallas_call | solution.py:280
  2.0 0.0 copy-start
  2.0 44.0 %all_to_all.43 = bf16[64,32,256]{2,1,0:T(8,128)(2,1)S(1)} all-to-all(bf16[64,32,256]{2,1,0:T(8,128)(2,1)} %bitcast.22), channel_id=1, replica_groups=mesh['head'=8,'zlo'=4,'core'=2,'x'=4,'zhi'=2] {'head','zhi','zlo'}, dimensions={0} | all-to-all | bytes 2097152 | tf_op jit(solution)/shard_map/all_to_all | solution.py:287
  46.0 3.1 %collective-permute-start = (bf16[8,8,32,256]{3,2,1,0:T(8,128)(2,1)S(1)}, bf16[8,8,32,256]{3,2,1,0:T(8,128)(2,1)S(1)}, u32[]{:S(2)}, u32[]{:S(2)}) collective-permute-start(bf16[8,8,32,256]{3,2,1,0:T(8,128)(2,1)S(1)} %bitcast.17), channel_id=1, source_target_pairs={{0,6},{2,0},{4,2},{6,4},{8,10},{10,12},{12,14},{14,8},{1,7},{3,1},... | collective-permute-start | bytes 3145736 | tf_op jit(solution)/shard_map/ppermute | solution.py:292
  49.1 0.0 copy-done.1
  49.1 0.8 copy.10
  49.9 6.6 %all-to-all-start.1 = ((bf16[32,8,768]{2,0,1:T(8,128)(2,1)}), bf16[32,8,768]{2,0,1:T(8,128)(2,1)S(1)}, u32[]{:S(2)}, u32[]{:S(2)}) async-start(bf16[32,8,768]{2,0,1:T(8,128)(2,1)} %bitcast.15), calls=%async_computation.1 | async-start | bytes 786432 | tf_op jit(solution)/shard_map/all_to_all | solution.py:291
  56.4 3.4 %collective-permute-start.2 = (bf16[8,8,32,256]{3,2,1,0:T(8,128)(2,1)S(1)}, bf16[8,8,32,256]{3,2,1,0:T(8,128)(2,1)S(1)}, u32[]{:S(2)}, u32[]{:S(2)}) collective-permute-start(bf16[8,8,32,256]{3,2,1,0:T(8,128)(2,1)S(1)} %bitcast.18), channel_id=1, source_target_pairs={{0,2},{2,4},{4,6},{6,0},{8,14},{10,8},{12,10},{14,12},{1,3},{3,5},... | collective-permute-start | bytes 3145736 | tf_op jit(solution)/shard_map/ppermute | solution.py:293
  59.8 7.3 %all-to-all-done.1 = bf16[32,8,768]{2,0,1:T(8,128)(2,1)S(1)} async-done(((bf16[32,8,768]{2,0,1:T(8,128)(2,1)}), bf16[32,8,768]{2,0,1:T(8,128)(2,1)S(1)}, u32[]{:S(2)}, u32[]{:S(2)}) %all-to-all-start.1) | async-done | bytes 393248 | tf_op jit(solution)/shard_map/all_to_all | solution.py:291
  67.1 7.0 %collective-permute-start.3 = (bf16[256,768]{1,0:T(8,128)(2,1)S(1)}, bf16[256,768]{1,0:T(8,128)(2,1)}, u32[]{:S(2)}, u32[]{:S(2)}) collective-permute-start(bf16[256,768]{1,0:T(8,128)(2,1)S(1)} %bitcast.20), channel_id=1, source_target_pairs={{0,8},{8,0},{1,9},{9,1},{2,10},{10,2},{3,11},{11,3},{4,12},{12,4},... | collective-permute-start | bytes 1179656 | tf_op jit(solution)/shard_map/ppermute | solution.py:294
  74.1 0.0 collective-permute-done.refs_3_
  74.1 3.0 %collective-permute-start.1 = (bf16[8,8,32,256]{3,2,1,0:T(8,128)(2,1)S(1)}, bf16[8,8,32,256]{3,2,1,0:T(8,128)(2,1)}, u32[]{:S(2)}, u32[]{:S(2)}) collective-permute-start(bf16[8,8,32,256]{3,2,1,0:T(8,128)(2,1)S(1)} %collective-permute-done.refs_3_), channel_id=1, source_target_pairs={{0,6},{2,0},{4,2},{6,4},{8,10},{10,12},{12,14},{14,8},{1,7},{3,1},... | collective-permute-start | bytes 3145736 | tf_op jit(solution)/shard_map/ppermute | solution.py:295
  77.1 0.1 pad_add_fusion.refs_1_
  77.2 0.0 collective-permute-done.3.refs_6_
  77.2 0.4 collective-permute-done.2.refs_4_
  77.6 0.0 copy-done
  77.6 12.4 %attend0.1 = (f32[4,144,768]{2,1,0:T(8,128)S(1)}, f32[4,1,768]{2,1,0:T(1,128)S(1)}, bf16[4,256,768]{2,1,0:T(8,128)(2,1)S(1)}) custom-call(s32[128]{0:T(128)S(1)} %copy-done, s32[3]{0:T(128)S(1)} %pad_add_fusion.refs_1_, bf16[8,8,32,256]{3,2,1,0:T(8,128)(2,1)S(1)} %bitcast.19, bf16[8,8,32,256]{3,2,1,0:T(8,128)(2,1)S(1)} %collective-permute-done.refs_3_, ...), custom_call_target="tpu_custom_call" | custom-call | flops 9663676416 | bytes 3145728 | tf_op jit(solution)/shard_map/attend0/pallas_call | solution.py:264
  90.0 0.9 collective-permute-done.1.refs_2_
  90.9 6.2 %attend1.1 = (f32[2,128,768]{2,1,0:T(8,128)S(1)}, f32[2,1,768]{2,1,0:T(1,128)S(1)}, bf16[2,144,768]{2,1,0:T(8,128)(2,1)S(1)}) custom-call(s32[128]{0:T(128)S(1)} %copy-done, s32[3]{0:T(128)S(1)} %pad_add_fusion.refs_1_, bf16[8,8,32,256]{3,2,1,0:T(8,128)(2,1)} %collective-permute-done.1.refs_2_, bf16[4,256,768]{2,1,0:T(8,128)(2,1)S(1)} %get-tuple-element.11.refs_3_, ...), custom_call_target="tpu_custom_call" | custom-call | flops 3221225472 | bytes 1048576 | tf_op jit(solution)/shard_map/attend1/pallas_call | solution.py:264
  97.1 2.8 %collective-permute-start.4 = (bf16[2,144,768]{2,1,0:T(8,128)(2,1)S(1)}, bf16[2,144,768]{2,1,0:T(8,128)(2,1)S(1)}, u32[]{:S(2)}, u32[]{:S(2)}) collective-permute-start(bf16[2,144,768]{2,1,0:T(8,128)(2,1)S(1)} %get-tuple-element.16), channel_id=1, source_target_pairs={{0,8},{8,0},{1,9},{9,1},{2,10},{10,2},{3,11},{11,3},{4,12},{12,4},... | collective-permute-start | bytes 1327112 | tf_op jit(solution)/shard_map/ppermute | solution.py:301
  99.9 1.4 %collective-permute-done.4.got_ref = bf16[2,144,768]{2,1,0:T(8,128)(2,1)S(1)} collective-permute-done((bf16[2,144,768]{2,1,0:T(8,128)(2,1)S(1)}, bf16[2,144,768]{2,1,0:T(8,128)(2,1)S(1)}, u32[]{:S(2)}, u32[]{:S(2)}) %collective-permute-start.4) | collective-permute-done | bytes 442400 | tf_op jit(solution)/shard_map/ppermute | solution.py:301
  101.3 0.3 merge.1
  101.6 23.0 %all_to_all.44 = bf16[8,32,768]{2,1,0:T(8,128)(2,1)S(1)} all-to-all(bf16[8,32,768]{2,1,0:T(8,128)(2,1)S(1)} %bitcast.16), channel_id=1, replica_groups=mesh['head'=8,'zlo'=4,'core'=2,'x'=4,'zhi'=2] {'head'}, dimensions={0} | all-to-all | bytes 786432 | tf_op jit(solution)/shard_map/all_to_all | solution.py:310
  124.6 0.8 copy.8
Async XLA Ops:
  0.0 49.1 %copy-start.1 = (bf16[32,6144]{1,0:T(8,128)(2,1)S(1)}, bf16[32,6144]{1,0:T(8,128)(2,1)}, u32[]{:S(2)}) copy-start(bf16[32,6144]{1,0:T(8,128)(2,1)} %param.4) | copy-start | bytes 1179652
  2.0 75.7 %copy-start = (s32[128]{0:T(128)S(1)}, s32[128]{0:T(128)}, u32[]{:S(2)}) copy-start(s32[128]{0:T(128)} %refs_0_.3) | copy-start | bytes 1540
  46.0 28.1 %collective-permute-start = (bf16[8,8,32,256]{3,2,1,0:T(8,128)(2,1)S(1)}, bf16[8,8,32,256]{3,2,1,0:T(8,128)(2,1)S(1)}, u32[]{:S(2)}, u32[]{:S(2)}) collective-permute-start(bf16[8,8,32,256]{3,2,1,0:T(8,128)(2,1)S(1)} %bitcast.17), channel_id=1, source_target_pairs={{0,6},{2,0},{4,2},{6,4},{8,10},{10,12},{12,14},{14,8},{1,7},{3,1},... | collective-permute-start | bytes 3145736 | tf_op jit(solution)/shard_map/ppermute | solution.py:292
  49.9 17.2 %all-to-all-start.1 = ((bf16[32,8,768]{2,0,1:T(8,128)(2,1)}), bf16[32,8,768]{2,0,1:T(8,128)(2,1)S(1)}, u32[]{:S(2)}, u32[]{:S(2)}) async-start(bf16[32,8,768]{2,0,1:T(8,128)(2,1)} %bitcast.15), calls=%async_computation.1 | async-start | bytes 786432 | tf_op jit(solution)/shard_map/all_to_all | solution.py:291
  56.4 21.2 %collective-permute-start.2 = (bf16[8,8,32,256]{3,2,1,0:T(8,128)(2,1)S(1)}, bf16[8,8,32,256]{3,2,1,0:T(8,128)(2,1)S(1)}, u32[]{:S(2)}, u32[]{:S(2)}) collective-permute-start(bf16[8,8,32,256]{3,2,1,0:T(8,128)(2,1)S(1)} %bitcast.18), channel_id=1, source_target_pairs={{0,2},{2,4},{4,6},{6,0},{8,14},{10,8},{12,10},{14,12},{1,3},{3,5},... | collective-permute-start | bytes 3145736 | tf_op jit(solution)/shard_map/ppermute | solution.py:293
  67.1 10.1 %collective-permute-start.3 = (bf16[256,768]{1,0:T(8,128)(2,1)S(1)}, bf16[256,768]{1,0:T(8,128)(2,1)}, u32[]{:S(2)}, u32[]{:S(2)}) collective-permute-start(bf16[256,768]{1,0:T(8,128)(2,1)S(1)} %bitcast.20), channel_id=1, source_target_pairs={{0,8},{8,0},{1,9},{9,1},{2,10},{10,2},{3,11},{11,3},{4,12},{12,4},... | collective-permute-start | bytes 1179656 | tf_op jit(solution)/shard_map/ppermute | solution.py:294
  74.1 16.9 %collective-permute-start.1 = (bf16[8,8,32,256]{3,2,1,0:T(8,128)(2,1)S(1)}, bf16[8,8,32,256]{3,2,1,0:T(8,128)(2,1)}, u32[]{:S(2)}, u32[]{:S(2)}) collective-permute-start(bf16[8,8,32,256]{3,2,1,0:T(8,128)(2,1)S(1)} %collective-permute-done.refs_3_), channel_id=1, source_target_pairs={{0,6},{2,0},{4,2},{6,4},{8,10},{10,12},{12,14},{14,8},{1,7},{3,1},... | collective-permute-start | bytes 3145736 | tf_op jit(solution)/shard_map/ppermute | solution.py:295
  97.1 4.2 %collective-permute-start.4 = (bf16[2,144,768]{2,1,0:T(8,128)(2,1)S(1)}, bf16[2,144,768]{2,1,0:T(8,128)(2,1)S(1)}, u32[]{:S(2)}, u32[]{:S(2)}) collective-permute-start(bf16[2,144,768]{2,1,0:T(8,128)(2,1)S(1)} %get-tuple-element.16), channel_id=1, source_target_pairs={{0,8},{8,0},{1,9},{9,1},{2,10},{10,2},{3,11},{11,3},{4,12},{12,4},... | collective-permute-start | bytes 1327112 | tf_op jit(solution)/shard_map/ppermute | solution.py:301

commit v5 on v4

--- a/solution.py
+++ b/solution.py
@@ -34,12 +34,12 @@
 
 
 def fill(piece, at, kbuf, vt):
-    for z in range(NZ):
-        for w in range(2):
-            to = (at + 2 * z + w) * CH
-            block = piece[4 * w : 4 * w + 4, z].reshape(CH, 2 * HD)
-            kbuf[to : to + CH, :] = block[:, :HD]
-            vt[:HD, to : to + CH] = block[:, HD:].T
+    for i in range(2 * NZ):
+        w = i % 2
+        to = (at + i) * CH
+        block = piece[i // 8, 4 * w : 4 * w + 4, i // 2 % 4].reshape(CH, 2 * HD)
+        kbuf[to : to + CH, :] = block[:, :HD]
+        vt[:HD, to : to + CH] = block[:, HD:].T
 
 
 def attend(stage, sources, *refs):
@@ -77,12 +77,11 @@
         for shifts in sources:
             xv = (x + jnp.where(core == 0, *shifts)) % NX
 
-            def scan(i, n, xv=xv, slot=slot, mine=mine):
+            for i in range(2 * NZ):
+                zv = i // 2 % 4 * 2 + (z + i // 8) % 2
                 tabk[n] = i + slot
                 tabv[n] = i + slot
-                return n + (order[stored(xv, i // 2, core, i % 2)] < mine).astype(jnp.int32)
-
-            n = lax.fori_loop(0, 2 * NZ, scan, n, unroll=True)
+                n = n + (order[stored(xv, zv, core, i % 2)] < mine).astype(jnp.int32)
             slot += 2 * NZ
         steps = (n - start + GB - 1) // GB
         keep = tabk[jnp.maximum(n - 1, 0)]
@@ -130,7 +129,7 @@
         below = lax.broadcasted_iota(jnp.int32, (CH, CH), 0) <= lax.broadcasted_iota(jnp.int32, (CH, CH), 1)
         below = jnp.concatenate([below] * GROUP, axis=1)
         for j in range(2):
-            r = pl.multiple_of((z * 2 + j) * CH, CH)
+            r = pl.multiple_of((z // 2 * 2 + j) * CH, CH)
             k = kbuf[pl.ds(r, CH), :]
             s = jnp.dot(jnp.concatenate([k, k], axis=1), qt[j], preferred_element_type=F32)
             s = jnp.where(below, s, MASKED)
@@ -211,7 +210,7 @@
     for h in range(HEADS):
         cols = slice(h * HD, (h + 1) * HD)
         both = jnp.concatenate([k_ref[:, cols], v_ref[:, cols]], axis=1)
-        for z in range(NZ):
+        for z in range(NZ // 2):
             out_ref[h, z] = both
 
 
@@ -232,7 +231,7 @@
 
 VMEM = pl.BlockSpec(memory_space=pltpu.VMEM)
 SMEM = pl.BlockSpec(memory_space=pltpu.SMEM)
-SOURCES = (((0, 0), (1, 3), (3, 1)), ((2, 2),))
+SOURCES = (((0, 0),), ((1, 3), (3, 1)), ((2, 2),))
 STAGES = len(SOURCES)
 
 
@@ -277,27 +276,33 @@
     def around(s):
         return [(c * NX + i, c * NX + (i + (s if c else -s)) % NX) for c in range(2) for i in range(NX)]
 
+    def along_z(z, c):
+        return ((z % 4 * 2) + c) * 2 + z // 4
+
+    beside = [(along_z(z, c), along_z((z + (1 if c else -1)) % NZ, c)) for z in range(NZ) for c in range(2)]
+
     kv = pl.pallas_call(
         arrange,
-        out_shape=jax.ShapeDtypeStruct((HEADS, NZ, SLICE, 2 * HD), BF16),
+        out_shape=jax.ShapeDtypeStruct((HEADS, NZ // 2, SLICE, 2 * HD), BF16),
         in_specs=[VMEM] * 2,
         out_specs=VMEM,
         name="arrange",
     )(keys, values)
     kv = lax.all_to_all(
-        kv.reshape(HEADS * NZ, SLICE, 2 * HD), ("head", "zhi", "zlo"), split_axis=0, concat_axis=0, tiled=True
-    )
-    kv0 = kv.reshape(HEADS, NZ, SLICE, 2 * HD)
+        kv.reshape(HEADS * NZ // 2, SLICE, 2 * HD), ("head", "zhi", "zmid"), split_axis=0, concat_axis=0, tiled=True
+    ).reshape(HEADS, NZ // 2, SLICE, 2 * HD)
+    kv0 = jnp.stack([kv, lax.ppermute(kv, ("zmid", "zlow", "core", "zhi"), beside)])
     q = lax.all_to_all(queries, "head", split_axis=1, concat_axis=0, tiled=True)
     kv1 = lax.ppermute(kv0, ("core", "x"), around(1))
     kv3 = lax.ppermute(kv0, ("core", "x"), around(-1))
     qo = lax.ppermute(q, "core", [(0, 1), (1, 0)])
     kv2 = lax.ppermute(kv1, ("core", "x"), around(1))
     pos = jnp.stack(
-        [lax.axis_index("x"), lax.axis_index("zhi") * 4 + lax.axis_index("zlo"), lax.axis_index("core")]
+        [lax.axis_index("x"), lax.axis_index("zhi") * 4 + lax.axis_index("zmid") * 2 + lax.axis_index("zlow"), lax.axis_index("core")]
     ).astype(jnp.int32)
-    acc, top, qt = call(0, order, pos, kv0, kv1, kv3, q, qo)
-    own, ownl, send = call(1, order, pos, kv2, qt, acc, top)
+    acc, top, qt = call(0, order, pos, kv0, q, qo)
+    acc, top = call(1, order, pos, kv1, kv3, qt, acc, top)
+    own, ownl, send = call(2, order, pos, kv2, qt, acc, top)
     got = lax.ppermute(send, "core", [(0, 1), (1, 0)])
     out = pl.pallas_call(
         merge,
@@ -311,8 +316,8 @@
 
 
 def solution(mesh):
-    split = Mesh(mesh.devices.reshape(HEADS, 4, 2, NX, 2), ("head", "zlo", "core", "x", "zhi"))
-    rows = P(("x", "zhi", "zlo", "core", "head"), None)
+    split = Mesh(mesh.devices.reshape(HEADS, 2, 2, 2, NX, 2), ("head", "zmid", "zlow", "core", "x", "zhi"))
+    rows = P(("x", "zhi", "zmid", "zlow", "core", "head"), None)
     return jax.shard_map(
         shards, mesh=split, in_specs=(rows, rows, rows, P()), out_specs=rows, check_vma=False
     )

time: 126 us -> 123 us (0.976)
  blocking collectives: 67 us -> 51.5 us
  waiting for transfers between devices: 10.1 us -> 16.9 us
  Pallas kernels: 20.8 us -> 23.6 us
  starting transfers between devices: 25.8 us -> 27.8 us
    all_to_all x1, blocking collectives: 44 us -> 33.6 us  [shards(): lax.all_to_all(kv.reshape(HEADS * NZ // 2, SLICE, 2 * HD), ('head', 'zhi'...]
    ppermute x0 -> x1, waiting for transfers between devices: none -> 8.08 us  [shards(): lax.ppermute(kv, ('zmid', 'zlow', 'core', 'zhi'), beside)]
    all_to_all x1, blocking collectives: 23 us -> 17.9 us  [shards(): return lax.all_to_all(out, 'head', split_axis=0, concat_axis=1, tiled=True)]
    ppermute x0 -> x1, starting transfers between devices: none -> 3.04 us  [shards(): lax.ppermute(kv, ('zmid', 'zlow', 'core', 'zhi'), beside)]
    pallas_call x2 -> x3, Pallas kernels: 18.6 us -> 21.6 us  [call(): pl.pallas_call(functools.partial(attend, stage, sources), out_shape=outs,...]
    all_to_all x1, starting transfers between devices: 6.55 us -> 4.54 us  [shards(): q = lax.all_to_all(queries, 'head', split_axis=1, concat_axis=0, tiled=True)]
  transfers between devices with their start and end apart: 6 -> 7, of which waited for: 4 -> 3; matrix products, arithmetic and copies ran while one was open for 1% -> 1% of each run, Pallas kernels for 10% -> 12%
where the time goes in v5:
time: 123 us; the launch traced here: 122 us
  blocking collectives  51.5 us (42%)
  starting transfers between devices  27.8 us (23%)
  Pallas kernels  23.6 us (19%)
  waiting for transfers between devices  16.9 us (14%)
  local copies, waits for them, and re-layouts  1.56 us (1%)
    all_to_all x1, blocking collectives, shards(): lax.all_to_all(kv.reshape(HEADS * NZ // 2, SLICE, 2 * HD), ('head', 'zhi'...  33.6 us
    pallas_call x3, Pallas kernels, call(): pl.pallas_call(functools.partial(attend, stage, sources), out_shape=outs,...  21.6 us
    all_to_all x1, blocking collectives, shards(): return lax.all_to_all(out, 'head', split_axis=0, concat_axis=1, tiled=True)  17.9 us
    ppermute x1, waiting for transfers between devices, shards(): lax.ppermute(kv, ('zmid', 'zlow', 'core', 'zhi'), beside)  8.08 us
    ppermute x1, starting transfers between devices, shards(): qo = lax.ppermute(q, 'core', [(0, 1), (1, 0)])  7.42 us
    all_to_all x1, waiting for transfers between devices, shards(): q = lax.all_to_all(queries, 'head', split_axis=1, concat_axis=0, tiled=True)  7.39 us
    all_to_all x1, starting transfers between devices, shards(): q = lax.all_to_all(queries, 'head', split_axis=1, concat_axis=0, tiled=True)  4.54 us
    ppermute x1, starting transfers between devices, shards(): got = lax.ppermute(send, 'core', [(0, 1), (1, 0)])  3.86 us
  transfers between devices with their start and end apart: 7, of which 3 were waited for; matrix products, arithmetic and copies ran while one was open for 1% of the time, Pallas kernels for 12%

profile of v5, /device:TPU:1, one launch (start us, length us, event | category | flops | bytes accessed | tf_op | source)
XLA Modules:
  0.0 121.6 jit_solution(12186391637168780682)
XLA Ops:
  0.0 0.0 copy-start.1
  0.0 1.8 %arrange.1 = bf16[8,4,32,256]{3,2,1,0:T(8,128)(2,1)} custom-call(bf16[32,1024]{1,0:T(8,128)(2,1)} %k_ref.1, bf16[32,1024]{1,0:T(8,128)(2,1)} %v_ref.1), custom_call_target="tpu_custom_call" | custom-call | tf_op jit(solution)/shard_map/arrange/pallas_call | solution.py:284
  1.8 33.6 %all_to_all.43 = bf16[32,32,256]{2,1,0:T(8,128)(2,1)S(1)} all-to-all(bf16[32,32,256]{2,1,0:T(8,128)(2,1)} %bitcast.21), channel_id=1, replica_groups=mesh['head'=8,'zmid'=2,'zlow'=2,'core'=2,'x'=4,'zhi'=2] {'head','zhi','z..., dimensions={0} | all-to-all | bytes 1048576 | tf_op jit(solution)/shard_map/all_to_all | solution.py:291
  35.3 3.0 %collective-permute-start = (bf16[8,4,32,256]{3,2,1,0:T(8,128)(2,1)S(1)}, bf16[8,4,32,256]{3,2,1,0:T(8,128)(2,1)S(1)}, u32[]{:S(2)}, u32[]{:S(2)}) collective-permute-start(bf16[8,4,32,256]{3,2,1,0:T(8,128)(2,1)S(1)} %bitcast.22), channel_id=1, source_target_pairs={{0,49},{8,24},{16,0},{24,40},{32,16},{40,56},{48,32},{56,9},{1,48}... | collective-permute-start | bytes 1572872 | tf_op jit(solution)/shard_map/ppermute | solution.py:294
  38.4 8.1 %collective-permute-done = bf16[8,4,32,256]{3,2,1,0:T(8,128)(2,1)S(1)} collective-permute-done((bf16[8,4,32,256]{3,2,1,0:T(8,128)(2,1)S(1)}, bf16[8,4,32,256]{3,2,1,0:T(8,128)(2,1)S(1)}, u32[]{:S(2)}, u32[]{:S(2)}) %collective-permute-start) | collective-permute-done | bytes 524320 | tf_op jit(solution)/shard_map/ppermute | solution.py:294
  46.5 0.0 copy-start
  46.5 0.1 pad_maximum_fusion.refs_2_
  46.6 3.1 %collective-permute-start.1 = (bf16[2,8,4,32,256]{4,3,2,1,0:T(8,128)(2,1)S(1)}, bf16[2,8,4,32,256]{4,3,2,1,0:T(8,128)(2,1)S(1)}, u32[]{:S(2)}, u32[]{:S(2)}) collective-permute-start(bf16[2,8,4,32,256]{4,3,2,1,0:T(8,128)(2,1)S(1)} %pad_maximum_fusion.refs_2_), channel_id=1, source_target_pairs={{0,6},{2,0},{4,2},{6,4},{8,10},{10,12},{12,14},{14,8},{1,7},{3,1},... | collective-permute-start | bytes 3145736 | tf_op jit(solution)/shard_map/ppermute | solution.py:296
  49.7 0.0 copy-done.1
  49.7 0.8 copy.10
  50.5 4.5 %all-to-all-start.1 = ((bf16[32,8,768]{2,0,1:T(8,128)(2,1)}), bf16[32,8,768]{2,0,1:T(8,128)(2,1)S(1)}, u32[]{:S(2)}, u32[]{:S(2)}) async-start(bf16[32,8,768]{2,0,1:T(8,128)(2,1)} %bitcast.17), calls=%async_computation.1 | async-start | bytes 786432 | tf_op jit(solution)/shard_map/all_to_all | solution.py:295
  55.0 3.4 %collective-permute-start.4 = (bf16[2,8,4,32,256]{4,3,2,1,0:T(8,128)(2,1)S(1)}, bf16[2,8,4,32,256]{4,3,2,1,0:T(8,128)(2,1)S(1)}, u32[]{:S(2)}, u32[]{:S(2)}) collective-permute-start(bf16[2,8,4,32,256]{4,3,2,1,0:T(8,128)(2,1)S(1)} %pad_maximum_fusion.refs_2_), channel_id=1, source_target_pairs={{0,2},{2,4},{4,6},{6,0},{8,14},{10,8},{12,10},{14,12},{1,3},{3,5},... | collective-permute-start | bytes 3145736 | tf_op jit(solution)/shard_map/ppermute | solution.py:297
  58.4 7.4 %all-to-all-done.1 = bf16[32,8,768]{2,0,1:T(8,128)(2,1)S(1)} async-done(((bf16[32,8,768]{2,0,1:T(8,128)(2,1)}), bf16[32,8,768]{2,0,1:T(8,128)(2,1)S(1)}, u32[]{:S(2)}, u32[]{:S(2)}) %all-to-all-start.1) | async-done | bytes 393248 | tf_op jit(solution)/shard_map/all_to_all | solution.py:295
  65.8 7.4 %collective-permute-start.3 = (bf16[256,768]{1,0:T(8,128)(2,1)S(1)}, bf16[256,768]{1,0:T(8,128)(2,1)}, u32[]{:S(2)}, u32[]{:S(2)}) collective-permute-start(bf16[256,768]{1,0:T(8,128)(2,1)S(1)} %bitcast.19), channel_id=1, source_target_pairs={{0,8},{8,0},{1,9},{9,1},{2,10},{10,2},{3,11},{11,3},{4,12},{12,4},... | collective-permute-start | bytes 1179656 | tf_op jit(solution)/shard_map/ppermute | solution.py:298
  73.2 0.0 collective-permute-done.1.refs_2_
  73.2 2.5 %collective-permute-start.2 = (bf16[2,8,4,32,256]{4,3,2,1,0:T(8,128)(2,1)S(1)}, bf16[2,8,4,32,256]{4,3,2,1,0:T(8,128)(2,1)}, u32[]{:S(2)}, u32[]{:S(2)}) collective-permute-start(bf16[2,8,4,32,256]{4,3,2,1,0:T(8,128)(2,1)S(1)} %collective-permute-done.1.refs_2_), channel_id=1, source_target_pairs={{0,6},{2,0},{4,2},{6,4},{8,10},{10,12},{12,14},{14,8},{1,7},{3,1},... | collective-permute-start | bytes 3145736 | tf_op jit(solution)/shard_map/ppermute | solution.py:299
  75.7 0.1 pad_add_fusion.refs_1_
  75.8 0.0 collective-permute-done.3.refs_4_
  75.8 0.0 copy-done
  75.8 6.4 %attend0.1 = (f32[4,144,768]{2,1,0:T(8,128)S(1)}, f32[4,1,768]{2,1,0:T(1,128)S(1)}, bf16[4,256,768]{2,1,0:T(8,128)(2,1)S(1)}) custom-call(s32[128]{0:T(128)S(1)} %copy-done, s32[3]{0:T(128)S(1)} %pad_add_fusion.refs_1_, bf16[2,8,4,32,256]{4,3,2,1,0:T(8,128)(2,1)S(1)} %pad_maximum_fusion.refs_2_, bf16[256,768]{1,0:T(8,128)(2,1)S(1)} %bitcast.20, ...), custom_call_target="tpu_custom_call" | custom-call | flops 3221225472 | bytes 1048576 | tf_op jit(solution)/shard_map/attend0/pallas_call | solution.py:263
  82.2 0.0 collective-permute-done.4.refs_3_
  82.2 8.8 %attend1.1 = (f32[4,144,768]{2,1,0:T(8,128)S(1)}, f32[4,1,768]{2,1,0:T(1,128)S(1)}) custom-call(s32[128]{0:T(128)S(1)} %copy-done, s32[3]{0:T(128)S(1)} %pad_add_fusion.refs_1_, bf16[2,8,4,32,256]{4,3,2,1,0:T(8,128)(2,1)S(1)} %collective-permute-done.1.refs_2_, bf16[2,8,4,32,256]{4,3,2,1,0:T(8,128)(2,1)S(1)} %collective-permute-done.4.refs_3_, ...), custom_call_target="tpu_custom_call" | custom-call | flops 6442450944 | bytes 2097152 | tf_op jit(solution)/shard_map/attend1/pallas_call | solution.py:263
  91.0 0.0 collective-permute-done.2.refs_2_
  91.0 6.4 %attend2.1 = (f32[2,128,768]{2,1,0:T(8,128)S(1)}, f32[2,1,768]{2,1,0:T(1,128)S(1)}, bf16[2,144,768]{2,1,0:T(8,128)(2,1)S(1)}) custom-call(s32[128]{0:T(128)S(1)} %copy-done, s32[3]{0:T(128)S(1)} %pad_add_fusion.refs_1_, bf16[2,8,4,32,256]{4,3,2,1,0:T(8,128)(2,1)} %collective-permute-done.2.refs_2_, ...), custom_call_target="tpu_custom_call" | custom-call | flops 3221225472 | bytes 1048576 | tf_op jit(solution)/shard_map/attend2/pallas_call | solution.py:263
  97.4 3.9 %collective-permute-start.5 = (bf16[2,144,768]{2,1,0:T(8,128)(2,1)S(1)}, bf16[2,144,768]{2,1,0:T(8,128)(2,1)S(1)}, u32[]{:S(2)}, u32[]{:S(2)}) collective-permute-start(bf16[2,144,768]{2,1,0:T(8,128)(2,1)S(1)} %get-tuple-element.20), channel_id=1, source_target_pairs={{0,8},{8,0},{1,9},{9,1},{2,10},{10,2},{3,11},{11,3},{4,12},{12,4},... | collective-permute-start | bytes 1327112 | tf_op jit(solution)/shard_map/ppermute | solution.py:306
  101.3 1.4 %collective-permute-done.5.got_ref = bf16[2,144,768]{2,1,0:T(8,128)(2,1)S(1)} collective-permute-done((bf16[2,144,768]{2,1,0:T(8,128)(2,1)S(1)}, bf16[2,144,768]{2,1,0:T(8,128)(2,1)S(1)}, u32[]{:S(2)}, u32[]{:S(2)}) %collective-permute-start.5) | collective-permute-done | bytes 442400 | tf_op jit(solution)/shard_map/ppermute | solution.py:306
  102.7 0.3 merge.1
  102.9 17.9 %all_to_all.44 = bf16[8,32,768]{2,1,0:T(8,128)(2,1)S(1)} all-to-all(bf16[8,32,768]{2,1,0:T(8,128)(2,1)S(1)} %bitcast.18), channel_id=1, replica_groups=mesh['head'=8,'zmid'=2,'zlow'=2,'core'=2,'x'=4,'zhi'=2] {'head'}, dimensions={0} | all-to-all | bytes 786432 | tf_op jit(solution)/shard_map/all_to_all | solution.py:315
  120.8 0.8 copy.8
Async XLA Ops:
  0.0 49.7 %copy-start.1 = (bf16[32,6144]{1,0:T(8,128)(2,1)S(1)}, bf16[32,6144]{1,0:T(8,128)(2,1)}, u32[]{:S(2)}) copy-start(bf16[32,6144]{1,0:T(8,128)(2,1)} %param.4) | copy-start | bytes 1179652
  35.3 11.1 %collective-permute-start = (bf16[8,4,32,256]{3,2,1,0:T(8,128)(2,1)S(1)}, bf16[8,4,32,256]{3,2,1,0:T(8,128)(2,1)S(1)}, u32[]{:S(2)}, u32[]{:S(2)}) collective-permute-start(bf16[8,4,32,256]{3,2,1,0:T(8,128)(2,1)S(1)} %bitcast.22), channel_id=1, source_target_pairs={{0,49},{8,24},{16,0},{24,40},{32,16},{40,56},{48,32},{56,9},{1,48}... | collective-permute-start | bytes 1572872 | tf_op jit(solution)/shard_map/ppermute | solution.py:294
  46.5 29.3 %copy-start = (s32[128]{0:T(128)S(1)}, s32[128]{0:T(128)}, u32[]{:S(2)}) copy-start(s32[128]{0:T(128)} %refs_0_.5) | copy-start | bytes 1540
  46.6 26.6 %collective-permute-start.1 = (bf16[2,8,4,32,256]{4,3,2,1,0:T(8,128)(2,1)S(1)}, bf16[2,8,4,32,256]{4,3,2,1,0:T(8,128)(2,1)S(1)}, u32[]{:S(2)}, u32[]{:S(2)}) collective-permute-start(bf16[2,8,4,32,256]{4,3,2,1,0:T(8,128)(2,1)S(1)} %pad_maximum_fusion.refs_2_), channel_id=1, source_target_pairs={{0,6},{2,0},{4,2},{6,4},{8,10},{10,12},{12,14},{14,8},{1,7},{3,1},... | collective-permute-start | bytes 3145736 | tf_op jit(solution)/shard_map/ppermute | solution.py:296
  50.5 15.3 %all-to-all-start.1 = ((bf16[32,8,768]{2,0,1:T(8,128)(2,1)}), bf16[32,8,768]{2,0,1:T(8,128)(2,1)S(1)}, u32[]{:S(2)}, u32[]{:S(2)}) async-start(bf16[32,8,768]{2,0,1:T(8,128)(2,1)} %bitcast.17), calls=%async_computation.1 | async-start | bytes 786432 | tf_op jit(solution)/shard_map/all_to_all | solution.py:295
  55.0 27.2 %collective-permute-start.4 = (bf16[2,8,4,32,256]{4,3,2,1,0:T(8,128)(2,1)S(1)}, bf16[2,8,4,32,256]{4,3,2,1,0:T(8,128)(2,1)S(1)}, u32[]{:S(2)}, u32[]{:S(2)}) collective-permute-start(bf16[2,8,4,32,256]{4,3,2,1,0:T(8,128)(2,1)S(1)} %pad_maximum_fusion.refs_2_), channel_id=1, source_target_pairs={{0,2},{2,4},{4,6},{6,0},{8,14},{10,8},{12,10},{14,12},{1,3},{3,5},... | collective-permute-start | bytes 3145736 | tf_op jit(solution)/shard_map/ppermute | solution.py:297
  65.8 10.0 %collective-permute-start.3 = (bf16[256,768]{1,0:T(8,128)(2,1)S(1)}, bf16[256,768]{1,0:T(8,128)(2,1)}, u32[]{:S(2)}, u32[]{:S(2)}) collective-permute-start(bf16[256,768]{1,0:T(8,128)(2,1)S(1)} %bitcast.19), channel_id=1, source_target_pairs={{0,8},{8,0},{1,9},{9,1},{2,10},{10,2},{3,11},{11,3},{4,12},{12,4},... | collective-permute-start | bytes 1179656 | tf_op jit(solution)/shard_map/ppermute | solution.py:298
  73.2 17.8 %collective-permute-start.2 = (bf16[2,8,4,32,256]{4,3,2,1,0:T(8,128)(2,1)S(1)}, bf16[2,8,4,32,256]{4,3,2,1,0:T(8,128)(2,1)}, u32[]{:S(2)}, u32[]{:S(2)}) collective-permute-start(bf16[2,8,4,32,256]{4,3,2,1,0:T(8,128)(2,1)S(1)} %collective-permute-done.1.refs_2_), channel_id=1, source_target_pairs={{0,6},{2,0},{4,2},{6,4},{8,10},{10,12},{12,14},{14,8},{1,7},{3,1},... | collective-permute-start | bytes 3145736 | tf_op jit(solution)/shard_map/ppermute | solution.py:299
  97.4 5.3 %collective-permute-start.5 = (bf16[2,144,768]{2,1,0:T(8,128)(2,1)S(1)}, bf16[2,144,768]{2,1,0:T(8,128)(2,1)S(1)}, u32[]{:S(2)}, u32[]{:S(2)}) collective-permute-start(bf16[2,144,768]{2,1,0:T(8,128)(2,1)S(1)} %get-tuple-element.20), channel_id=1, source_target_pairs={{0,8},{8,0},{1,9},{9,1},{2,10},{10,2},{3,11},{11,3},{4,12},{12,4},... | collective-permute-start | bytes 1327112 | tf_op jit(solution)/shard_map/ppermute | solution.py:306

commit v6 on v5

--- a/solution.py
+++ b/solution.py
@@ -206,7 +206,9 @@
                 send_ref[j - 2, HD:] = tail.astype(BF16)
 
 
-def arrange(k_ref, v_ref, out_ref):
+def arrange(k_ref, v_ref, q_ref, out_ref, qout_ref):
+    for h in range(HEADS):
+        qout_ref[h] = q_ref[:, h * ROWS : (h + 1) * ROWS]
     for h in range(HEADS):
         cols = slice(h * HD, (h + 1) * HD)
         both = jnp.concatenate([k_ref[:, cols], v_ref[:, cols]], axis=1)
@@ -281,26 +283,30 @@
 
     beside = [(along_z(z, c), along_z((z + (1 if c else -1)) % NZ, c)) for z in range(NZ) for c in range(2)]
 
-    kv = pl.pallas_call(
+    kv, q = pl.pallas_call(
         arrange,
-        out_shape=jax.ShapeDtypeStruct((HEADS, NZ // 2, SLICE, 2 * HD), BF16),
-        in_specs=[VMEM] * 2,
-        out_specs=VMEM,
+        out_shape=(
+            jax.ShapeDtypeStruct((HEADS, NZ // 2, SLICE, 2 * HD), BF16),
+            jax.ShapeDtypeStruct((HEADS, SLICE, ROWS), BF16),
+        ),
+        in_specs=[VMEM] * 3,
+        out_specs=(VMEM,) * 2,
         name="arrange",
-    )(keys, values)
+    )(keys, values, queries)
     kv = lax.all_to_all(
         kv.reshape(HEADS * NZ // 2, SLICE, 2 * HD), ("head", "zhi", "zmid"), split_axis=0, concat_axis=0, tiled=True
     ).reshape(HEADS, NZ // 2, SLICE, 2 * HD)
     kv0 = jnp.stack([kv, lax.ppermute(kv, ("zmid", "zlow", "core", "zhi"), beside)])
-    q = lax.all_to_all(queries, "head", split_axis=1, concat_axis=0, tiled=True)
+    q = lax.all_to_all(q, "head", split_axis=0, concat_axis=0, tiled=True).reshape(2 * CH, ROWS)
     kv1 = lax.ppermute(kv0, ("core", "x"), around(1))
     kv3 = lax.ppermute(kv0, ("core", "x"), around(-1))
     qo = lax.ppermute(q, "core", [(0, 1), (1, 0)])
-    kv2 = lax.ppermute(kv1, ("core", "x"), around(1))
     pos = jnp.stack(
         [lax.axis_index("x"), lax.axis_index("zhi") * 4 + lax.axis_index("zmid") * 2 + lax.axis_index("zlow"), lax.axis_index("core")]
     ).astype(jnp.int32)
     acc, top, qt = call(0, order, pos, kv0, q, qo)
+    kv1, kv3, top = lax.optimization_barrier((kv1, kv3, top))
+    kv2 = lax.ppermute(kv1, ("core", "x"), around(1))
     acc, top = call(1, order, pos, kv1, kv3, qt, acc, top)
     own, ownl, send = call(2, order, pos, kv2, qt, acc, top)
     got = lax.ppermute(send, "core", [(0, 1), (1, 0)])

time: 123 us -> 125 us (1.016)
  waiting for transfers between devices: 16.9 us -> 20.7 us
  starting transfers between devices: 27.8 us -> 26 us
    ppermute x1, waiting for transfers between devices: 0.01 us -> 8.28 us  [shards(): kv3 = lax.ppermute(kv0, ('core', 'x'), around(-1))]
    all_to_all x1, waiting for transfers between devices: 7.39 us -> 1.35 us  [shards(): lax.all_to_all(q, 'head', split_axis=0, concat_axis=0, tiled=True)]
    ppermute x1, waiting for transfers between devices: 0.01 us -> 4.69 us  [shards(): kv2 = lax.ppermute(kv1, ('core', 'x'), around(1))]
    ppermute x1, waiting for transfers between devices: 8.08 us -> 3.62 us  [shards(): lax.ppermute(kv, ('zmid', 'zlow', 'core', 'zhi'), beside)]
    ppermute x1, starting transfers between devices: 7.42 us -> 5.95 us  [shards(): qo = lax.ppermute(q, 'core', [(0, 1), (1, 0)])]
    ppermute x1, waiting for transfers between devices: 0.01 us -> 1.37 us  [shards(): qo = lax.ppermute(q, 'core', [(0, 1), (1, 0)])]
  transfers between devices with their start and end apart: 7 -> 7, of which waited for: 3 -> 6; matrix products, arithmetic and copies ran while one was open for 1% -> 0% of each run, Pallas kernels for 12% -> 12%
where the time goes in v6:
time: 125 us; the launch traced here: 123 us
  blocking collectives  51.9 us (42%)
  starting transfers between devices  26 us (21%)
  Pallas kernels  23.4 us (19%)
  waiting for transfers between devices  20.7 us (17%)
    all_to_all x1, blocking collectives, shards(): lax.all_to_all(kv.reshape(HEADS * NZ // 2, SLICE, 2 * HD), ('head', 'zhi'...  33.7 us
    pallas_call x3, Pallas kernels, call(): pl.pallas_call(functools.partial(attend, stage, sources), out_shape=outs,...  21.1 us
    all_to_all x1, blocking collectives, shards(): return lax.all_to_all(out, 'head', split_axis=0, concat_axis=1, tiled=True)  18.2 us
    ppermute x1, waiting for transfers between devices, shards(): kv3 = lax.ppermute(kv0, ('core', 'x'), around(-1))  8.28 us
    ppermute x1, starting transfers between devices, shards(): qo = lax.ppermute(q, 'core', [(0, 1), (1, 0)])  5.95 us
    ppermute x1, waiting for transfers between devices, shards(): kv2 = lax.ppermute(kv1, ('core', 'x'), around(1))  4.69 us
    all_to_all x1, starting transfers between devices, shards(): lax.all_to_all(q, 'head', split_axis=0, concat_axis=0, tiled=True)  4.46 us
    ppermute x1, waiting for transfers between devices, shards(): lax.ppermute(kv, ('zmid', 'zlow', 'core', 'zhi'), beside)  3.62 us
  transfers between devices with their start and end apart: 7, of which 6 were waited for; matrix products, arithmetic and copies ran while one was open for 0% of the time, Pallas kernels for 12%

profile of v6, /device:TPU:1, one launch (start us, length us, event | category | flops | bytes accessed | tf_op | source)
XLA Modules:
  0.0 123.1 jit_solution(13458616174047461569)
XLA Ops:
  0.0 2.0 %arrange.1 = (bf16[8,4,32,256]{3,2,1,0:T(8,128)(2,1)}, bf16[8,32,768]{2,1,0:T(8,128)(2,1)}) custom-call(bf16[32,1024]{1,0:T(8,128)(2,1)} %k_ref.1, bf16[32,1024]{1,0:T(8,128)(2,1)} %v_ref.1, bf16[32,6144]{1,0:T(8,128)(2,1)} %q_ref.1), custom_call_target="tpu_custom_call" | custom-call | tf_op jit(solution)/shard_map/arrange/pallas_call | solution.py:286
  2.0 0.0 copy-start
  2.1 33.7 %all_to_all.29 = bf16[32,32,256]{2,1,0:T(8,128)(2,1)S(1)} all-to-all(bf16[32,32,256]{2,1,0:T(8,128)(2,1)} %bitcast.18), channel_id=1, replica_groups=mesh['head'=8,'zmid'=2,'zlow'=2,'core'=2,'x'=4,'zhi'=2] {'head','zhi','z..., dimensions={0} | all-to-all | bytes 1048576 | tf_op jit(solution)/shard_map/all_to_all | solution.py:296
  35.8 3.0 %collective-permute-start = (bf16[8,4,32,256]{3,2,1,0:T(8,128)(2,1)S(1)}, bf16[8,4,32,256]{3,2,1,0:T(8,128)(2,1)S(1)}, u32[]{:S(2)}, u32[]{:S(2)}) collective-permute-start(bf16[8,4,32,256]{3,2,1,0:T(8,128)(2,1)S(1)} %bitcast.15), channel_id=1, source_target_pairs={{0,49},{8,24},{16,0},{24,40},{32,16},{40,56},{48,32},{56,9},{1,48}... | collective-permute-start | bytes 1572872 | tf_op jit(solution)/shard_map/ppermute | solution.py:299
  38.8 4.5 %all-to-all-start.1 = ((bf16[8,32,768]{2,1,0:T(8,128)(2,1)}), bf16[8,32,768]{2,1,0:T(8,128)(2,1)S(1)}, u32[]{:S(2)}, u32[]{:S(2)}) async-start(bf16[8,32,768]{2,1,0:T(8,128)(2,1)} %get-tuple-element.19), calls=%async_computation.1 | async-start | bytes 786432 | tf_op jit(solution)/shard_map/all_to_all | solution.py:300
  43.3 3.6 %collective-permute-done = bf16[8,4,32,256]{3,2,1,0:T(8,128)(2,1)S(1)} collective-permute-done((bf16[8,4,32,256]{3,2,1,0:T(8,128)(2,1)S(1)}, bf16[8,4,32,256]{3,2,1,0:T(8,128)(2,1)S(1)}, u32[]{:S(2)}, u32[]{:S(2)}) %collective-permute-start) | collective-permute-done | bytes 524320 | tf_op jit(solution)/shard_map/ppermute | solution.py:299
  46.9 0.1 pad_maximum_fusion.refs_2_
  47.0 3.1 %collective-permute-start.1 = (bf16[2,8,4,32,256]{4,3,2,1,0:T(8,128)(2,1)S(1)}, bf16[2,8,4,32,256]{4,3,2,1,0:T(8,128)(2,1)S(1)}, u32[]{:S(2)}, u32[]{:S(2)}) collective-permute-start(bf16[2,8,4,32,256]{4,3,2,1,0:T(8,128)(2,1)S(1)} %pad_maximum_fusion.refs_2_), channel_id=1, source_target_pairs={{0,6},{2,0},{4,2},{6,4},{8,10},{10,12},{12,14},{14,8},{1,7},{3,1},... | collective-permute-start | bytes 3145736 | tf_op jit(solution)/shard_map/ppermute | solution.py:301
  50.1 3.4 %collective-permute-start.2 = (bf16[2,8,4,32,256]{4,3,2,1,0:T(8,128)(2,1)S(1)}, bf16[2,8,4,32,256]{4,3,2,1,0:T(8,128)(2,1)S(1)}, u32[]{:S(2)}, u32[]{:S(2)}) collective-permute-start(bf16[2,8,4,32,256]{4,3,2,1,0:T(8,128)(2,1)S(1)} %pad_maximum_fusion.refs_2_), channel_id=1, source_target_pairs={{0,2},{2,4},{4,6},{6,0},{8,14},{10,8},{12,10},{14,12},{1,3},{3,5},... | collective-permute-start | bytes 3145736 | tf_op jit(solution)/shard_map/ppermute | solution.py:302
  53.5 1.4 %all-to-all-done.1 = bf16[8,32,768]{2,1,0:T(8,128)(2,1)S(1)} async-done(((bf16[8,32,768]{2,1,0:T(8,128)(2,1)}), bf16[8,32,768]{2,1,0:T(8,128)(2,1)S(1)}, u32[]{:S(2)}, u32[]{:S(2)}) %all-to-all-start.1) | async-done | bytes 393248 | tf_op jit(solution)/shard_map/all_to_all | solution.py:300
  54.8 6.0 %collective-permute-start.3 = (bf16[256,768]{1,0:T(8,128)(2,1)S(1)}, bf16[256,768]{1,0:T(8,128)(2,1)}, u32[]{:S(2)}, u32[]{:S(2)}) collective-permute-start(bf16[256,768]{1,0:T(8,128)(2,1)S(1)} %bitcast.13), channel_id=1, source_target_pairs={{0,8},{8,0},{1,9},{9,1},{2,10},{10,2},{3,11},{11,3},{4,12},{12,4},... | collective-permute-start | bytes 1179656 | tf_op jit(solution)/shard_map/ppermute | solution.py:303
  60.8 0.1 pad_add_fusion.refs_1_
  60.9 1.4 %collective-permute-done.3.refs_4_ = bf16[256,768]{1,0:T(8,128)(2,1)} collective-permute-done((bf16[256,768]{1,0:T(8,128)(2,1)S(1)}, bf16[256,768]{1,0:T(8,128)(2,1)}, u32[]{:S(2)}, u32[]{:S(2)}) %collective-permute-start.3) | collective-permute-done | bytes 393248 | tf_op jit(solution)/shard_map/ppermute | solution.py:303
  62.3 0.0 copy-done
  62.3 6.4 %attend0.1 = (f32[4,144,768]{2,1,0:T(8,128)S(1)}, f32[4,1,768]{2,1,0:T(1,128)S(1)}, bf16[4,256,768]{2,1,0:T(8,128)(2,1)S(1)}) custom-call(s32[128]{0:T(128)S(1)} %copy-done, s32[3]{0:T(128)S(1)} %pad_add_fusion.refs_1_, bf16[2,8,4,32,256]{4,3,2,1,0:T(8,128)(2,1)S(1)} %pad_maximum_fusion.refs_2_, bf16[256,768]{1,0:T(8,128)(2,1)S(1)} %bitcast.14, ...), custom_call_target="tpu_custom_call" | custom-call | flops 3221225472 | bytes 1048576 | tf_op jit(solution)/shard_map/attend0/pallas_call | solution.py:265
  68.7 0.0 collective-permute-done.1.refs_2_
  68.7 8.3 %collective-permute-done.2.refs_3_ = bf16[2,8,4,32,256]{4,3,2,1,0:T(8,128)(2,1)S(1)} collective-permute-done((bf16[2,8,4,32,256]{4,3,2,1,0:T(8,128)(2,1)S(1)}, bf16[2,8,4,32,256]{4,3,2,1,0:T(8,128)(2,1)S(1)}, u32[]{:S(2)}, u32[]{:S(2)}) %collective-permute-start.2) | collective-permute-done | bytes 1048608 | tf_op jit(solution)/shard_map/ppermute | solution.py:302
  77.0 3.1 %collective-permute-start.4 = (bf16[2,8,4,32,256]{4,3,2,1,0:T(8,128)(2,1)S(1)}, bf16[2,8,4,32,256]{4,3,2,1,0:T(8,128)(2,1)S(1)}, u32[]{:S(2)}, u32[]{:S(2)}) collective-permute-start(bf16[2,8,4,32,256]{4,3,2,1,0:T(8,128)(2,1)S(1)} %collective-permute-done.1.refs_2_), channel_id=1, source_target_pairs={{0,6},{2,0},{4,2},{6,4},{8,10},{10,12},{12,14},{14,8},{1,7},{3,1},... | collective-permute-start | bytes 3145736 | tf_op jit(solution)/shard_map/ppermute | solution.py:309
  80.1 8.9 %attend1.1 = (f32[4,144,768]{2,1,0:T(8,128)S(1)}, f32[4,1,768]{2,1,0:T(1,128)S(1)}) custom-call(s32[128]{0:T(128)S(1)} %copy-done, s32[3]{0:T(128)S(1)} %pad_add_fusion.refs_1_, bf16[2,8,4,32,256]{4,3,2,1,0:T(8,128)(2,1)S(1)} %collective-permute-done.1.refs_2_, bf16[2,8,4,32,256]{4,3,2,1,0:T(8,128)(2,1)S(1)} %collective-permute-done.2.refs_3_, ...), custom_call_target="tpu_custom_call" | custom-call | flops 6442450944 | bytes 2097152 | tf_op jit(solution)/shard_map/attend1/pallas_call | solution.py:265
  89.0 4.7 %collective-permute-done.4.refs_2_ = bf16[2,8,4,32,256]{4,3,2,1,0:T(8,128)(2,1)S(1)} collective-permute-done((bf16[2,8,4,32,256]{4,3,2,1,0:T(8,128)(2,1)S(1)}, bf16[2,8,4,32,256]{4,3,2,1,0:T(8,128)(2,1)S(1)}, u32[]{:S(2)}, u32[]{:S(2)}) %collective-permute-start.4) | collective-permute-done | bytes 1048608 | tf_op jit(solution)/shard_map/ppermute | solution.py:309
  93.7 5.7 %attend2.1 = (f32[2,128,768]{2,1,0:T(8,128)S(1)}, f32[2,1,768]{2,1,0:T(1,128)S(1)}, bf16[2,144,768]{2,1,0:T(8,128)(2,1)S(1)}) custom-call(s32[128]{0:T(128)S(1)} %copy-done, s32[3]{0:T(128)S(1)} %pad_add_fusion.refs_1_, bf16[2,8,4,32,256]{4,3,2,1,0:T(8,128)(2,1)S(1)} %collective-permute-done.4.refs_2_, ...), custom_call_target="tpu_custom_call" | custom-call | flops 3221225472 | bytes 1048576 | tf_op jit(solution)/shard_map/attend2/pallas_call | solution.py:265
  99.5 2.9 %collective-permute-start.5 = (bf16[2,144,768]{2,1,0:T(8,128)(2,1)S(1)}, bf16[2,144,768]{2,1,0:T(8,128)(2,1)S(1)}, u32[]{:S(2)}, u32[]{:S(2)}) collective-permute-start(bf16[2,144,768]{2,1,0:T(8,128)(2,1)S(1)} %get-tuple-element.30), channel_id=1, source_target_pairs={{0,8},{8,0},{1,9},{9,1},{2,10},{10,2},{3,11},{11,3},{4,12},{12,4},... | collective-permute-start | bytes 1327112 | tf_op jit(solution)/shard_map/ppermute | solution.py:312
  102.4 1.4 %collective-permute-done.5.got_ref = bf16[2,144,768]{2,1,0:T(8,128)(2,1)S(1)} collective-permute-done((bf16[2,144,768]{2,1,0:T(8,128)(2,1)S(1)}, bf16[2,144,768]{2,1,0:T(8,128)(2,1)S(1)}, u32[]{:S(2)}, u32[]{:S(2)}) %collective-permute-start.5) | collective-permute-done | bytes 442400 | tf_op jit(solution)/shard_map/ppermute | solution.py:312
  103.8 0.3 merge.1
  104.1 18.2 %all_to_all.30 = bf16[8,32,768]{2,1,0:T(8,128)(2,1)S(1)} all-to-all(bf16[8,32,768]{2,1,0:T(8,128)(2,1)S(1)} %bitcast.12), channel_id=1, replica_groups=mesh['head'=8,'zmid'=2,'zlow'=2,'core'=2,'x'=4,'zhi'=2] {'head'}, dimensions={0} | all-to-all | bytes 786432 | tf_op jit(solution)/shard_map/all_to_all | solution.py:321
  122.3 0.8 copy.6
Async XLA Ops:
  2.0 60.2 %copy-start = (s32[128]{0:T(128)S(1)}, s32[128]{0:T(128)}, u32[]{:S(2)}) copy-start(s32[128]{0:T(128)} %refs_0_.5) | copy-start | bytes 1540
  35.8 11.1 %collective-permute-start = (bf16[8,4,32,256]{3,2,1,0:T(8,128)(2,1)S(1)}, bf16[8,4,32,256]{3,2,1,0:T(8,128)(2,1)S(1)}, u32[]{:S(2)}, u32[]{:S(2)}) collective-permute-start(bf16[8,4,32,256]{3,2,1,0:T(8,128)(2,1)S(1)} %bitcast.15), channel_id=1, source_target_pairs={{0,49},{8,24},{16,0},{24,40},{32,16},{40,56},{48,32},{56,9},{1,48}... | collective-permute-start | bytes 1572872 | tf_op jit(solution)/shard_map/ppermute | solution.py:299
  38.8 16.0 %all-to-all-start.1 = ((bf16[8,32,768]{2,1,0:T(8,128)(2,1)}), bf16[8,32,768]{2,1,0:T(8,128)(2,1)S(1)}, u32[]{:S(2)}, u32[]{:S(2)}) async-start(bf16[8,32,768]{2,1,0:T(8,128)(2,1)} %get-tuple-element.19), calls=%async_computation.1 | async-start | bytes 786432 | tf_op jit(solution)/shard_map/all_to_all | solution.py:300
  47.0 21.7 %collective-permute-start.1 = (bf16[2,8,4,32,256]{4,3,2,1,0:T(8,128)(2,1)S(1)}, bf16[2,8,4,32,256]{4,3,2,1,0:T(8,128)(2,1)S(1)}, u32[]{:S(2)}, u32[]{:S(2)}) collective-permute-start(bf16[2,8,4,32,256]{4,3,2,1,0:T(8,128)(2,1)S(1)} %pad_maximum_fusion.refs_2_), channel_id=1, source_target_pairs={{0,6},{2,0},{4,2},{6,4},{8,10},{10,12},{12,14},{14,8},{1,7},{3,1},... | collective-permute-start | bytes 3145736 | tf_op jit(solution)/shard_map/ppermute | solution.py:301
  50.1 26.9 %collective-permute-start.2 = (bf16[2,8,4,32,256]{4,3,2,1,0:T(8,128)(2,1)S(1)}, bf16[2,8,4,32,256]{4,3,2,1,0:T(8,128)(2,1)S(1)}, u32[]{:S(2)}, u32[]{:S(2)}) collective-permute-start(bf16[2,8,4,32,256]{4,3,2,1,0:T(8,128)(2,1)S(1)} %pad_maximum_fusion.refs_2_), channel_id=1, source_target_pairs={{0,2},{2,4},{4,6},{6,0},{8,14},{10,8},{12,10},{14,12},{1,3},{3,5},... | collective-permute-start | bytes 3145736 | tf_op jit(solution)/shard_map/ppermute | solution.py:302
  54.8 7.4 %collective-permute-start.3 = (bf16[256,768]{1,0:T(8,128)(2,1)S(1)}, bf16[256,768]{1,0:T(8,128)(2,1)}, u32[]{:S(2)}, u32[]{:S(2)}) collective-permute-start(bf16[256,768]{1,0:T(8,128)(2,1)S(1)} %bitcast.13), channel_id=1, source_target_pairs={{0,8},{8,0},{1,9},{9,1},{2,10},{10,2},{3,11},{11,3},{4,12},{12,4},... | collective-permute-start | bytes 1179656 | tf_op jit(solution)/shard_map/ppermute | solution.py:303
  77.0 16.7 %collective-permute-start.4 = (bf16[2,8,4,32,256]{4,3,2,1,0:T(8,128)(2,1)S(1)}, bf16[2,8,4,32,256]{4,3,2,1,0:T(8,128)(2,1)S(1)}, u32[]{:S(2)}, u32[]{:S(2)}) collective-permute-start(bf16[2,8,4,32,256]{4,3,2,1,0:T(8,128)(2,1)S(1)} %collective-permute-done.1.refs_2_), channel_id=1, source_target_pairs={{0,6},{2,0},{4,2},{6,4},{8,10},{10,12},{12,14},{14,8},{1,7},{3,1},... | collective-permute-start | bytes 3145736 | tf_op jit(solution)/shard_map/ppermute | solution.py:309
  99.5 4.3 %collective-permute-start.5 = (bf16[2,144,768]{2,1,0:T(8,128)(2,1)S(1)}, bf16[2,144,768]{2,1,0:T(8,128)(2,1)S(1)}, u32[]{:S(2)}, u32[]{:S(2)}) collective-permute-start(bf16[2,144,768]{2,1,0:T(8,128)(2,1)S(1)} %get-tuple-element.30), channel_id=1, source_target_pairs={{0,8},{8,0},{1,9},{9,1},{2,10},{10,2},{3,11},{11,3},{4,12},{12,4},... | collective-permute-start | bytes 1327112 | tf_op jit(solution)/shard_map/ppermute | solution.py:312

commit v7 on v6

--- a/solution.py
+++ b/solution.py
@@ -305,7 +305,7 @@
         [lax.axis_index("x"), lax.axis_index("zhi") * 4 + lax.axis_index("zmid") * 2 + lax.axis_index("zlow"), lax.axis_index("core")]
     ).astype(jnp.int32)
     acc, top, qt = call(0, order, pos, kv0, q, qo)
-    kv1, kv3, top = lax.optimization_barrier((kv1, kv3, top))
+    kv1, top = lax.optimization_barrier((kv1, top))
     kv2 = lax.ppermute(kv1, ("core", "x"), around(1))
     acc, top = call(1, order, pos, kv1, kv3, qt, acc, top)
     own, ownl, send = call(2, order, pos, kv2, qt, acc, top)

time: 125 us -> 119 us (0.952)
  waiting for transfers between devices: 20.7 us -> 16.8 us
    ppermute x1, waiting for transfers between devices: 4.69 us -> 0.8 us  [shards(): kv2 = lax.ppermute(kv1, ('core', 'x'), around(1))]
    all_to_all x1, waiting for transfers between devices: 1.35 us -> 4.74 us  [shards(): lax.all_to_all(q, 'head', split_axis=0, concat_axis=0, tiled=True)]
    ppermute x1, waiting for transfers between devices: 8.28 us -> 5.84 us  [shards(): kv3 = lax.ppermute(kv0, ('core', 'x'), around(-1))]
    ppermute x1, waiting for transfers between devices: 1.37 us -> 0.01 us  [shards(): qo = lax.ppermute(q, 'core', [(0, 1), (1, 0)])]
  transfers between devices with their start and end apart: 7 -> 7, of which waited for: 6 -> 5; matrix products, arithmetic and copies ran while one was open for 0% -> 0% of each run, Pallas kernels for 12% -> 13%
where the time goes in v7:
time: 119 us; the launch traced here: 117 us
  blocking collectives  51.3 us (43%)
  starting transfers between devices  24.8 us (21%)
  Pallas kernels  23.4 us (20%)
  waiting for transfers between devices  16.8 us (14%)
    all_to_all x1, blocking collectives, shards(): lax.all_to_all(kv.reshape(HEADS * NZ // 2, SLICE, 2 * HD), ('head', 'zhi'...  33.7 us
    pallas_call x3, Pallas kernels, call(): pl.pallas_call(functools.partial(attend, stage, sources), out_shape=outs,...  21.1 us
    all_to_all x1, blocking collectives, shards(): return lax.all_to_all(out, 'head', split_axis=0, concat_axis=1, tiled=True)  17.5 us
    ppermute x1, starting transfers between devices, shards(): qo = lax.ppermute(q, 'core', [(0, 1), (1, 0)])  5.95 us
    ppermute x1, waiting for transfers between devices, shards(): kv3 = lax.ppermute(kv0, ('core', 'x'), around(-1))  5.84 us
    all_to_all x1, waiting for transfers between devices, shards(): lax.all_to_all(q, 'head', split_axis=0, concat_axis=0, tiled=True)  4.74 us
    all_to_all x1, starting transfers between devices, shards(): lax.all_to_all(q, 'head', split_axis=0, concat_axis=0, tiled=True)  4.46 us
    ppermute x1, starting transfers between devices, shards(): kv3 = lax.ppermute(kv0, ('core', 'x'), around(-1))  4.39 us
  transfers between devices with their start and end apart: 7, of which 5 were waited for; matrix products, arithmetic and copies ran while one was open for 0% of the time, Pallas kernels for 13%

profile of v7, /device:TPU:1, one launch (start us, length us, event | category | flops | bytes accessed | tf_op | source)
XLA Modules:
  0.0 117.3 jit_solution(11976360715183807700)
XLA Ops:
  0.0 2.0 %arrange.1 = (bf16[8,4,32,256]{3,2,1,0:T(8,128)(2,1)}, bf16[8,32,768]{2,1,0:T(8,128)(2,1)}) custom-call(bf16[32,1024]{1,0:T(8,128)(2,1)} %k_ref.1, bf16[32,1024]{1,0:T(8,128)(2,1)} %v_ref.1, bf16[32,6144]{1,0:T(8,128)(2,1)} %q_ref.1), custom_call_target="tpu_custom_call" | custom-call | tf_op jit(solution)/shard_map/arrange/pallas_call | solution.py:286
  2.0 0.0 copy-start
  2.1 33.7 %all_to_all.29 = bf16[32,32,256]{2,1,0:T(8,128)(2,1)S(1)} all-to-all(bf16[32,32,256]{2,1,0:T(8,128)(2,1)} %bitcast.18), channel_id=1, replica_groups=mesh['head'=8,'zmid'=2,'zlow'=2,'core'=2,'x'=4,'zhi'=2] {'head','zhi','z..., dimensions={0} | all-to-all | bytes 1048576 | tf_op jit(solution)/shard_map/all_to_all | solution.py:296
  35.8 3.0 %collective-permute-start = (bf16[8,4,32,256]{3,2,1,0:T(8,128)(2,1)S(1)}, bf16[8,4,32,256]{3,2,1,0:T(8,128)(2,1)S(1)}, u32[]{:S(2)}, u32[]{:S(2)}) collective-permute-start(bf16[8,4,32,256]{3,2,1,0:T(8,128)(2,1)S(1)} %bitcast.15), channel_id=1, source_target_pairs={{0,49},{8,24},{16,0},{24,40},{32,16},{40,56},{48,32},{56,9},{1,48}... | collective-permute-start | bytes 1572872 | tf_op jit(solution)/shard_map/ppermute | solution.py:299
  38.8 4.5 %all-to-all-start.1 = ((bf16[8,32,768]{2,1,0:T(8,128)(2,1)}), bf16[8,32,768]{2,1,0:T(8,128)(2,1)S(1)}, u32[]{:S(2)}, u32[]{:S(2)}) async-start(bf16[8,32,768]{2,1,0:T(8,128)(2,1)} %get-tuple-element.18), calls=%async_computation.1 | async-start | bytes 786432 | tf_op jit(solution)/shard_map/all_to_all | solution.py:300
  43.3 3.6 %collective-permute-done = bf16[8,4,32,256]{3,2,1,0:T(8,128)(2,1)S(1)} collective-permute-done((bf16[8,4,32,256]{3,2,1,0:T(8,128)(2,1)S(1)}, bf16[8,4,32,256]{3,2,1,0:T(8,128)(2,1)S(1)}, u32[]{:S(2)}, u32[]{:S(2)}) %collective-permute-start) | collective-permute-done | bytes 524320 | tf_op jit(solution)/shard_map/ppermute | solution.py:299
  46.9 0.1 pad_maximum_fusion.refs_2_
  47.0 3.1 %collective-permute-start.1 = (bf16[2,8,4,32,256]{4,3,2,1,0:T(8,128)(2,1)S(1)}, bf16[2,8,4,32,256]{4,3,2,1,0:T(8,128)(2,1)S(1)}, u32[]{:S(2)}, u32[]{:S(2)}) collective-permute-start(bf16[2,8,4,32,256]{4,3,2,1,0:T(8,128)(2,1)S(1)} %pad_maximum_fusion.refs_2_), channel_id=1, source_target_pairs={{0,6},{2,0},{4,2},{6,4},{8,10},{10,12},{12,14},{14,8},{1,7},{3,1},... | collective-permute-start | bytes 3145736 | tf_op jit(solution)/shard_map/ppermute | solution.py:301
  50.1 4.7 %all-to-all-done.1 = bf16[8,32,768]{2,1,0:T(8,128)(2,1)S(1)} async-done(((bf16[8,32,768]{2,1,0:T(8,128)(2,1)}), bf16[8,32,768]{2,1,0:T(8,128)(2,1)S(1)}, u32[]{:S(2)}, u32[]{:S(2)}) %all-to-all-start.1) | async-done | bytes 393248 | tf_op jit(solution)/shard_map/all_to_all | solution.py:300
  54.8 6.0 %collective-permute-start.2 = (bf16[256,768]{1,0:T(8,128)(2,1)S(1)}, bf16[256,768]{1,0:T(8,128)(2,1)}, u32[]{:S(2)}, u32[]{:S(2)}) collective-permute-start(bf16[256,768]{1,0:T(8,128)(2,1)S(1)} %bitcast.13), channel_id=1, source_target_pairs={{0,8},{8,0},{1,9},{9,1},{2,10},{10,2},{3,11},{11,3},{4,12},{12,4},... | collective-permute-start | bytes 1179656 | tf_op jit(solution)/shard_map/ppermute | solution.py:303
  60.8 4.4 %collective-permute-start.4 = (bf16[2,8,4,32,256]{4,3,2,1,0:T(8,128)(2,1)S(1)}, bf16[2,8,4,32,256]{4,3,2,1,0:T(8,128)(2,1)S(1)}, u32[]{:S(2)}, u32[]{:S(2)}) collective-permute-start(bf16[2,8,4,32,256]{4,3,2,1,0:T(8,128)(2,1)S(1)} %pad_maximum_fusion.refs_2_), channel_id=1, source_target_pairs={{0,2},{2,4},{4,6},{6,0},{8,14},{10,8},{12,10},{14,12},{1,3},{3,5},... | collective-permute-start | bytes 3145736 | tf_op jit(solution)/shard_map/ppermute | solution.py:302
  65.2 0.1 pad_add_fusion.refs_1_
  65.3 0.0 collective-permute-done.2.refs_4_
  65.3 0.0 copy-done
  65.3 6.5 %attend0.1 = (f32[4,144,768]{2,1,0:T(8,128)S(1)}, f32[4,1,768]{2,1,0:T(1,128)S(1)}, bf16[4,256,768]{2,1,0:T(8,128)(2,1)S(1)}) custom-call(s32[128]{0:T(128)S(1)} %copy-done, s32[3]{0:T(128)S(1)} %pad_add_fusion.refs_1_, bf16[2,8,4,32,256]{4,3,2,1,0:T(8,128)(2,1)S(1)} %pad_maximum_fusion.refs_2_, bf16[256,768]{1,0:T(8,128)(2,1)S(1)} %bitcast.14, ...), custom_call_target="tpu_custom_call" | custom-call | flops 3221225472 | bytes 1048576 | tf_op jit(solution)/shard_map/attend0/pallas_call | solution.py:265
  71.8 0.0 collective-permute-done.1.refs_2_
  71.8 1.9 %collective-permute-start.3 = (bf16[2,8,4,32,256]{4,3,2,1,0:T(8,128)(2,1)S(1)}, bf16[2,8,4,32,256]{4,3,2,1,0:T(8,128)(2,1)S(1)}, u32[]{:S(2)}, u32[]{:S(2)}) collective-permute-start(bf16[2,8,4,32,256]{4,3,2,1,0:T(8,128)(2,1)S(1)} %collective-permute-done.1.refs_2_), channel_id=1, source_target_pairs={{0,6},{2,0},{4,2},{6,4},{8,10},{10,12},{12,14},{14,8},{1,7},{3,1},... | collective-permute-start | bytes 3145736 | tf_op jit(solution)/shard_map/ppermute | solution.py:309
  73.7 5.8 %collective-permute-done.4.refs_3_ = bf16[2,8,4,32,256]{4,3,2,1,0:T(8,128)(2,1)S(1)} collective-permute-done((bf16[2,8,4,32,256]{4,3,2,1,0:T(8,128)(2,1)S(1)}, bf16[2,8,4,32,256]{4,3,2,1,0:T(8,128)(2,1)S(1)}, u32[]{:S(2)}, u32[]{:S(2)}) %collective-permute-start.4) | collective-permute-done | bytes 1048608 | tf_op jit(solution)/shard_map/ppermute | solution.py:302
  79.5 8.9 %attend1.1 = (f32[4,144,768]{2,1,0:T(8,128)S(1)}, f32[4,1,768]{2,1,0:T(1,128)S(1)}) custom-call(s32[128]{0:T(128)S(1)} %copy-done, s32[3]{0:T(128)S(1)} %pad_add_fusion.refs_1_, bf16[2,8,4,32,256]{4,3,2,1,0:T(8,128)(2,1)S(1)} %collective-permute-done.1.refs_2_, bf16[2,8,4,32,256]{4,3,2,1,0:T(8,128)(2,1)S(1)} %collective-permute-done.4.refs_3_, ...), custom_call_target="tpu_custom_call" | custom-call | flops 6442450944 | bytes 2097152 | tf_op jit(solution)/shard_map/attend1/pallas_call | solution.py:265
  88.5 0.8 collective-permute-done.3.refs_2_
  89.3 5.8 %attend2.1 = (f32[2,128,768]{2,1,0:T(8,128)S(1)}, f32[2,1,768]{2,1,0:T(1,128)S(1)}, bf16[2,144,768]{2,1,0:T(8,128)(2,1)S(1)}) custom-call(s32[128]{0:T(128)S(1)} %copy-done, s32[3]{0:T(128)S(1)} %pad_add_fusion.refs_1_, bf16[2,8,4,32,256]{4,3,2,1,0:T(8,128)(2,1)S(1)} %collective-permute-done.3.refs_2_, ...), custom_call_target="tpu_custom_call" | custom-call | flops 3221225472 | bytes 1048576 | tf_op jit(solution)/shard_map/attend2/pallas_call | solution.py:265
  95.0 1.9 %collective-permute-start.5 = (bf16[2,144,768]{2,1,0:T(8,128)(2,1)S(1)}, bf16[2,144,768]{2,1,0:T(8,128)(2,1)S(1)}, u32[]{:S(2)}, u32[]{:S(2)}) collective-permute-start(bf16[2,144,768]{2,1,0:T(8,128)(2,1)S(1)} %get-tuple-element.28), channel_id=1, source_target_pairs={{0,8},{8,0},{1,9},{9,1},{2,10},{10,2},{3,11},{11,3},{4,12},{12,4},... | collective-permute-start | bytes 1327112 | tf_op jit(solution)/shard_map/ppermute | solution.py:312
  97.0 1.8 %collective-permute-done.5.got_ref = bf16[2,144,768]{2,1,0:T(8,128)(2,1)S(1)} collective-permute-done((bf16[2,144,768]{2,1,0:T(8,128)(2,1)S(1)}, bf16[2,144,768]{2,1,0:T(8,128)(2,1)S(1)}, u32[]{:S(2)}, u32[]{:S(2)}) %collective-permute-start.5) | collective-permute-done | bytes 442400 | tf_op jit(solution)/shard_map/ppermute | solution.py:312
  98.7 0.3 merge.1
  99.0 17.5 %all_to_all.30 = bf16[8,32,768]{2,1,0:T(8,128)(2,1)S(1)} all-to-all(bf16[8,32,768]{2,1,0:T(8,128)(2,1)S(1)} %bitcast.12), channel_id=1, replica_groups=mesh['head'=8,'zmid'=2,'zlow'=2,'core'=2,'x'=4,'zhi'=2] {'head'}, dimensions={0} | all-to-all | bytes 786432 | tf_op jit(solution)/shard_map/all_to_all | solution.py:321
  116.5 0.8 copy.6
Async XLA Ops:
  2.0 63.2 %copy-start = (s32[128]{0:T(128)S(1)}, s32[128]{0:T(128)}, u32[]{:S(2)}) copy-start(s32[128]{0:T(128)} %refs_0_.5) | copy-start | bytes 1540
  35.8 11.1 %collective-permute-start = (bf16[8,4,32,256]{3,2,1,0:T(8,128)(2,1)S(1)}, bf16[8,4,32,256]{3,2,1,0:T(8,128)(2,1)S(1)}, u32[]{:S(2)}, u32[]{:S(2)}) collective-permute-start(bf16[8,4,32,256]{3,2,1,0:T(8,128)(2,1)S(1)} %bitcast.15), channel_id=1, source_target_pairs={{0,49},{8,24},{16,0},{24,40},{32,16},{40,56},{48,32},{56,9},{1,48}... | collective-permute-start | bytes 1572872 | tf_op jit(solution)/shard_map/ppermute | solution.py:299
  38.8 16.0 %all-to-all-start.1 = ((bf16[8,32,768]{2,1,0:T(8,128)(2,1)}), bf16[8,32,768]{2,1,0:T(8,128)(2,1)S(1)}, u32[]{:S(2)}, u32[]{:S(2)}) async-start(bf16[8,32,768]{2,1,0:T(8,128)(2,1)} %get-tuple-element.18), calls=%async_computation.1 | async-start | bytes 786432 | tf_op jit(solution)/shard_map/all_to_all | solution.py:300
  47.0 24.8 %collective-permute-start.1 = (bf16[2,8,4,32,256]{4,3,2,1,0:T(8,128)(2,1)S(1)}, bf16[2,8,4,32,256]{4,3,2,1,0:T(8,128)(2,1)S(1)}, u32[]{:S(2)}, u32[]{:S(2)}) collective-permute-start(bf16[2,8,4,32,256]{4,3,2,1,0:T(8,128)(2,1)S(1)} %pad_maximum_fusion.refs_2_), channel_id=1, source_target_pairs={{0,6},{2,0},{4,2},{6,4},{8,10},{10,12},{12,14},{14,8},{1,7},{3,1},... | collective-permute-start | bytes 3145736 | tf_op jit(solution)/shard_map/ppermute | solution.py:301
  54.8 10.4 %collective-permute-start.2 = (bf16[256,768]{1,0:T(8,128)(2,1)S(1)}, bf16[256,768]{1,0:T(8,128)(2,1)}, u32[]{:S(2)}, u32[]{:S(2)}) collective-permute-start(bf16[256,768]{1,0:T(8,128)(2,1)S(1)} %bitcast.13), channel_id=1, source_target_pairs={{0,8},{8,0},{1,9},{9,1},{2,10},{10,2},{3,11},{11,3},{4,12},{12,4},... | collective-permute-start | bytes 1179656 | tf_op jit(solution)/shard_map/ppermute | solution.py:303
  60.8 18.7 %collective-permute-start.4 = (bf16[2,8,4,32,256]{4,3,2,1,0:T(8,128)(2,1)S(1)}, bf16[2,8,4,32,256]{4,3,2,1,0:T(8,128)(2,1)S(1)}, u32[]{:S(2)}, u32[]{:S(2)}) collective-permute-start(bf16[2,8,4,32,256]{4,3,2,1,0:T(8,128)(2,1)S(1)} %pad_maximum_fusion.refs_2_), channel_id=1, source_target_pairs={{0,2},{2,4},{4,6},{6,0},{8,14},{10,8},{12,10},{14,12},{1,3},{3,5},... | collective-permute-start | bytes 3145736 | tf_op jit(solution)/shard_map/ppermute | solution.py:302
  71.8 17.5 %collective-permute-start.3 = (bf16[2,8,4,32,256]{4,3,2,1,0:T(8,128)(2,1)S(1)}, bf16[2,8,4,32,256]{4,3,2,1,0:T(8,128)(2,1)S(1)}, u32[]{:S(2)}, u32[]{:S(2)}) collective-permute-start(bf16[2,8,4,32,256]{4,3,2,1,0:T(8,128)(2,1)S(1)} %collective-permute-done.1.refs_2_), channel_id=1, source_target_pairs={{0,6},{2,0},{4,2},{6,4},{8,10},{10,12},{12,14},{14,8},{1,7},{3,1},... | collective-permute-start | bytes 3145736 | tf_op jit(solution)/shard_map/ppermute | solution.py:309
  95.0 3.7 %collective-permute-start.5 = (bf16[2,144,768]{2,1,0:T(8,128)(2,1)S(1)}, bf16[2,144,768]{2,1,0:T(8,128)(2,1)S(1)}, u32[]{:S(2)}, u32[]{:S(2)}) collective-permute-start(bf16[2,144,768]{2,1,0:T(8,128)(2,1)S(1)} %get-tuple-element.28), channel_id=1, source_target_pairs={{0,8},{8,0},{1,9},{9,1},{2,10},{10,2},{3,11},{11,3},{4,12},{12,4},... | collective-permute-start | bytes 1327112 | tf_op jit(solution)/shard_map/ppermute | solution.py:312

commit v8 on v7

--- a/solution.py
+++ b/solution.py
@@ -296,9 +296,12 @@
     kv = lax.all_to_all(
         kv.reshape(HEADS * NZ // 2, SLICE, 2 * HD), ("head", "zhi", "zmid"), split_axis=0, concat_axis=0, tiled=True
     ).reshape(HEADS, NZ // 2, SLICE, 2 * HD)
-    kv0 = jnp.stack([kv, lax.ppermute(kv, ("zmid", "zlow", "core", "zhi"), beside)])
+    kvz = lax.ppermute(kv, ("zmid", "zlow", "core", "zhi"), beside)
+    kv0 = jnp.stack([kv, kvz])
     q = lax.all_to_all(q, "head", split_axis=0, concat_axis=0, tiled=True).reshape(2 * CH, ROWS)
-    kv1 = lax.ppermute(kv0, ("core", "x"), around(1))
+    near = [lax.ppermute(part, ("core", "x"), around(1)) for part in (kv, kvz)]
+    near[0], near[1], q = lax.optimization_barrier((near[0], near[1], q))
+    kv1 = jnp.stack(near)
     kv3 = lax.ppermute(kv0, ("core", "x"), around(-1))
     qo = lax.ppermute(q, "core", [(0, 1), (1, 0)])
     pos = jnp.stack(

time: 119 us -> 128 us (1.076)
  blocking collectives: 51.3 us -> 55.4 us
  starting transfers between devices: 24.8 us -> 27.7 us
  other arithmetic: 0.17 us -> 2.36 us
  waiting for transfers between devices: 16.8 us -> 18.2 us
    all_to_all x1, blocking collectives: 17.5 us -> 21.8 us  [shards(): return lax.all_to_all(out, 'head', split_axis=0, concat_axis=1, tiled=True)]
    ppermute x2 -> x3, starting transfers between devices: 6.16 us -> 9.25 us  [the longest x2 6.22 us: shards(): near = [lax.ppermute(part, ('core', 'x'), around(1)) for part in (kv, kvz)]]
    another operation x1 -> x2, other arithmetic: 0.1 us -> 2.29 us  [the longest x1 1.15 us: shards(): kv0 = jnp.stack([kv, kvz])]
    ppermute x2 -> x3, waiting for transfers between devices: 3.62 us -> 5.66 us  [the longest x2 5.15 us: shards(): near = [lax.ppermute(part, ('core', 'x'), around(1)) for part in (kv, kvz)]]
  transfers between devices with their start and end apart: 7 -> 8, of which waited for: 5 -> 6; matrix products, arithmetic and copies ran while one was open for 0% -> 2% of each run, Pallas kernels for 13% -> 12%
where the time goes in v8:
time: 128 us; the launch traced here: 127 us
  blocking collectives  55.4 us (43%)
  starting transfers between devices  27.7 us (22%)
  Pallas kernels  22.6 us (18%)
  waiting for transfers between devices  18.2 us (14%)
  other arithmetic  2.36 us (2%)
    all_to_all x1, blocking collectives, shards(): lax.all_to_all(kv.reshape(HEADS * NZ // 2, SLICE, 2 * HD), ('head', 'zhi'...  33.6 us
    all_to_all x1, blocking collectives, shards(): return lax.all_to_all(out, 'head', split_axis=0, concat_axis=1, tiled=True)  21.8 us
    pallas_call x3, Pallas kernels, call(): pl.pallas_call(functools.partial(attend, stage, sources), out_shape=outs,...  20.3 us
    ppermute x2, starting transfers between devices, shards(): near = [lax.ppermute(part, ('core', 'x'), around(1)) for part in (kv, kvz)]  6.22 us
    ppermute x1, starting transfers between devices, shards(): kv3 = lax.ppermute(kv0, ('core', 'x'), around(-1))  5.32 us
    ppermute x2, waiting for transfers between devices, shards(): near = [lax.ppermute(part, ('core', 'x'), around(1)) for part in (kv, kvz)]  5.15 us
    ppermute x1, waiting for transfers between devices, shards(): kv3 = lax.ppermute(kv0, ('core', 'x'), around(-1))  5.07 us
    all_to_all x1, waiting for transfers between devices, shards(): lax.all_to_all(q, 'head', split_axis=0, concat_axis=0, tiled=True)  4.85 us
  transfers between devices with their start and end apart: 8, of which 6 were waited for; matrix products, arithmetic and copies ran while one was open for 2% of the time, Pallas kernels for 12%

profile of v8, /device:TPU:1, one launch (start us, length us, event | category | flops | bytes accessed | tf_op | source)
XLA Modules:
  0.0 127.1 jit_solution(13514753239565170046)
XLA Ops:
  0.0 2.0 %arrange.1 = (bf16[8,4,32,256]{3,2,1,0:T(8,128)(2,1)}, bf16[8,32,768]{2,1,0:T(8,128)(2,1)}) custom-call(bf16[32,1024]{1,0:T(8,128)(2,1)} %k_ref.1, bf16[32,1024]{1,0:T(8,128)(2,1)} %v_ref.1, bf16[32,6144]{1,0:T(8,128)(2,1)} %q_ref.1), custom_call_target="tpu_custom_call" | custom-call | tf_op jit(solution)/shard_map/arrange/pallas_call | solution.py:286
  2.0 33.6 %all_to_all.29 = bf16[32,32,256]{2,1,0:T(8,128)(2,1)S(1)} all-to-all(bf16[32,32,256]{2,1,0:T(8,128)(2,1)} %bitcast.21), channel_id=1, replica_groups=mesh['head'=8,'zmid'=2,'zlow'=2,'core'=2,'x'=4,'zhi'=2] {'head','zhi','z..., dimensions={0} | all-to-all | bytes 1048576 | tf_op jit(solution)/shard_map/all_to_all | solution.py:296
  35.6 3.0 %collective-permute-start.1 = (bf16[8,4,32,256]{3,2,1,0:T(8,128)(2,1)S(1)}, bf16[8,4,32,256]{3,2,1,0:T(8,128)(2,1)S(1)}, u32[]{:S(2)}, u32[]{:S(2)}) collective-permute-start(bf16[8,4,32,256]{3,2,1,0:T(8,128)(2,1)S(1)} %bitcast.17), channel_id=1, source_target_pairs={{0,49},{8,24},{16,0},{24,40},{32,16},{40,56},{48,32},{56,9},{1,48}... | collective-permute-start | bytes 1572872 | tf_op jit(solution)/shard_map/ppermute | solution.py:299
  38.7 4.5 %all-to-all-start.1 = ((bf16[8,32,768]{2,1,0:T(8,128)(2,1)}), bf16[8,32,768]{2,1,0:T(8,128)(2,1)S(1)}, u32[]{:S(2)}, u32[]{:S(2)}) async-start(bf16[8,32,768]{2,1,0:T(8,128)(2,1)} %get-tuple-element.21), calls=%async_computation.1 | async-start | bytes 786432 | tf_op jit(solution)/shard_map/all_to_all | solution.py:301
  43.1 3.1 %collective-permute-start = (bf16[8,4,32,256]{3,2,1,0:T(8,128)(2,1)S(1)}, bf16[8,4,32,256]{3,2,1,0:T(8,128)(2,1)S(1)}, u32[]{:S(2)}, u32[]{:S(2)}) collective-permute-start(bf16[8,4,32,256]{3,2,1,0:T(8,128)(2,1)S(1)} %bitcast.18), channel_id=1, source_target_pairs={{0,6},{2,0},{4,2},{6,4},{8,10},{10,12},{12,14},{14,8},{1,7},{3,1},... | collective-permute-start | bytes 1572872 | tf_op jit(solution)/shard_map/ppermute | solution.py:302
  46.2 0.5 collective-permute-done.1
  46.7 0.0 copy-start.2
  46.7 3.1 %collective-permute-start.2 = (bf16[8,4,32,256]{3,2,1,0:T(8,128)(2,1)S(1)}, bf16[8,4,32,256]{3,2,1,0:T(8,128)(2,1)S(1)}, u32[]{:S(2)}, u32[]{:S(2)}) collective-permute-start(bf16[8,4,32,256]{3,2,1,0:T(8,128)(2,1)S(1)} %collective-permute-done.1), channel_id=1, source_target_pairs={{0,6},{2,0},{4,2},{6,4},{8,10},{10,12},{12,14},{14,8},{1,7},{3,1},... | collective-permute-start | bytes 1572872 | tf_op jit(solution)/shard_map/ppermute | solution.py:302
  49.9 4.8 %all-to-all-done.1 = bf16[8,32,768]{2,1,0:T(8,128)(2,1)S(1)} async-done(((bf16[8,32,768]{2,1,0:T(8,128)(2,1)}), bf16[8,32,768]{2,1,0:T(8,128)(2,1)S(1)}, u32[]{:S(2)}, u32[]{:S(2)}) %all-to-all-start.1) | async-done | bytes 393248 | tf_op jit(solution)/shard_map/all_to_all | solution.py:301
  54.7 0.0 collective-permute-done
  54.7 5.2 %collective-permute-done.2 = bf16[8,4,32,256]{3,2,1,0:T(8,128)(2,1)S(1)} collective-permute-done((bf16[8,4,32,256]{3,2,1,0:T(8,128)(2,1)S(1)}, bf16[8,4,32,256]{3,2,1,0:T(8,128)(2,1)S(1)}, u32[]{:S(2)}, u32[]{:S(2)}) %collective-permute-start.2) | collective-permute-done | bytes 524320 | tf_op jit(solution)/shard_map/ppermute | solution.py:302
  59.9 4.8 %collective-permute-start.3 = (bf16[256,768]{1,0:T(8,128)(2,1)S(1)}, bf16[256,768]{1,0:T(8,128)(2,1)S(1)}, u32[]{:S(2)}, u32[]{:S(2)}) collective-permute-start(bf16[256,768]{1,0:T(8,128)(2,1)S(1)} %bitcast.15), channel_id=1, source_target_pairs={{0,8},{8,0},{1,9},{9,1},{2,10},{10,2},{3,11},{11,3},{4,12},{12,4},... | collective-permute-start | bytes 1179656 | tf_op jit(solution)/shard_map/ppermute | solution.py:306
  64.7 0.0 copy-done.2
  64.7 0.0 copy-done.1
  64.7 0.0 copy-start
  64.7 1.1 pad_maximum_fusion.1.refs_2_
  65.8 5.3 %collective-permute-start.5 = (bf16[2,8,4,32,256]{4,3,2,1,0:T(8,128)(2,1)S(1)}, bf16[2,8,4,32,256]{4,3,2,1,0:T(8,128)(2,1)S(1)}, u32[]{:S(2)}, u32[]{:S(2)}) collective-permute-start(bf16[2,8,4,32,256]{4,3,2,1,0:T(8,128)(2,1)S(1)} %pad_maximum_fusion.1.refs_2_), channel_id=1, source_target_pairs={{0,2},{2,4},{4,6},{6,0},{8,14},{10,8},{12,10},{14,12},{1,3},{3,5},... | collective-permute-start | bytes 3145736 | tf_op jit(solution)/shard_map/ppermute | solution.py:305
  71.2 0.1 pad_add_fusion.refs_1_
  71.3 1.1 pad_maximum_fusion.refs_2_
  72.4 0.0 collective-permute-done.3.refs_4_
  72.4 0.0 copy-done
  72.4 5.9 %attend0.1 = (f32[4,144,768]{2,1,0:T(8,128)S(1)}, f32[4,1,768]{2,1,0:T(1,128)S(1)}, bf16[4,256,768]{2,1,0:T(8,128)(2,1)S(1)}) custom-call(s32[128]{0:T(128)S(1)} %copy-done, s32[3]{0:T(128)S(1)} %pad_add_fusion.refs_1_, bf16[2,8,4,32,256]{4,3,2,1,0:T(8,128)(2,1)S(1)} %pad_maximum_fusion.1.refs_2_, bf16[256,768]{1,0:T(8,128)(2,1)S(1)} %bitcast.16, ...), custom_call_target="tpu_custom_call" | custom-call | flops 3221225472 | bytes 1048576 | tf_op jit(solution)/shard_map/attend0/pallas_call | solution.py:265
  78.4 1.9 %collective-permute-start.4 = (bf16[2,8,4,32,256]{4,3,2,1,0:T(8,128)(2,1)S(1)}, bf16[2,8,4,32,256]{4,3,2,1,0:T(8,128)(2,1)S(1)}, u32[]{:S(2)}, u32[]{:S(2)}) collective-permute-start(bf16[2,8,4,32,256]{4,3,2,1,0:T(8,128)(2,1)S(1)} %pad_maximum_fusion.refs_2_), channel_id=1, source_target_pairs={{0,6},{2,0},{4,2},{6,4},{8,10},{10,12},{12,14},{14,8},{1,7},{3,1},... | collective-permute-start | bytes 3145736 | tf_op jit(solution)/shard_map/ppermute | solution.py:312
  80.3 5.1 %collective-permute-done.5.refs_3_ = bf16[2,8,4,32,256]{4,3,2,1,0:T(8,128)(2,1)S(1)} collective-permute-done((bf16[2,8,4,32,256]{4,3,2,1,0:T(8,128)(2,1)S(1)}, bf16[2,8,4,32,256]{4,3,2,1,0:T(8,128)(2,1)S(1)}, u32[]{:S(2)}, u32[]{:S(2)}) %collective-permute-start.5) | collective-permute-done | bytes 1048608 | tf_op jit(solution)/shard_map/ppermute | solution.py:305
  85.4 8.9 %attend1.1 = (f32[4,144,768]{2,1,0:T(8,128)S(1)}, f32[4,1,768]{2,1,0:T(1,128)S(1)}) custom-call(s32[128]{0:T(128)S(1)} %copy-done, s32[3]{0:T(128)S(1)} %pad_add_fusion.refs_1_, bf16[2,8,4,32,256]{4,3,2,1,0:T(8,128)(2,1)S(1)} %pad_maximum_fusion.refs_2_, bf16[2,8,4,32,256]{4,3,2,1,0:T(8,128)(2,1)S(1)} %collective-permute-done.5.refs_3_, ...), custom_call_target="tpu_custom_call" | custom-call | flops 6442450944 | bytes 2097152 | tf_op jit(solution)/shard_map/attend1/pallas_call | solution.py:265
  94.3 0.9 collective-permute-done.4.refs_2_
  95.1 5.5 %attend2.1 = (f32[2,128,768]{2,1,0:T(8,128)S(1)}, f32[2,1,768]{2,1,0:T(1,128)S(1)}, bf16[2,144,768]{2,1,0:T(8,128)(2,1)S(1)}) custom-call(s32[128]{0:T(128)S(1)} %copy-done, s32[3]{0:T(128)S(1)} %pad_add_fusion.refs_1_, bf16[2,8,4,32,256]{4,3,2,1,0:T(8,128)(2,1)S(1)} %collective-permute-done.4.refs_2_, ...), custom_call_target="tpu_custom_call" | custom-call | flops 3221225472 | bytes 1048576 | tf_op jit(solution)/shard_map/attend2/pallas_call | solution.py:265
  100.6 1.9 %collective-permute-start.6 = (bf16[2,144,768]{2,1,0:T(8,128)(2,1)S(1)}, bf16[2,144,768]{2,1,0:T(8,128)(2,1)S(1)}, u32[]{:S(2)}, u32[]{:S(2)}) collective-permute-start(bf16[2,144,768]{2,1,0:T(8,128)(2,1)S(1)} %get-tuple-element.34), channel_id=1, source_target_pairs={{0,8},{8,0},{1,9},{9,1},{2,10},{10,2},{3,11},{11,3},{4,12},{12,4},... | collective-permute-start | bytes 1327112 | tf_op jit(solution)/shard_map/ppermute | solution.py:315
  102.5 1.8 %collective-permute-done.6.got_ref = bf16[2,144,768]{2,1,0:T(8,128)(2,1)S(1)} collective-permute-done((bf16[2,144,768]{2,1,0:T(8,128)(2,1)S(1)}, bf16[2,144,768]{2,1,0:T(8,128)(2,1)S(1)}, u32[]{:S(2)}, u32[]{:S(2)}) %collective-permute-start.6) | collective-permute-done | bytes 442400 | tf_op jit(solution)/shard_map/ppermute | solution.py:315
  104.3 0.3 merge.1
  104.5 21.8 %all_to_all.30 = bf16[8,32,768]{2,1,0:T(8,128)(2,1)S(1)} all-to-all(bf16[8,32,768]{2,1,0:T(8,128)(2,1)S(1)} %bitcast.14), channel_id=1, replica_groups=mesh['head'=8,'zmid'=2,'zlow'=2,'core'=2,'x'=4,'zhi'=2] {'head'}, dimensions={0} | all-to-all | bytes 786432 | tf_op jit(solution)/shard_map/all_to_all | solution.py:324
  126.3 0.8 copy.6
  (1 shorter events, 0.0 us)
Async XLA Ops:
  35.6 11.1 %collective-permute-start.1 = (bf16[8,4,32,256]{3,2,1,0:T(8,128)(2,1)S(1)}, bf16[8,4,32,256]{3,2,1,0:T(8,128)(2,1)S(1)}, u32[]{:S(2)}, u32[]{:S(2)}) collective-permute-start(bf16[8,4,32,256]{3,2,1,0:T(8,128)(2,1)S(1)} %bitcast.17), channel_id=1, source_target_pairs={{0,49},{8,24},{16,0},{24,40},{32,16},{40,56},{48,32},{56,9},{1,48}... | collective-permute-start | bytes 1572872 | tf_op jit(solution)/shard_map/ppermute | solution.py:299
  38.7 16.0 %all-to-all-start.1 = ((bf16[8,32,768]{2,1,0:T(8,128)(2,1)}), bf16[8,32,768]{2,1,0:T(8,128)(2,1)S(1)}, u32[]{:S(2)}, u32[]{:S(2)}) async-start(bf16[8,32,768]{2,1,0:T(8,128)(2,1)} %get-tuple-element.21), calls=%async_computation.1 | async-start | bytes 786432 | tf_op jit(solution)/shard_map/all_to_all | solution.py:301
  43.1 11.6 %collective-permute-start = (bf16[8,4,32,256]{3,2,1,0:T(8,128)(2,1)S(1)}, bf16[8,4,32,256]{3,2,1,0:T(8,128)(2,1)S(1)}, u32[]{:S(2)}, u32[]{:S(2)}) collective-permute-start(bf16[8,4,32,256]{3,2,1,0:T(8,128)(2,1)S(1)} %bitcast.18), channel_id=1, source_target_pairs={{0,6},{2,0},{4,2},{6,4},{8,10},{10,12},{12,14},{14,8},{1,7},{3,1},... | collective-permute-start | bytes 1572872 | tf_op jit(solution)/shard_map/ppermute | solution.py:302
  46.7 17.9 %copy-start.2 = (bf16[8,4,32,256]{3,2,1,0:T(8,128)(2,1)}, bf16[8,4,32,256]{3,2,1,0:T(8,128)(2,1)S(1)}, u32[]{:S(2)}) copy-start(bf16[8,4,32,256]{3,2,1,0:T(8,128)(2,1)S(1)} %collective-permute-done.1) | copy-start | bytes 1572868
  46.7 13.1 %collective-permute-start.2 = (bf16[8,4,32,256]{3,2,1,0:T(8,128)(2,1)S(1)}, bf16[8,4,32,256]{3,2,1,0:T(8,128)(2,1)S(1)}, u32[]{:S(2)}, u32[]{:S(2)}) collective-permute-start(bf16[8,4,32,256]{3,2,1,0:T(8,128)(2,1)S(1)} %collective-permute-done.1), channel_id=1, source_target_pairs={{0,6},{2,0},{4,2},{6,4},{8,10},{10,12},{12,14},{14,8},{1,7},{3,1},... | collective-permute-start | bytes 1572872 | tf_op jit(solution)/shard_map/ppermute | solution.py:302
  59.9 4.8 %copy-start.1 = (bf16[8,4,32,256]{3,2,1,0:T(8,128)(2,1)}, bf16[8,4,32,256]{3,2,1,0:T(8,128)(2,1)S(1)}, u32[]{:S(2)}) copy-start(bf16[8,4,32,256]{3,2,1,0:T(8,128)(2,1)S(1)} %collective-permute-done.2) | copy-start | bytes 1572868
  59.9 12.5 %collective-permute-start.3 = (bf16[256,768]{1,0:T(8,128)(2,1)S(1)}, bf16[256,768]{1,0:T(8,128)(2,1)S(1)}, u32[]{:S(2)}, u32[]{:S(2)}) collective-permute-start(bf16[256,768]{1,0:T(8,128)(2,1)S(1)} %bitcast.15), channel_id=1, source_target_pairs={{0,8},{8,0},{1,9},{9,1},{2,10},{10,2},{3,11},{11,3},{4,12},{12,4},... | collective-permute-start | bytes 1179656 | tf_op jit(solution)/shard_map/ppermute | solution.py:306
  64.7 7.7 %copy-start = (s32[128]{0:T(128)S(1)}, s32[128]{0:T(128)}, u32[]{:S(2)}) copy-start(s32[128]{0:T(128)} %refs_0_.5) | copy-start | bytes 1540
  65.8 19.5 %collective-permute-start.5 = (bf16[2,8,4,32,256]{4,3,2,1,0:T(8,128)(2,1)S(1)}, bf16[2,8,4,32,256]{4,3,2,1,0:T(8,128)(2,1)S(1)}, u32[]{:S(2)}, u32[]{:S(2)}) collective-permute-start(bf16[2,8,4,32,256]{4,3,2,1,0:T(8,128)(2,1)S(1)} %pad_maximum_fusion.1.refs_2_), channel_id=1, source_target_pairs={{0,2},{2,4},{4,6},{6,0},{8,14},{10,8},{12,10},{14,12},{1,3},{3,5},... | collective-permute-start | bytes 3145736 | tf_op jit(solution)/shard_map/ppermute | solution.py:305
  78.4 16.8 %collective-permute-start.4 = (bf16[2,8,4,32,256]{4,3,2,1,0:T(8,128)(2,1)S(1)}, bf16[2,8,4,32,256]{4,3,2,1,0:T(8,128)(2,1)S(1)}, u32[]{:S(2)}, u32[]{:S(2)}) collective-permute-start(bf16[2,8,4,32,256]{4,3,2,1,0:T(8,128)(2,1)S(1)} %pad_maximum_fusion.refs_2_), channel_id=1, source_target_pairs={{0,6},{2,0},{4,2},{6,4},{8,10},{10,12},{12,14},{14,8},{1,7},{3,1},... | collective-permute-start | bytes 3145736 | tf_op jit(solution)/shard_map/ppermute | solution.py:312
  100.6 3.7 %collective-permute-start.6 = (bf16[2,144,768]{2,1,0:T(8,128)(2,1)S(1)}, bf16[2,144,768]{2,1,0:T(8,128)(2,1)S(1)}, u32[]{:S(2)}, u32[]{:S(2)}) collective-permute-start(bf16[2,144,768]{2,1,0:T(8,128)(2,1)S(1)} %get-tuple-element.34), channel_id=1, source_target_pairs={{0,8},{8,0},{1,9},{9,1},{2,10},{10,2},{3,11},{11,3},{4,12},{12,4},... | collective-permute-start | bytes 1327112 | tf_op jit(solution)/shard_map/ppermute | solution.py:315

commit v9 on v7

--- a/solution.py
+++ b/solution.py
@@ -299,7 +299,8 @@
     kv0 = jnp.stack([kv, lax.ppermute(kv, ("zmid", "zlow", "core", "zhi"), beside)])
     q = lax.all_to_all(q, "head", split_axis=0, concat_axis=0, tiled=True).reshape(2 * CH, ROWS)
     kv1 = lax.ppermute(kv0, ("core", "x"), around(1))
-    kv3 = lax.ppermute(kv0, ("core", "x"), around(-1))
+    late, q = lax.optimization_barrier((kv0, q))
+    kv3 = lax.ppermute(late, ("core", "x"), around(-1))
     qo = lax.ppermute(q, "core", [(0, 1), (1, 0)])
     pos = jnp.stack(
         [lax.axis_index("x"), lax.axis_index("zhi") * 4 + lax.axis_index("zmid") * 2 + lax.axis_index("zlow"), lax.axis_index("core")]

time: 119 us -> 119 us (level)
  transfers between devices with their start and end apart: 7 -> 7, of which waited for: 5 -> 5; matrix products, arithmetic and copies ran while one was open for 0% -> 0% of each run, Pallas kernels for 13% -> 12%
where the time goes in v9:
time: 119 us; the launch traced here: 118 us
  blocking collectives  52 us (44%)
  starting transfers between devices  24.8 us (21%)
  Pallas kernels  22.5 us (19%)
  waiting for transfers between devices  17.7 us (15%)
    all_to_all x1, blocking collectives, shards(): lax.all_to_all(kv.reshape(HEADS * NZ // 2, SLICE, 2 * HD), ('head', 'zhi'...  33.7 us
    pallas_call x3, Pallas kernels, call(): pl.pallas_call(functools.partial(attend, stage, sources), out_shape=outs,...  20.2 us
    all_to_all x1, blocking collectives, shards(): return lax.all_to_all(out, 'head', split_axis=0, concat_axis=1, tiled=True)  18.3 us
    ppermute x1, waiting for transfers between devices, shards(): kv3 = lax.ppermute(late, ('core', 'x'), around(-1))  6.76 us
    ppermute x1, starting transfers between devices, shards(): qo = lax.ppermute(q, 'core', [(0, 1), (1, 0)])  5.95 us
    all_to_all x1, waiting for transfers between devices, shards(): lax.all_to_all(q, 'head', split_axis=0, concat_axis=0, tiled=True)  4.74 us
    all_to_all x1, starting transfers between devices, shards(): lax.all_to_all(q, 'head', split_axis=0, concat_axis=0, tiled=True)  4.46 us
    ppermute x1, starting transfers between devices, shards(): kv3 = lax.ppermute(late, ('core', 'x'), around(-1))  4.39 us
  transfers between devices with their start and end apart: 7, of which 5 were waited for; matrix products, arithmetic and copies ran while one was open for 0% of the time, Pallas kernels for 12%

profile of v9, /device:TPU:1, one launch (start us, length us, event | category | flops | bytes accessed | tf_op | source)
XLA Modules:
  0.0 118.0 jit_solution(11976360715183807700)
XLA Ops:
  0.0 2.0 %arrange.1 = (bf16[8,4,32,256]{3,2,1,0:T(8,128)(2,1)}, bf16[8,32,768]{2,1,0:T(8,128)(2,1)}) custom-call(bf16[32,1024]{1,0:T(8,128)(2,1)} %k_ref.1, bf16[32,1024]{1,0:T(8,128)(2,1)} %v_ref.1, bf16[32,6144]{1,0:T(8,128)(2,1)} %q_ref.1), custom_call_target="tpu_custom_call" | custom-call | tf_op jit(solution)/shard_map/arrange/pallas_call | solution.py:286
  2.0 0.0 copy-start
  2.1 33.7 %all_to_all.29 = bf16[32,32,256]{2,1,0:T(8,128)(2,1)S(1)} all-to-all(bf16[32,32,256]{2,1,0:T(8,128)(2,1)} %bitcast.18), channel_id=1, replica_groups=mesh['head'=8,'zmid'=2,'zlow'=2,'core'=2,'x'=4,'zhi'=2] {'head','zhi','z..., dimensions={0} | all-to-all | bytes 1048576 | tf_op jit(solution)/shard_map/all_to_all | solution.py:296
  35.8 3.0 %collective-permute-start = (bf16[8,4,32,256]{3,2,1,0:T(8,128)(2,1)S(1)}, bf16[8,4,32,256]{3,2,1,0:T(8,128)(2,1)S(1)}, u32[]{:S(2)}, u32[]{:S(2)}) collective-permute-start(bf16[8,4,32,256]{3,2,1,0:T(8,128)(2,1)S(1)} %bitcast.15), channel_id=1, source_target_pairs={{0,49},{8,24},{16,0},{24,40},{32,16},{40,56},{48,32},{56,9},{1,48}... | collective-permute-start | bytes 1572872 | tf_op jit(solution)/shard_map/ppermute | solution.py:299
  38.8 4.5 %all-to-all-start.1 = ((bf16[8,32,768]{2,1,0:T(8,128)(2,1)}), bf16[8,32,768]{2,1,0:T(8,128)(2,1)S(1)}, u32[]{:S(2)}, u32[]{:S(2)}) async-start(bf16[8,32,768]{2,1,0:T(8,128)(2,1)} %get-tuple-element.20), calls=%async_computation.1 | async-start | bytes 786432 | tf_op jit(solution)/shard_map/all_to_all | solution.py:300
  43.3 3.6 %collective-permute-done = bf16[8,4,32,256]{3,2,1,0:T(8,128)(2,1)S(1)} collective-permute-done((bf16[8,4,32,256]{3,2,1,0:T(8,128)(2,1)S(1)}, bf16[8,4,32,256]{3,2,1,0:T(8,128)(2,1)S(1)}, u32[]{:S(2)}, u32[]{:S(2)}) %collective-permute-start) | collective-permute-done | bytes 524320 | tf_op jit(solution)/shard_map/ppermute | solution.py:299
  46.9 0.1 pad_maximum_fusion.refs_2_
  47.0 3.1 %collective-permute-start.1 = (bf16[2,8,4,32,256]{4,3,2,1,0:T(8,128)(2,1)S(1)}, bf16[2,8,4,32,256]{4,3,2,1,0:T(8,128)(2,1)S(1)}, u32[]{:S(2)}, u32[]{:S(2)}) collective-permute-start(bf16[2,8,4,32,256]{4,3,2,1,0:T(8,128)(2,1)S(1)} %pad_maximum_fusion.refs_2_), channel_id=1, source_target_pairs={{0,6},{2,0},{4,2},{6,4},{8,10},{10,12},{12,14},{14,8},{1,7},{3,1},... | collective-permute-start | bytes 3145736 | tf_op jit(solution)/shard_map/ppermute | solution.py:301
  50.1 4.7 %all-to-all-done.1 = bf16[8,32,768]{2,1,0:T(8,128)(2,1)S(1)} async-done(((bf16[8,32,768]{2,1,0:T(8,128)(2,1)}), bf16[8,32,768]{2,1,0:T(8,128)(2,1)S(1)}, u32[]{:S(2)}, u32[]{:S(2)}) %all-to-all-start.1) | async-done | bytes 393248 | tf_op jit(solution)/shard_map/all_to_all | solution.py:300
  54.8 6.0 %collective-permute-start.2 = (bf16[256,768]{1,0:T(8,128)(2,1)S(1)}, bf16[256,768]{1,0:T(8,128)(2,1)}, u32[]{:S(2)}, u32[]{:S(2)}) collective-permute-start(bf16[256,768]{1,0:T(8,128)(2,1)S(1)} %bitcast.13), channel_id=1, source_target_pairs={{0,8},{8,0},{1,9},{9,1},{2,10},{10,2},{3,11},{11,3},{4,12},{12,4},... | collective-permute-start | bytes 1179656 | tf_op jit(solution)/shard_map/ppermute | solution.py:304
  60.8 4.4 %collective-permute-start.4 = (bf16[2,8,4,32,256]{4,3,2,1,0:T(8,128)(2,1)S(1)}, bf16[2,8,4,32,256]{4,3,2,1,0:T(8,128)(2,1)S(1)}, u32[]{:S(2)}, u32[]{:S(2)}) collective-permute-start(bf16[2,8,4,32,256]{4,3,2,1,0:T(8,128)(2,1)S(1)} %pad_maximum_fusion.refs_2_), channel_id=1, source_target_pairs={{0,2},{2,4},{4,6},{6,0},{8,14},{10,8},{12,10},{14,12},{1,3},{3,5},... | collective-permute-start | bytes 3145736 | tf_op jit(solution)/shard_map/ppermute | solution.py:303
  65.2 0.1 pad_add_fusion.refs_1_
  65.3 0.0 collective-permute-done.2.refs_4_
  65.3 0.0 copy-done
  65.3 5.5 %attend0.1 = (f32[4,144,768]{2,1,0:T(8,128)S(1)}, f32[4,1,768]{2,1,0:T(1,128)S(1)}, bf16[4,256,768]{2,1,0:T(8,128)(2,1)S(1)}) custom-call(s32[128]{0:T(128)S(1)} %copy-done, s32[3]{0:T(128)S(1)} %pad_add_fusion.refs_1_, bf16[2,8,4,32,256]{4,3,2,1,0:T(8,128)(2,1)S(1)} %pad_maximum_fusion.refs_2_, bf16[256,768]{1,0:T(8,128)(2,1)S(1)} %bitcast.14, ...), custom_call_target="tpu_custom_call" | custom-call | flops 3221225472 | bytes 1048576 | tf_op jit(solution)/shard_map/attend0/pallas_call | solution.py:265
  70.8 0.0 collective-permute-done.1.refs_2_
  70.9 1.9 %collective-permute-start.3 = (bf16[2,8,4,32,256]{4,3,2,1,0:T(8,128)(2,1)S(1)}, bf16[2,8,4,32,256]{4,3,2,1,0:T(8,128)(2,1)S(1)}, u32[]{:S(2)}, u32[]{:S(2)}) collective-permute-start(bf16[2,8,4,32,256]{4,3,2,1,0:T(8,128)(2,1)S(1)} %collective-permute-done.1.refs_2_), channel_id=1, source_target_pairs={{0,6},{2,0},{4,2},{6,4},{8,10},{10,12},{12,14},{14,8},{1,7},{3,1},... | collective-permute-start | bytes 3145736 | tf_op jit(solution)/shard_map/ppermute | solution.py:310
  72.8 6.8 %collective-permute-done.4.refs_3_ = bf16[2,8,4,32,256]{4,3,2,1,0:T(8,128)(2,1)S(1)} collective-permute-done((bf16[2,8,4,32,256]{4,3,2,1,0:T(8,128)(2,1)S(1)}, bf16[2,8,4,32,256]{4,3,2,1,0:T(8,128)(2,1)S(1)}, u32[]{:S(2)}, u32[]{:S(2)}) %collective-permute-start.4) | collective-permute-done | bytes 1048608 | tf_op jit(solution)/shard_map/ppermute | solution.py:303
  79.5 8.9 %attend1.1 = (f32[4,144,768]{2,1,0:T(8,128)S(1)}, f32[4,1,768]{2,1,0:T(1,128)S(1)}) custom-call(s32[128]{0:T(128)S(1)} %copy-done, s32[3]{0:T(128)S(1)} %pad_add_fusion.refs_1_, bf16[2,8,4,32,256]{4,3,2,1,0:T(8,128)(2,1)S(1)} %collective-permute-done.1.refs_2_, bf16[2,8,4,32,256]{4,3,2,1,0:T(8,128)(2,1)S(1)} %collective-permute-done.4.refs_3_, ...), custom_call_target="tpu_custom_call" | custom-call | flops 6442450944 | bytes 2097152 | tf_op jit(solution)/shard_map/attend1/pallas_call | solution.py:265
  88.5 0.8 collective-permute-done.3.refs_2_
  89.3 5.7 %attend2.1 = (f32[2,128,768]{2,1,0:T(8,128)S(1)}, f32[2,1,768]{2,1,0:T(1,128)S(1)}, bf16[2,144,768]{2,1,0:T(8,128)(2,1)S(1)}) custom-call(s32[128]{0:T(128)S(1)} %copy-done, s32[3]{0:T(128)S(1)} %pad_add_fusion.refs_1_, bf16[2,8,4,32,256]{4,3,2,1,0:T(8,128)(2,1)S(1)} %collective-permute-done.3.refs_2_, ...), custom_call_target="tpu_custom_call" | custom-call | flops 3221225472 | bytes 1048576 | tf_op jit(solution)/shard_map/attend2/pallas_call | solution.py:265
  95.0 1.9 %collective-permute-start.5 = (bf16[2,144,768]{2,1,0:T(8,128)(2,1)S(1)}, bf16[2,144,768]{2,1,0:T(8,128)(2,1)S(1)}, u32[]{:S(2)}, u32[]{:S(2)}) collective-permute-start(bf16[2,144,768]{2,1,0:T(8,128)(2,1)S(1)} %get-tuple-element.32), channel_id=1, source_target_pairs={{0,8},{8,0},{1,9},{9,1},{2,10},{10,2},{3,11},{11,3},{4,12},{12,4},... | collective-permute-start | bytes 1327112 | tf_op jit(solution)/shard_map/ppermute | solution.py:313
  97.0 1.8 %collective-permute-done.5.got_ref = bf16[2,144,768]{2,1,0:T(8,128)(2,1)S(1)} collective-permute-done((bf16[2,144,768]{2,1,0:T(8,128)(2,1)S(1)}, bf16[2,144,768]{2,1,0:T(8,128)(2,1)S(1)}, u32[]{:S(2)}, u32[]{:S(2)}) %collective-permute-start.5) | collective-permute-done | bytes 442400 | tf_op jit(solution)/shard_map/ppermute | solution.py:313
  98.7 0.3 merge.1
  99.0 18.3 %all_to_all.30 = bf16[8,32,768]{2,1,0:T(8,128)(2,1)S(1)} all-to-all(bf16[8,32,768]{2,1,0:T(8,128)(2,1)S(1)} %bitcast.12), channel_id=1, replica_groups=mesh['head'=8,'zmid'=2,'zlow'=2,'core'=2,'x'=4,'zhi'=2] {'head'}, dimensions={0} | all-to-all | bytes 786432 | tf_op jit(solution)/shard_map/all_to_all | solution.py:322
  117.2 0.8 copy.6
Async XLA Ops:
  2.0 63.2 %copy-start = (s32[128]{0:T(128)S(1)}, s32[128]{0:T(128)}, u32[]{:S(2)}) copy-start(s32[128]{0:T(128)} %refs_0_.5) | copy-start | bytes 1540
  35.8 11.1 %collective-permute-start = (bf16[8,4,32,256]{3,2,1,0:T(8,128)(2,1)S(1)}, bf16[8,4,32,256]{3,2,1,0:T(8,128)(2,1)S(1)}, u32[]{:S(2)}, u32[]{:S(2)}) collective-permute-start(bf16[8,4,32,256]{3,2,1,0:T(8,128)(2,1)S(1)} %bitcast.15), channel_id=1, source_target_pairs={{0,49},{8,24},{16,0},{24,40},{32,16},{40,56},{48,32},{56,9},{1,48}... | collective-permute-start | bytes 1572872 | tf_op jit(solution)/shard_map/ppermute | solution.py:299
  38.8 16.0 %all-to-all-start.1 = ((bf16[8,32,768]{2,1,0:T(8,128)(2,1)}), bf16[8,32,768]{2,1,0:T(8,128)(2,1)S(1)}, u32[]{:S(2)}, u32[]{:S(2)}) async-start(bf16[8,32,768]{2,1,0:T(8,128)(2,1)} %get-tuple-element.20), calls=%async_computation.1 | async-start | bytes 786432 | tf_op jit(solution)/shard_map/all_to_all | solution.py:300
  47.0 23.9 %collective-permute-start.1 = (bf16[2,8,4,32,256]{4,3,2,1,0:T(8,128)(2,1)S(1)}, bf16[2,8,4,32,256]{4,3,2,1,0:T(8,128)(2,1)S(1)}, u32[]{:S(2)}, u32[]{:S(2)}) collective-permute-start(bf16[2,8,4,32,256]{4,3,2,1,0:T(8,128)(2,1)S(1)} %pad_maximum_fusion.refs_2_), channel_id=1, source_target_pairs={{0,6},{2,0},{4,2},{6,4},{8,10},{10,12},{12,14},{14,8},{1,7},{3,1},... | collective-permute-start | bytes 3145736 | tf_op jit(solution)/shard_map/ppermute | solution.py:301
  54.8 10.4 %collective-permute-start.2 = (bf16[256,768]{1,0:T(8,128)(2,1)S(1)}, bf16[256,768]{1,0:T(8,128)(2,1)}, u32[]{:S(2)}, u32[]{:S(2)}) collective-permute-start(bf16[256,768]{1,0:T(8,128)(2,1)S(1)} %bitcast.13), channel_id=1, source_target_pairs={{0,8},{8,0},{1,9},{9,1},{2,10},{10,2},{3,11},{11,3},{4,12},{12,4},... | collective-permute-start | bytes 1179656 | tf_op jit(solution)/shard_map/ppermute | solution.py:304
  60.8 18.7 %collective-permute-start.4 = (bf16[2,8,4,32,256]{4,3,2,1,0:T(8,128)(2,1)S(1)}, bf16[2,8,4,32,256]{4,3,2,1,0:T(8,128)(2,1)S(1)}, u32[]{:S(2)}, u32[]{:S(2)}) collective-permute-start(bf16[2,8,4,32,256]{4,3,2,1,0:T(8,128)(2,1)S(1)} %pad_maximum_fusion.refs_2_), channel_id=1, source_target_pairs={{0,2},{2,4},{4,6},{6,0},{8,14},{10,8},{12,10},{14,12},{1,3},{3,5},... | collective-permute-start | bytes 3145736 | tf_op jit(solution)/shard_map/ppermute | solution.py:303
  70.9 18.4 %collective-permute-start.3 = (bf16[2,8,4,32,256]{4,3,2,1,0:T(8,128)(2,1)S(1)}, bf16[2,8,4,32,256]{4,3,2,1,0:T(8,128)(2,1)S(1)}, u32[]{:S(2)}, u32[]{:S(2)}) collective-permute-start(bf16[2,8,4,32,256]{4,3,2,1,0:T(8,128)(2,1)S(1)} %collective-permute-done.1.refs_2_), channel_id=1, source_target_pairs={{0,6},{2,0},{4,2},{6,4},{8,10},{10,12},{12,14},{14,8},{1,7},{3,1},... | collective-permute-start | bytes 3145736 | tf_op jit(solution)/shard_map/ppermute | solution.py:310
  95.0 3.7 %collective-permute-start.5 = (bf16[2,144,768]{2,1,0:T(8,128)(2,1)S(1)}, bf16[2,144,768]{2,1,0:T(8,128)(2,1)S(1)}, u32[]{:S(2)}, u32[]{:S(2)}) collective-permute-start(bf16[2,144,768]{2,1,0:T(8,128)(2,1)S(1)} %get-tuple-element.32), channel_id=1, source_target_pairs={{0,8},{8,0},{1,9},{9,1},{2,10},{10,2},{3,11},{11,3},{4,12},{12,4},... | collective-permute-start | bytes 1327112 | tf_op jit(solution)/shard_map/ppermute | solution.py:313

commit v10 on v9

--- a/solution.py
+++ b/solution.py
@@ -33,11 +33,11 @@
         qt[j, HD:, h * CH : (h + 1) * CH] = (t - hi.astype(F32)).astype(BF16)
 
 
-def fill(piece, at, kbuf, vt):
+def fill(sets, at, kbuf, vt):
     for i in range(2 * NZ):
         w = i % 2
         to = (at + i) * CH
-        block = piece[i // 8, 4 * w : 4 * w + 4, i // 2 % 4].reshape(CH, 2 * HD)
+        block = sets[i // 8][4 * w : 4 * w + 4, i // 2 % 4].reshape(CH, 2 * HD)
         kbuf[to : to + CH, :] = block[:, :HD]
         vt[:HD, to : to + CH] = block[:, HD:].T
 
@@ -46,7 +46,11 @@
     first, last = stage == 0, stage == STAGES - 1
     order, pos = refs[:2]
     refs = refs[2:]
-    pieces, refs = refs[: len(sources)], refs[len(sources) :]
+    if last:
+        pieces, refs = [refs[:2]], refs[2:]
+    else:
+        pieces = [(ref.at[0], ref.at[1]) for ref in refs[: len(sources)]]
+        refs = refs[len(sources) :]
     if first:
         q_ref, qo_ref, acc, top, qt = refs[:5]
         refs = refs[5:]
@@ -307,9 +311,9 @@
     ).astype(jnp.int32)
     acc, top, qt = call(0, order, pos, kv0, q, qo)
     kv1, top = lax.optimization_barrier((kv1, top))
-    kv2 = lax.ppermute(kv1, ("core", "x"), around(1))
+    far = [lax.ppermute(kv1[i], ("core", "x"), around(1)) for i in range(2)]
     acc, top = call(1, order, pos, kv1, kv3, qt, acc, top)
-    own, ownl, send = call(2, order, pos, kv2, qt, acc, top)
+    own, ownl, send = call(2, order, pos, *far, qt, acc, top)
     got = lax.ppermute(send, "core", [(0, 1), (1, 0)])
     out = pl.pallas_call(
         merge,

time: 119 us -> 124 us (1.042)
  starting transfers between devices: 24.8 us -> 29.7 us
  waiting for transfers between devices: 17.7 us -> 13.9 us
  blocking collectives: 52 us -> 54.6 us
    ppermute x1, waiting for transfers between devices: 6.76 us -> 0.01 us  [shards(): kv3 = lax.ppermute(late, ('core', 'x'), around(-1))]
    ppermute x1 -> x2, starting transfers between devices: 1.92 us -> 5.94 us  [shards(): far = [lax.ppermute(kv1[i], ('core', 'x'), around(1)) for i in range(2)]]
    all_to_all x1, blocking collectives: 18.3 us -> 20.9 us  [shards(): return lax.all_to_all(out, 'head', split_axis=0, concat_axis=1, tiled=True)]
    ppermute x1 -> x2, waiting for transfers between devices: 0.8 us -> 2.78 us  [shards(): far = [lax.ppermute(kv1[i], ('core', 'x'), around(1)) for i in range(2)]]
    ppermute x1, starting transfers between devices: 1.92 us -> 3.78 us  [shards(): got = lax.ppermute(send, 'core', [(0, 1), (1, 0)])]
    ppermute x1, waiting for transfers between devices: 0.01 us -> 1.37 us  [shards(): qo = lax.ppermute(q, 'core', [(0, 1), (1, 0)])]
  transfers between devices with their start and end apart: 7 -> 8, of which waited for: 5 -> 5; matrix products, arithmetic and copies ran while one was open for 0% -> 0% of each run, Pallas kernels for 12% -> 12%
where the time goes in v10:
time: 124 us; the launch traced here: 122 us
  blocking collectives  54.6 us (44%)
  starting transfers between devices  29.7 us (24%)
  Pallas kernels  22.5 us (18%)
  waiting for transfers between devices  13.9 us (11%)
    all_to_all x1, blocking collectives, shards(): lax.all_to_all(kv.reshape(HEADS * NZ // 2, SLICE, 2 * HD), ('head', 'zhi'...  33.7 us
    all_to_all x1, blocking collectives, shards(): return lax.all_to_all(out, 'head', split_axis=0, concat_axis=1, tiled=True)  20.9 us
    pallas_call x3, Pallas kernels, call(): pl.pallas_call(functools.partial(attend, stage, sources), out_shape=outs,...  20.2 us
    ppermute x2, starting transfers between devices, shards(): far = [lax.ppermute(kv1[i], ('core', 'x'), around(1)) for i in range(2)]  5.94 us
    ppermute x1, starting transfers between devices, shards(): qo = lax.ppermute(q, 'core', [(0, 1), (1, 0)])  4.98 us
    all_to_all x1, waiting for transfers between devices, shards(): lax.all_to_all(q, 'head', split_axis=0, concat_axis=0, tiled=True)  4.74 us
    all_to_all x1, starting transfers between devices, shards(): lax.all_to_all(q, 'head', split_axis=0, concat_axis=0, tiled=True)  4.46 us
    ppermute x1, starting transfers between devices, shards(): kv3 = lax.ppermute(late, ('core', 'x'), around(-1))  4.38 us
  transfers between devices with their start and end apart: 8, of which 5 were waited for; matrix products, arithmetic and copies ran while one was open for 0% of the time, Pallas kernels for 12%

profile of v10, /device:TPU:1, one launch (start us, length us, event | category | flops | bytes accessed | tf_op | source)
XLA Modules:
  0.0 121.9 jit_solution(5761257002415086102)
XLA Ops:
  0.0 2.0 %arrange.1 = (bf16[8,4,32,256]{3,2,1,0:T(8,128)(2,1)}, bf16[8,32,768]{2,1,0:T(8,128)(2,1)}) custom-call(bf16[32,1024]{1,0:T(8,128)(2,1)} %k_ref.1, bf16[32,1024]{1,0:T(8,128)(2,1)} %v_ref.1, bf16[32,6144]{1,0:T(8,128)(2,1)} %q_ref.1), custom_call_target="tpu_custom_call" | custom-call | tf_op jit(solution)/shard_map/arrange/pallas_call | solution.py:290
  2.0 0.0 copy-start
  2.0 33.7 %all_to_all.29 = bf16[32,32,256]{2,1,0:T(8,128)(2,1)S(1)} all-to-all(bf16[32,32,256]{2,1,0:T(8,128)(2,1)} %bitcast.22), channel_id=1, replica_groups=mesh['head'=8,'zmid'=2,'zlow'=2,'core'=2,'x'=4,'zhi'=2] {'head','zhi','z..., dimensions={0} | all-to-all | bytes 1048576 | tf_op jit(solution)/shard_map/all_to_all | solution.py:300
  35.7 3.0 %collective-permute-start = (bf16[8,4,32,256]{3,2,1,0:T(8,128)(2,1)S(1)}, bf16[8,4,32,256]{3,2,1,0:T(8,128)(2,1)S(1)}, u32[]{:S(2)}, u32[]{:S(2)}) collective-permute-start(bf16[8,4,32,256]{3,2,1,0:T(8,128)(2,1)S(1)} %bitcast.19), channel_id=1, source_target_pairs={{0,49},{8,24},{16,0},{24,40},{32,16},{40,56},{48,32},{56,9},{1,48}... | collective-permute-start | bytes 1572872 | tf_op jit(solution)/shard_map/ppermute | solution.py:303
  38.8 4.5 %all-to-all-start.1 = ((bf16[8,32,768]{2,1,0:T(8,128)(2,1)}), bf16[8,32,768]{2,1,0:T(8,128)(2,1)S(1)}, u32[]{:S(2)}, u32[]{:S(2)}) async-start(bf16[8,32,768]{2,1,0:T(8,128)(2,1)} %get-tuple-element.20), calls=%async_computation.1 | async-start | bytes 786432 | tf_op jit(solution)/shard_map/all_to_all | solution.py:304
  43.2 3.6 %collective-permute-done = bf16[8,4,32,256]{3,2,1,0:T(8,128)(2,1)S(1)} collective-permute-done((bf16[8,4,32,256]{3,2,1,0:T(8,128)(2,1)S(1)}, bf16[8,4,32,256]{3,2,1,0:T(8,128)(2,1)S(1)}, u32[]{:S(2)}, u32[]{:S(2)}) %collective-permute-start) | collective-permute-done | bytes 524320 | tf_op jit(solution)/shard_map/ppermute | solution.py:303
  46.9 0.1 pad_maximum_fusion.refs_2_
  47.0 3.1 %collective-permute-start.1 = (bf16[2,8,4,32,256]{4,3,2,1,0:T(8,128)(2,1)S(1)}, bf16[2,8,4,32,256]{4,3,2,1,0:T(8,128)(2,1)S(1)}, u32[]{:S(2)}, u32[]{:S(2)}) collective-permute-start(bf16[2,8,4,32,256]{4,3,2,1,0:T(8,128)(2,1)S(1)} %pad_maximum_fusion.refs_2_), channel_id=1, source_target_pairs={{0,6},{2,0},{4,2},{6,4},{8,10},{10,12},{12,14},{14,8},{1,7},{3,1},... | collective-permute-start | bytes 3145736 | tf_op jit(solution)/shard_map/ppermute | solution.py:305
  50.1 4.7 %all-to-all-done.1 = bf16[8,32,768]{2,1,0:T(8,128)(2,1)S(1)} async-done(((bf16[8,32,768]{2,1,0:T(8,128)(2,1)}), bf16[8,32,768]{2,1,0:T(8,128)(2,1)S(1)}, u32[]{:S(2)}, u32[]{:S(2)}) %all-to-all-start.1) | async-done | bytes 393248 | tf_op jit(solution)/shard_map/all_to_all | solution.py:304
  54.8 4.4 %collective-permute-start.5 = (bf16[2,8,4,32,256]{4,3,2,1,0:T(8,128)(2,1)S(1)}, bf16[2,8,4,32,256]{4,3,2,1,0:T(8,128)(2,1)S(1)}, u32[]{:S(2)}, u32[]{:S(2)}) collective-permute-start(bf16[2,8,4,32,256]{4,3,2,1,0:T(8,128)(2,1)S(1)} %pad_maximum_fusion.refs_2_), channel_id=1, source_target_pairs={{0,2},{2,4},{4,6},{6,0},{8,14},{10,8},{12,10},{14,12},{1,3},{3,5},... | collective-permute-start | bytes 3145736 | tf_op jit(solution)/shard_map/ppermute | solution.py:307
  59.2 5.0 %collective-permute-start.2 = (bf16[256,768]{1,0:T(8,128)(2,1)S(1)}, bf16[256,768]{1,0:T(8,128)(2,1)}, u32[]{:S(2)}, u32[]{:S(2)}) collective-permute-start(bf16[256,768]{1,0:T(8,128)(2,1)S(1)} %bitcast.17), channel_id=1, source_target_pairs={{0,8},{8,0},{1,9},{9,1},{2,10},{10,2},{3,11},{11,3},{4,12},{12,4},... | collective-permute-start | bytes 1179656 | tf_op jit(solution)/shard_map/ppermute | solution.py:308
  64.2 0.1 pad_add_fusion.refs_1_
  64.3 1.4 %collective-permute-done.2.refs_4_ = bf16[256,768]{1,0:T(8,128)(2,1)} collective-permute-done((bf16[256,768]{1,0:T(8,128)(2,1)S(1)}, bf16[256,768]{1,0:T(8,128)(2,1)}, u32[]{:S(2)}, u32[]{:S(2)}) %collective-permute-start.2) | collective-permute-done | bytes 393248 | tf_op jit(solution)/shard_map/ppermute | solution.py:308
  65.7 0.0 copy-done
  65.7 6.4 %attend0.1 = (f32[4,144,768]{2,1,0:T(8,128)S(1)}, f32[4,1,768]{2,1,0:T(1,128)S(1)}, bf16[4,256,768]{2,1,0:T(8,128)(2,1)S(1)}) custom-call(s32[128]{0:T(128)S(1)} %copy-done, s32[3]{0:T(128)S(1)} %pad_add_fusion.refs_1_, bf16[2,8,4,32,256]{4,3,2,1,0:T(8,128)(2,1)S(1)} %pad_maximum_fusion.refs_2_, bf16[256,768]{1,0:T(8,128)(2,1)S(1)} %bitcast.18, ...), custom_call_target="tpu_custom_call" | custom-call | flops 3221225472 | bytes 1048576 | tf_op jit(solution)/shard_map/attend0/pallas_call | solution.py:269
  72.1 0.0 collective-permute-done.1.refs_2_
  72.1 0.1 slice_bitcast_fusion
  72.2 3.1 %collective-permute-start.3 = (bf16[8,4,32,256]{3,2,1,0:T(8,128)(2,1)S(1)}, bf16[8,4,32,256]{3,2,1,0:T(8,128)(2,1)S(1)}, u32[]{:S(2)}, u32[]{:S(2)}) collective-permute-start(bf16[8,4,32,256]{3,2,1,0:T(8,128)(2,1)S(1)} %get-tuple-element.34), channel_id=1, source_target_pairs={{0,6},{2,0},{4,2},{6,4},{8,10},{10,12},{12,14},{14,8},{1,7},{3,1},... | collective-permute-start | bytes 1572872 | tf_op jit(solution)/shard_map/ppermute | solution.py:314
  75.4 2.8 %collective-permute-start.4 = (bf16[8,4,32,256]{3,2,1,0:T(8,128)(2,1)S(1)}, bf16[8,4,32,256]{3,2,1,0:T(8,128)(2,1)S(1)}, u32[]{:S(2)}, u32[]{:S(2)}) collective-permute-start(bf16[8,4,32,256]{3,2,1,0:T(8,128)(2,1)S(1)} %get-tuple-element.33), channel_id=1, source_target_pairs={{0,6},{2,0},{4,2},{6,4},{8,10},{10,12},{12,14},{14,8},{1,7},{3,1},... | collective-permute-start | bytes 1572872 | tf_op jit(solution)/shard_map/ppermute | solution.py:314
  78.2 0.0 collective-permute-done.5.refs_3_
  78.2 8.0 %attend1.1 = (f32[4,144,768]{2,1,0:T(8,128)S(1)}, f32[4,1,768]{2,1,0:T(1,128)S(1)}) custom-call(s32[128]{0:T(128)S(1)} %copy-done, s32[3]{0:T(128)S(1)} %pad_add_fusion.refs_1_, bf16[2,8,4,32,256]{4,3,2,1,0:T(8,128)(2,1)S(1)} %collective-permute-done.1.refs_2_, bf16[2,8,4,32,256]{4,3,2,1,0:T(8,128)(2,1)S(1)} %collective-permute-done.5.refs_3_, ...), custom_call_target="tpu_custom_call" | custom-call | flops 6442450944 | bytes 2097152 | tf_op jit(solution)/shard_map/attend1/pallas_call | solution.py:269
  86.2 0.0 collective-permute-done.3.refs_2_
  86.2 2.8 %collective-permute-done.4.refs_3_ = bf16[8,4,32,256]{3,2,1,0:T(8,128)(2,1)S(1)} collective-permute-done((bf16[8,4,32,256]{3,2,1,0:T(8,128)(2,1)S(1)}, bf16[8,4,32,256]{3,2,1,0:T(8,128)(2,1)S(1)}, u32[]{:S(2)}, u32[]{:S(2)}) %collective-permute-start.4) | collective-permute-done | bytes 524320 | tf_op jit(solution)/shard_map/ppermute | solution.py:314
  89.0 5.7 %attend2.1 = (f32[2,128,768]{2,1,0:T(8,128)S(1)}, f32[2,1,768]{2,1,0:T(1,128)S(1)}, bf16[2,144,768]{2,1,0:T(8,128)(2,1)S(1)}) custom-call(s32[128]{0:T(128)S(1)} %copy-done, s32[3]{0:T(128)S(1)} %pad_add_fusion.refs_1_, bf16[8,4,32,256]{3,2,1,0:T(8,128)(2,1)S(1)} %collective-permute-done.3.refs_2_, ...), custom_call_target="tpu_custom_call" | custom-call | flops 3221225472 | bytes 1048576 | tf_op jit(solution)/shard_map/attend2/pallas_call | solution.py:269
  94.7 3.8 %collective-permute-start.6 = (bf16[2,144,768]{2,1,0:T(8,128)(2,1)S(1)}, bf16[2,144,768]{2,1,0:T(8,128)(2,1)S(1)}, u32[]{:S(2)}, u32[]{:S(2)}) collective-permute-start(bf16[2,144,768]{2,1,0:T(8,128)(2,1)S(1)} %get-tuple-element.32), channel_id=1, source_target_pairs={{0,8},{8,0},{1,9},{9,1},{2,10},{10,2},{3,11},{11,3},{4,12},{12,4},... | collective-permute-start | bytes 1327112 | tf_op jit(solution)/shard_map/ppermute | solution.py:317
  98.5 1.4 %collective-permute-done.6.got_ref = bf16[2,144,768]{2,1,0:T(8,128)(2,1)S(1)} collective-permute-done((bf16[2,144,768]{2,1,0:T(8,128)(2,1)S(1)}, bf16[2,144,768]{2,1,0:T(8,128)(2,1)S(1)}, u32[]{:S(2)}, u32[]{:S(2)}) %collective-permute-start.6) | collective-permute-done | bytes 442400 | tf_op jit(solution)/shard_map/ppermute | solution.py:317
  99.9 0.3 merge.1
  100.2 20.9 %all_to_all.30 = bf16[8,32,768]{2,1,0:T(8,128)(2,1)S(1)} all-to-all(bf16[8,32,768]{2,1,0:T(8,128)(2,1)S(1)} %bitcast.16), channel_id=1, replica_groups=mesh['head'=8,'zmid'=2,'zlow'=2,'core'=2,'x'=4,'zhi'=2] {'head'}, dimensions={0} | all-to-all | bytes 786432 | tf_op jit(solution)/shard_map/all_to_all | solution.py:326
  121.1 0.8 copy.6
Async XLA Ops:
  2.0 63.6 %copy-start = (s32[128]{0:T(128)S(1)}, s32[128]{0:T(128)}, u32[]{:S(2)}) copy-start(s32[128]{0:T(128)} %refs_0_.5) | copy-start | bytes 1540
  35.7 11.1 %collective-permute-start = (bf16[8,4,32,256]{3,2,1,0:T(8,128)(2,1)S(1)}, bf16[8,4,32,256]{3,2,1,0:T(8,128)(2,1)S(1)}, u32[]{:S(2)}, u32[]{:S(2)}) collective-permute-start(bf16[8,4,32,256]{3,2,1,0:T(8,128)(2,1)S(1)} %bitcast.19), channel_id=1, source_target_pairs={{0,49},{8,24},{16,0},{24,40},{32,16},{40,56},{48,32},{56,9},{1,48}... | collective-permute-start | bytes 1572872 | tf_op jit(solution)/shard_map/ppermute | solution.py:303
  38.8 16.0 %all-to-all-start.1 = ((bf16[8,32,768]{2,1,0:T(8,128)(2,1)}), bf16[8,32,768]{2,1,0:T(8,128)(2,1)S(1)}, u32[]{:S(2)}, u32[]{:S(2)}) async-start(bf16[8,32,768]{2,1,0:T(8,128)(2,1)} %get-tuple-element.20), calls=%async_computation.1 | async-start | bytes 786432 | tf_op jit(solution)/shard_map/all_to_all | solution.py:304
  47.0 25.2 %collective-permute-start.1 = (bf16[2,8,4,32,256]{4,3,2,1,0:T(8,128)(2,1)S(1)}, bf16[2,8,4,32,256]{4,3,2,1,0:T(8,128)(2,1)S(1)}, u32[]{:S(2)}, u32[]{:S(2)}) collective-permute-start(bf16[2,8,4,32,256]{4,3,2,1,0:T(8,128)(2,1)S(1)} %pad_maximum_fusion.refs_2_), channel_id=1, source_target_pairs={{0,6},{2,0},{4,2},{6,4},{8,10},{10,12},{12,14},{14,8},{1,7},{3,1},... | collective-permute-start | bytes 3145736 | tf_op jit(solution)/shard_map/ppermute | solution.py:305
  54.8 23.4 %collective-permute-start.5 = (bf16[2,8,4,32,256]{4,3,2,1,0:T(8,128)(2,1)S(1)}, bf16[2,8,4,32,256]{4,3,2,1,0:T(8,128)(2,1)S(1)}, u32[]{:S(2)}, u32[]{:S(2)}) collective-permute-start(bf16[2,8,4,32,256]{4,3,2,1,0:T(8,128)(2,1)S(1)} %pad_maximum_fusion.refs_2_), channel_id=1, source_target_pairs={{0,2},{2,4},{4,6},{6,0},{8,14},{10,8},{12,10},{14,12},{1,3},{3,5},... | collective-permute-start | bytes 3145736 | tf_op jit(solution)/shard_map/ppermute | solution.py:307
  59.2 6.4 %collective-permute-start.2 = (bf16[256,768]{1,0:T(8,128)(2,1)S(1)}, bf16[256,768]{1,0:T(8,128)(2,1)}, u32[]{:S(2)}, u32[]{:S(2)}) collective-permute-start(bf16[256,768]{1,0:T(8,128)(2,1)S(1)} %bitcast.17), channel_id=1, source_target_pairs={{0,8},{8,0},{1,9},{9,1},{2,10},{10,2},{3,11},{11,3},{4,12},{12,4},... | collective-permute-start | bytes 1179656 | tf_op jit(solution)/shard_map/ppermute | solution.py:308
  72.2 14.0 %collective-permute-start.3 = (bf16[8,4,32,256]{3,2,1,0:T(8,128)(2,1)S(1)}, bf16[8,4,32,256]{3,2,1,0:T(8,128)(2,1)S(1)}, u32[]{:S(2)}, u32[]{:S(2)}) collective-permute-start(bf16[8,4,32,256]{3,2,1,0:T(8,128)(2,1)S(1)} %get-tuple-element.34), channel_id=1, source_target_pairs={{0,6},{2,0},{4,2},{6,4},{8,10},{10,12},{12,14},{14,8},{1,7},{3,1},... | collective-permute-start | bytes 1572872 | tf_op jit(solution)/shard_map/ppermute | solution.py:314
  75.4 13.6 %collective-permute-start.4 = (bf16[8,4,32,256]{3,2,1,0:T(8,128)(2,1)S(1)}, bf16[8,4,32,256]{3,2,1,0:T(8,128)(2,1)S(1)}, u32[]{:S(2)}, u32[]{:S(2)}) collective-permute-start(bf16[8,4,32,256]{3,2,1,0:T(8,128)(2,1)S(1)} %get-tuple-element.33), channel_id=1, source_target_pairs={{0,6},{2,0},{4,2},{6,4},{8,10},{10,12},{12,14},{14,8},{1,7},{3,1},... | collective-permute-start | bytes 1572872 | tf_op jit(solution)/shard_map/ppermute | solution.py:314
  94.7 5.2 %collective-permute-start.6 = (bf16[2,144,768]{2,1,0:T(8,128)(2,1)S(1)}, bf16[2,144,768]{2,1,0:T(8,128)(2,1)S(1)}, u32[]{:S(2)}, u32[]{:S(2)}) collective-permute-start(bf16[2,144,768]{2,1,0:T(8,128)(2,1)S(1)} %get-tuple-element.32), channel_id=1, source_target_pairs={{0,8},{8,0},{1,9},{9,1},{2,10},{10,2},{3,11},{11,3},{4,12},{12,4},... | collective-permute-start | bytes 1327112 | tf_op jit(solution)/shard_map/ppermute | solution.py:317
